TPU v7x, 32 devices: a whole 2x2x4 slice. The times are simulated.
32 devices in a mesh: seq: 4 (over x, core), tp: 8 (over z, y).
Axes of the slice: x: 2, y: 2, z: 4, core: 2. Of those that a mesh axis runs over, the one named last changes fastest.
Arguments:
- tokens: bfloat16 [3, 4096, 2048], P(None, 'seq', 'tp'), may hold values from -6 to 6
- cotangent: bfloat16 [3, 4096, 2048], P(None, 'seq', 'tp'), may hold values from -6 to 6
- lengths: int32 [3], replicated, may hold values from 1024 to 4096, as said below
- in_gain: float32 [2048], replicated, may hold values from 0.1 to 1.9
- w_input: bfloat16 [2048, 2048], P(None, 'tp'), may hold values from -0.125 to 0.125
- w_forget: bfloat16 [2048, 2048], P(None, 'tp'), may hold values from -0.125 to 0.125
- w_output_gate: bfloat16 [2048, 2048], P(None, 'tp'), may hold values from -0.125 to 0.125
- lower_bound: float32 [2048], P('tp'), may hold values from 0 to 1
- mix_gain: float32 [2048], P('tp'), may hold values from 0.1 to 1.9
- w_out: bfloat16 [2048, 2048], P('tp'), may hold values from -0.25 to 0.25
- mlp_gain: float32 [2048], P('tp'), may hold values from 0.1 to 1.9
- w_gate: bfloat16 [2048, 5632], P(None, 'tp'), may hold values from -0.125 to 0.125
- w_up: bfloat16 [2048, 5632], P(None, 'tp'), may hold values from -0.125 to 0.125
- w_down: bfloat16 [5632, 2048], P('tp'), may hold values from -0.15625 to 0.15625
Outputs:
- mixed: bfloat16 [3, 4096, 2048], P(None, 'seq', 'tp')
- grad_tokens: float32 [3, 4096, 2048], P(None, 'seq', 'tp')
- grad_in_gain: float32 [2048], P('tp')
- grad_w_input: float32 [2048, 2048], P(None, 'tp')
- grad_w_forget: float32 [2048, 2048], P(None, 'tp')
- grad_w_output_gate: float32 [2048, 2048], P(None, 'tp')
- grad_lower_bound: float32 [2048], P('tp')
- grad_mix_gain: float32 [2048], P('tp')
- grad_w_out: float32 [2048, 2048], P('tp')
- grad_mlp_gain: float32 [2048], P('tp')
- grad_w_gate: float32 [2048, 5632], P(None, 'tp')
- grad_w_up: float32 [2048, 5632], P(None, 'tp')
- grad_w_down: float32 [5632, 2048], P('tp')
Inputs may be any that keep to these rules, and one draw needn't show every extreme that they name: `lengths`: one slot, chosen by the seed, has exactly 4096 valid positions.
All inputs are finite; a program needn't handle non-finite values.
Results may differ from a plain program's by a relative error of at most 0.024.
Values may be sent and summed in bfloat16 or wider, within the bound.
No kernel may reach another device: no remote copies, remote signals or barrier semaphores. Data moves between devices by JAX's collectives and lax.ppermute only.
A program may use at most 256 MiB of HBM per device.

v0:
```python
import jax
import jax.numpy as jnp
from jax import lax
from jax.sharding import PartitionSpec as P

epsilon = 1e-06


def prefix(part, axis, combine, identity, reverse):
    count = lax.axis_size(axis)
    place = lax.axis_index(axis)
    ahead = count - 1 - place if reverse else place
    gathered = jax.tree.map(lambda a: lax.all_gather(a, axis), part)
    state = jax.tree.map(lambda a, e: jnp.zeros_like(a) + jnp.asarray(e, a.dtype), part, identity)

    def one(turn, state):
        source = count - 1 - turn if reverse else turn
        return combine(
            state, jax.tree.map(lambda a: lax.dynamic_index_in_dim(a, source, 0, False), gathered)
        )

    return lax.fori_loop(0, ahead, one, state)


def combine_pair(earlier, later):
    return (earlier[0] * later[0], later[0] * earlier[1] + later[1])


def linear_scan(decay, drive):
    return lax.associative_scan(combine_pair, (decay, drive), axis=1)


def silu_parts(value):
    sig = jax.nn.sigmoid(value)
    return (value * sig, sig * (1.0 + value * (1.0 - sig)))


def project(left, weight):
    return jnp.einsum("scd,de->sce", left, weight, preferred_element_type=jnp.float32)


def project_back(left, weight):
    return jnp.einsum("sce,de->scd", left, weight, preferred_element_type=jnp.float32)


def outer_sum(left, right):
    return jnp.einsum("scd,sce->de", left, right, preferred_element_type=jnp.float32)


def row_total(values):
    return lax.psum(values, "tp")


def pass_carry(decay_all, state_end, reverse):
    identity = (jnp.ones_like(decay_all), jnp.zeros_like(state_end))
    return prefix((decay_all, state_end), "seq", combine_pair, identity, reverse)[1]


def on_device(
    tokens,
    cotangent,
    lengths,
    in_gain,
    w_input,
    w_forget,
    w_output_gate,
    lower_bound,
    mix_gain,
    w_out,
    mlp_gain,
    w_gate,
    w_up,
    w_down,
):
    shard_width = tokens.shape[2]
    width = shard_width * lax.axis_size("tp")
    group = tokens.shape[1]
    offset = lax.axis_index("tp") * shard_width
    places = lax.axis_index("seq") * group + jnp.arange(group, dtype=jnp.int32)
    live = (places[None, :] < lengths[:, None]).astype(jnp.float32)[:, :, None]
    full_tokens = lax.all_gather(tokens, "tp", axis=2, tiled=True)
    full_x = full_tokens.astype(jnp.float32)
    r_in = lax.rsqrt(jnp.mean(full_x * full_x, axis=-1, keepdims=True) + epsilon)
    normed = (full_x * r_in * in_gain).astype(jnp.bfloat16)
    pre_in = project(normed, w_input)
    pre_fg = project(normed, w_forget)
    pre_og = project(normed, w_output_gate)
    sig_f = jax.nn.sigmoid(pre_fg)
    forget = lower_bound + (1.0 - lower_bound) * sig_f
    act_in, slope_in = silu_parts(pre_in)
    drive = act_in * (1.0 - forget)
    cumul, local_state = linear_scan(forget, drive)
    head = pass_carry(cumul[:, -1], local_state[:, -1], False)
    state = local_state + cumul * head[:, None, :]
    r_mix = lax.rsqrt(row_total(jnp.sum(state * state, axis=-1, keepdims=True)) / width + epsilon)
    act_og, slope_og = silu_parts(pre_og)
    state_norm = state * r_mix
    mixer_out = (state_norm * mix_gain * act_og).astype(jnp.bfloat16)
    shard_x = tokens.astype(jnp.float32)
    branch = lax.psum_scatter(
        project(mixer_out, w_out).astype(jnp.bfloat16), "tp", scatter_dimension=2, tiled=True
    ).astype(jnp.float32)
    resid = shard_x + branch
    r_mlp = lax.rsqrt(row_total(jnp.sum(resid * resid, axis=-1, keepdims=True)) / width + epsilon)
    scaled = resid * r_mlp
    mlp_shard = (scaled * mlp_gain).astype(jnp.bfloat16)
    mlp_in = lax.all_gather(mlp_shard, "tp", axis=2, tiled=True)
    gate_pre = project(mlp_in, w_gate)
    up_pre = project(mlp_in, w_up)
    act_gate, slope_gate = silu_parts(gate_pre)
    hidden = (act_gate * up_pre).astype(jnp.bfloat16)
    ffn = lax.psum_scatter(
        project(hidden, w_down).astype(jnp.bfloat16), "tp", scatter_dimension=2, tiled=True
    ).astype(jnp.float32)
    mixed = (live * (resid + ffn)).astype(jnp.bfloat16)
    full_tokens, mlp_in, full_cot = (
        lax.all_gather(tokens, "tp", axis=2, tiled=True),
        lax.all_gather(mlp_shard, "tp", axis=2, tiled=True),
        lax.all_gather(cotangent, "tp", axis=2, tiled=True),
    )
    full_x = full_tokens.astype(jnp.float32)
    normed = (full_x * r_in * in_gain).astype(jnp.bfloat16)
    grad_out = (full_cot.astype(jnp.float32) * live).astype(jnp.bfloat16)
    grad_res = cotangent.astype(jnp.float32) * live
    grad_hidden = project_back(grad_out, w_down)
    grad_w_down = outer_sum(hidden, grad_out)
    grad_gate = (grad_hidden * up_pre * slope_gate).astype(jnp.bfloat16)
    grad_up = (grad_hidden * act_gate).astype(jnp.bfloat16)
    grad_mlp_in = lax.psum_scatter(
        (project_back(grad_gate, w_gate) + project_back(grad_up, w_up)).astype(jnp.bfloat16),
        "tp",
        scatter_dimension=2,
        tiled=True,
    ).astype(jnp.float32)
    grad_w_gate = outer_sum(mlp_in, grad_gate)
    grad_w_up = outer_sum(mlp_in, grad_up)
    grad_mlp_gain = jnp.sum(grad_mlp_in * scaled, axis=(0, 1))
    grad_scaled = grad_mlp_in * mlp_gain
    inner_mlp = row_total(jnp.sum(resid * grad_scaled, axis=-1, keepdims=True))
    grad_resid = grad_res + r_mlp * grad_scaled - resid * r_mlp**3 * inner_mlp / width
    grad_branch = lax.all_gather(grad_resid.astype(jnp.bfloat16), "tp", axis=2, tiled=True)
    grad_mix = project_back(grad_branch, w_out)
    grad_w_out = outer_sum(mixer_out, grad_branch)
    grad_mix_gain = jnp.sum(grad_mix * state_norm * act_og, axis=(0, 1))
    grad_og = (grad_mix * state_norm * mix_gain * slope_og).astype(jnp.bfloat16)
    grad_norm = grad_mix * mix_gain * act_og
    inner_mix = row_total(jnp.sum(state * grad_norm, axis=-1, keepdims=True))
    grad_local = r_mix * grad_norm - state * r_mix**3 * inner_mix / width
    next_forget = jnp.concatenate([forget[:, 1:], jnp.ones_like(forget[:, :1])], axis=1)
    back_cumul, back_state = linear_scan(jnp.flip(next_forget, 1), jnp.flip(grad_local, 1))
    back_cumul = jnp.flip(back_cumul, 1)
    back_state = jnp.flip(back_state, 1)
    tail = pass_carry(forget[:, 0] * back_cumul[:, 0], forget[:, 0] * back_state[:, 0], True)
    grad_state = back_state + back_cumul * tail[:, None, :]
    prev_state = jnp.concatenate([head[:, None, :], state[:, :-1]], axis=1)
    grad_forget = grad_state * (prev_state - act_in)
    grad_in = (grad_state * (1.0 - forget) * slope_in).astype(jnp.bfloat16)
    grad_lower_bound = jnp.sum(grad_forget * (1.0 - sig_f), axis=(0, 1))
    grad_fg = (grad_forget * (1.0 - lower_bound) * sig_f * (1.0 - sig_f)).astype(jnp.bfloat16)
    in_term = (
        project_back(grad_in, w_input)
        + project_back(grad_fg, w_forget)
        + project_back(grad_og, w_output_gate)
    )
    inner_term = jnp.sum(full_x * in_gain * in_term, axis=-1, keepdims=True)
    inner_tiled = jnp.broadcast_to(inner_term, inner_term.shape[:2] + (lax.axis_size("tp"),))
    grad_normed, inner_in = (
        lax.psum_scatter(
            in_term.astype(jnp.bfloat16), "tp", scatter_dimension=2, tiled=True
        ).astype(jnp.float32),
        lax.psum_scatter(
            inner_tiled.astype(jnp.bfloat16), "tp", scatter_dimension=2, tiled=True
        ).astype(jnp.float32),
    )
    grad_w_input = outer_sum(normed, grad_in)
    grad_w_forget = outer_sum(normed, grad_fg)
    grad_w_output_gate = outer_sum(normed, grad_og)
    gain_shard = lax.dynamic_slice_in_dim(in_gain, offset, shard_width)
    grad_in_gain = jnp.sum(grad_normed * shard_x * r_in, axis=(0, 1))
    grad_tokens = (
        grad_resid + r_in * gain_shard * grad_normed - shard_x * r_in**3 * inner_in / width
    )
    summed = (
        lax.psum(grad_in_gain.astype(jnp.bfloat16), "seq").astype(jnp.float32),
        lax.psum(grad_w_input.astype(jnp.bfloat16), "seq").astype(jnp.float32),
        lax.psum(grad_w_forget.astype(jnp.bfloat16), "seq").astype(jnp.float32),
        lax.psum(grad_w_output_gate.astype(jnp.bfloat16), "seq").astype(jnp.float32),
        lax.psum(grad_lower_bound.astype(jnp.bfloat16), "seq").astype(jnp.float32),
        lax.psum(grad_mix_gain.astype(jnp.bfloat16), "seq").astype(jnp.float32),
        lax.psum(grad_w_out.astype(jnp.bfloat16), "seq").astype(jnp.float32),
        lax.psum(grad_mlp_gain.astype(jnp.bfloat16), "seq").astype(jnp.float32),
        lax.psum(grad_w_gate.astype(jnp.bfloat16), "seq").astype(jnp.float32),
        lax.psum(grad_w_up.astype(jnp.bfloat16), "seq").astype(jnp.float32),
        lax.psum(grad_w_down.astype(jnp.bfloat16), "seq").astype(jnp.float32),
    )
    return (
        mixed,
        grad_tokens,
        summed[0],
        summed[1],
        summed[2],
        summed[3],
        summed[4],
        summed[5],
        summed[6],
        summed[7],
        summed[8],
        summed[9],
        summed[10],
    )


def solution(mesh):
    return jax.shard_map(
        on_device,
        mesh=mesh,
        in_specs=(
            P(None, "seq", "tp"),
            P(None, "seq", "tp"),
            P(),
            P(),
            P(None, "tp"),
            P(None, "tp"),
            P(None, "tp"),
            P("tp"),
            P("tp"),
            P("tp", None),
            P("tp"),
            P(None, "tp"),
            P(None, "tp"),
            P("tp", None),
        ),
        out_specs=(
            P(None, "seq", "tp"),
            P(None, "seq", "tp"),
            P("tp"),
            P(None, "tp"),
            P(None, "tp"),
            P(None, "tp"),
            P("tp"),
            P("tp"),
            P("tp", None),
            P("tp"),
            P(None, "tp"),
            P(None, "tp"),
            P("tp", None),
        ),
        check_vma=False,
    )
```

profile of v0, /device:TPU:0, one launch (start us, length us, event | category | flops | bytes accessed | tf_op | source)
XLA Modules:
  0.0 2703.9 jit_solution(7772964556900281276)
XLA Ops:
  8.7 180.6 %all-gather.9.cloned.1.call-done = bf16[3,1024,2048]{2,1,0:T(8,128)(2,1)} async-done(((bf16[3,1024,256]{2,1,0:T(8,128)(2,1)}), bf16[3,1024,2048]{2,1,0:T(8,128)(2,1)}) %all-gather.9.cloned.1.call-update) | async-done | bytes 12582928 | tf_op jit(solution)/shard_map/all_gather | solution.py:81
  489.0 34.3 %psum.105 = f32[3,1024,1]{1,0,2:T(4,128)S(1)} all-reduce(f32[3,1024,1]{1,0,2:T(4,128)S(1)} %bitcast.125), channel_id=1, replica_groups=mesh['seq'=4,'tp'=8] {'tp'}, use_global_device_ids=true, to_apply=%region_4.5 | all-reduce | flops 3072 | bytes 24576 | tf_op jit(solution)/shard_map/psum | solution.py:51
  540.8 205.1 %reduce-scatter.5.cloned.1.call-done = bf16[3,1024,256]{2,1,0:T(8,128)(2,1)} async-done(((bf16[3,1024,2048]{2,1,0:T(8,128)(2,1)}), bf16[3,1024,256]{2,1,0:T(8,128)(2,1)}) %reduce-scatter.5.cloned.1.call-update) | async-done | bytes 1572880 | tf_op jit(solution)/shard_map/reduce_scatter | solution.py:100
  748.4 35.2 %psum.106 = f32[3,1024,1]{1,0,2:T(4,128)S(1)} all-reduce(f32[3,1024,1]{1,0,2:T(4,128)S(1)} %bitcast.126), channel_id=1, replica_groups=mesh['seq'=4,'tp'=8] {'tp'}, use_global_device_ids=true, to_apply=%region_7.8 | all-reduce | flops 3072 | bytes 24576 | tf_op jit(solution)/shard_map/psum | solution.py:51
  788.4 172.8 %all-gather.11.cloned.1.call-done = bf16[3,1024,2048]{2,1,0:T(8,128)(2,1)} async-done(((bf16[3,1024,256]{2,1,0:T(8,128)(2,1)}), bf16[3,1024,2048]{2,1,0:T(8,128)(2,1)}) %all-gather.11.cloned.1.call-update) | async-done | bytes 12582928 | tf_op jit(solution)/shard_map/all_gather | solution.py:107
  961.2 15.2 fusion.26
  988.0 149.9 %all-gather.13.cloned.1.call-done = bf16[3,1024,2048]{2,1,0:T(8,128)(2,1)} async-done(((bf16[3,1024,256]{2,1,0:T(8,128)(2,1)}), bf16[3,1024,2048]{2,1,0:T(8,128)(2,1)}) %all-gather.13.cloned.1.call-update) | async-done | bytes 12582928 | tf_op jit(solution)/shard_map/all_gather | solution.py:119
  1137.9 20.4 multiply_convert_fusion.3
  1158.3 17.3 fusion.28
  1175.6 19.3 add_convert_fusion
  1194.9 206.0 %reduce-scatter.9.cloned.1.call-done = bf16[3,1024,256]{2,1,0:T(8,128)(2,1)} async-done(((bf16[3,1024,2048]{2,1,0:T(8,128)(2,1)}), bf16[3,1024,256]{2,1,0:T(8,128)(2,1)}) %reduce-scatter.9.cloned.1.call-update) | async-done | bytes 1572880 | tf_op jit(solution)/shard_map/reduce_scatter | solution.py:129
  1404.7 35.2 %psum.107 = f32[3,1024]{1,0:T(4,128)S(1)} all-reduce(f32[3,1024]{1,0:T(4,128)S(1)} %get-tuple-element.146), channel_id=1, replica_groups=mesh['seq'=4,'tp'=8] {'tp'}, use_global_device_ids=true, to_apply=%region_11.12 | all-reduce | flops 3072 | bytes 24576 | tf_op jit(solution)/shard_map/psum | solution.py:51
  1515.7 15.0 bitcast_convert_fusion.1
  1530.8 14.7 bitcast_convert_fusion.2
  1556.2 62.9 %all-gather.15.cloned.1.call-done = bf16[3,1024,2048]{2,1,0:T(8,128)(2,1)} async-done(((bf16[3,1024,256]{2,1,0:T(8,128)(2,1)}), bf16[3,1024,2048]{2,1,0:T(8,128)(2,1)}) %all-gather.15.cloned.1.call-update) | async-done | bytes 12582928 | tf_op jit(solution)/shard_map/all_gather | solution.py:141
  1630.6 34.5 %psum.108 = f32[3,1024]{1,0:T(4,128)S(1)} all-reduce(f32[3,1024]{1,0:T(4,128)S(1)} %get-tuple-element.144), channel_id=1, replica_groups=mesh['seq'=4,'tp'=8] {'tp'}, use_global_device_ids=true, to_apply=%region_13.14 | all-reduce | flops 3072 | bytes 24576 | tf_op jit(solution)/shard_map/psum | solution.py:51
  1934.3 24.5 rev.9
  1958.8 24.5 rev.10
  2031.8 14.8 convolution_convert_fusion
  2071.2 27.7 %fusion.4 = (bf16[3,1024]{1,0:T(4,128)(2,1)S(1)}, bf16[3,1024,2048]{2,1,0:T(8,128)(2,1)}) fusion(bf16[3,1024,2048]{2,1,0:T(8,128)(2,1)} %all-gather.9.cloned.1.call-done, f32[2048]{0:T(1024)S(1)} %copy-done.61, bf16[3,1024,256]{2,1,0:T(8,128)(2,1)S(1)} %copy-done.44, bf16[2048,256]{1,0:T(8,128)(2,1)S(1)} %copy-done.45, f32[3,1024,2048]{2,1,0:T(8,128)} %fusion.47, ...), kind=kOutput, calls=%fused_computation.11 | convolution fusion | flops 3265262592 | bytes 78133248 | tf_op jit(solution)/shard_map/sce,de->scd/dot_general | solution.py:43
  2100.2 33.4 %all-reduce.82 = bf16[3,1024,8]{1,0,2:T(4,128)(2,1)S(1)} all-reduce(bf16[3,1024,8]{1,0,2:T(4,128)(2,1)S(1)} %broadcast_in_dim.17), channel_id=10, replica_groups=mesh['seq'=4,'tp'=8] {'tp'}, use_global_device_ids=true, to_apply=%region_18.19.clone | all-reduce | flops 24576 | bytes 98304
  2134.2 121.9 %all-reduce.87.cloned.1.call-done = (bf16[2048,256]{1,0:T(8,128)(2,1)}, bf16[2048,256]{1,0:T(8,128)(2,1)}, bf16[2048,256]{1,0:T(8,128)(2,1)}, bf16[256,2048]{1,0...) async-done(((bf16[2048,256]{1,0:T(8,128)(2,1)}, bf16[2048,256]{1,0:T(8,128)(2,1)}, bf16[2048,256]{1,0:T(8,128)(2,1)}, ...) | async-done | bytes 12845072 | tf_op jit(solution)/shard_map/psum | solution.py:185
  2273.6 194.0 %reduce-scatter.7.cloned.1.call-done = bf16[3,1024,256]{2,1,0:T(8,128)(2,1)} async-done(((bf16[3,1024,2048]{2,1,0:T(8,128)(2,1)}), bf16[3,1024,256]{2,1,0:T(8,128)(2,1)}) %reduce-scatter.7.cloned.1.call-update) | async-done | bytes 1572880 | tf_op jit(solution)/shard_map/reduce_scatter | solution.py:112
  2467.7 210.5 %reduce-scatter.11.cloned.1.call-done = bf16[3,1024,256]{2,1,0:T(8,128)(2,1)} async-done(((bf16[3,1024,2048]{2,1,0:T(8,128)(2,1)}), bf16[3,1024,256]{2,1,0:T(8,128)(2,1)}) %reduce-scatter.11.cloned.1.call-update) | async-done | bytes 1572880 | tf_op jit(solution)/shard_map/reduce_scatter | solution.py:168
  (608 shorter events, 818.2 us)
Async XLA Ops:
  7.2 1130.7 %copy-start = (bf16[704,2048]{1,0:T(8,128)(2,1)S(1)}, bf16[704,2048]{1,0:T(8,128)(2,1)}, u32[]{:S(2)}) copy-start(bf16[704,2048]{1,0:T(8,128)(2,1)} %param.31) | copy-start | bytes 8650756
  7.2 182.2 %all-gather.9.cloned.1.call-start = ((), (), s32[]{:S(2)}) async-start(), calls=%async_computation.4 | async-start | bytes 14155776 | tf_op jit(solution)/shard_map/all_gather | solution.py:81
  7.9 738.0 %reduce-scatter.5.cloned.1.call-start = ((), (), s32[]{:S(2)}) async-start(), calls=%async_computation.5 | async-start | bytes 14155776 | tf_op jit(solution)/shard_map/reduce_scatter | solution.py:100
  8.7 195.9 %copy-start.78 = (f32[256]{0:T(256)}, f32[256]{0:T(256)S(1)}, u32[]{:S(2)}) copy-start(f32[256]{0:T(256)S(1)} %broadcast_subtract_fusion) | copy-start | bytes 3076
  8.7 188.5 %copy-start.60 = (f32[2048]{0:T(1024)S(1)}, f32[2048]{0:T(1024)}, u32[]{:S(2)}) copy-start(f32[2048]{0:T(1024)} %param.21) | copy-start | bytes 24580
  197.2 326.7 %copy-start.66 = (f32[3,1024]{1,0:T(4,128)}, f32[3,1024]{1,0:T(4,128)S(1)}, u32[]{:S(2)}) copy-start(f32[3,1024]{1,0:T(4,128)S(1)} %get-tuple-element.253) | copy-start | bytes 36868
  540.7 242.9 %copy-start.68 = (f32[256]{0:T(256)S(1)}, f32[256]{0:T(256)}, u32[]{:S(2)}) copy-start(f32[256]{0:T(256)} %param.28) | copy-start | bytes 3076
  540.8 420.5 %all-gather.11.cloned.1.call-start = ((), (), s32[]{:S(2)}) async-start(), calls=%async_computation.6 | async-start | bytes 14155776 | tf_op jit(solution)/shard_map/all_gather | solution.py:107
  783.6 656.3 %copy-start.52 = (f32[3,1024]{1,0:T(4,128)}, f32[3,1024]{1,0:T(4,128)S(1)}, u32[]{:S(2)}) copy-start(f32[3,1024]{1,0:T(4,128)S(1)} %get-tuple-element.257) | copy-start | bytes 36868
  783.6 656.3 %copy-start.54 = (f32[3,1024]{1,0:T(4,128)}, f32[3,1024]{1,0:T(4,128)S(1)}, u32[]{:S(2)}) copy-start(f32[3,1024]{1,0:T(4,128)S(1)} %get-tuple-element.256) | copy-start | bytes 36868
  787.3 350.7 %all-gather.13.cloned.1.call-start = ((), (), s32[]{:S(2)}) async-start(), calls=%async_computation.8 | async-start | bytes 14155776 | tf_op jit(solution)/shard_map/all_gather | solution.py:119
  787.8 613.1 %reduce-scatter.9.cloned.1.call-start = ((), (), s32[]{:S(2)}) async-start(), calls=%async_computation.9 | async-start | bytes 14155776 | tf_op jit(solution)/shard_map/reduce_scatter | solution.py:129
  788.4 757.1 %copy-start.56 = (f32[3,1024]{1,0:T(4,128)}, f32[3,1024]{1,0:T(4,128)S(1)}, u32[]{:S(2)}) copy-start(f32[3,1024]{1,0:T(4,128)S(1)} %compare_convert_fusion) | copy-start | bytes 36868
  1194.9 424.3 %all-gather.15.cloned.1.call-start = ((), (), s32[]{:S(2)}) async-start(), calls=%async_computation.10 | async-start | bytes 14155776 | tf_op jit(solution)/shard_map/all_gather | solution.py:141
  1445.2 811.0 %all-reduce.87.cloned.1.call-start = ((), (), s32[]{:S(2)}) async-start(), calls=%async_computation.12 | async-start | bytes 25690112 | tf_op jit(solution)/shard_map/psum | solution.py:185
  1545.5 73.6 %copy-start.64 = (f32[3,1024]{1,0:T(4,128)S(1)}, f32[3,1024]{1,0:T(4,128)}, u32[]{:S(2)}) copy-start(f32[3,1024]{1,0:T(4,128)} %copy-done.63) | copy-start | bytes 36868
  2031.8 435.9 %reduce-scatter.7.cloned.1.call-start = ((), (), s32[]{:S(2)}) async-start(), calls=%async_computation.7 | async-start | bytes 14155776 | tf_op jit(solution)/shard_map/reduce_scatter | solution.py:112
  2046.7 631.5 %reduce-scatter.11.cloned.1.call-start = ((), (), s32[]{:S(2)}) async-start(), calls=%async_computation.11 | async-start | bytes 14155776 | tf_op jit(solution)/shard_map/reduce_scatter | solution.py:168
  2270.3 407.9 %copy-start.53 = (f32[3,1024]{1,0:T(4,128)S(1)}, f32[3,1024]{1,0:T(4,128)}, u32[]{:S(2)}) copy-start(f32[3,1024]{1,0:T(4,128)} %copy-done.52) | copy-start | bytes 36868
  2270.3 407.9 %copy-start.55 = (f32[3,1024]{1,0:T(4,128)S(1)}, f32[3,1024]{1,0:T(4,128)}, u32[]{:S(2)}) copy-start(f32[3,1024]{1,0:T(4,128)} %copy-done.54) | copy-start | bytes 36868
  2270.3 407.9 %copy-start.57 = (f32[3,1024]{1,0:T(4,128)S(1)}, f32[3,1024]{1,0:T(4,128)}, u32[]{:S(2)}) copy-start(f32[3,1024]{1,0:T(4,128)} %copy-done.56) | copy-start | bytes 36868
  2270.3 407.9 %copy-start.59 = (f32[3,1024]{1,0:T(4,128)S(1)}, f32[3,1024]{1,0:T(4,128)}, u32[]{:S(2)}) copy-start(f32[3,1024]{1,0:T(4,128)} %copy-done.58) | copy-start | bytes 36868
  2270.3 407.9 %copy-start.65 = (f32[3,1024]{1,0:T(4,128)S(1)}, f32[3,1024]{1,0:T(4,128)}, u32[]{:S(2)}) copy-start(f32[3,1024]{1,0:T(4,128)} %get-tuple-element.252) | copy-start | bytes 36868
  2270.3 407.9 %copy-start.69 = (f32[256]{0:T(256)S(1)}, f32[256]{0:T(256)}, u32[]{:S(2)}) copy-start(f32[256]{0:T(256)} %param.28) | copy-start | bytes 3076
  (82 other events, 730.7 us)
Sparse Core Ops, SparseCore 0:
  10.1 179.2 all-gather.8
  540.9 205.0 reduce-scatter.4
  787.4 173.7 all-gather.10
  963.1 174.7 all-gather.12
  1195.0 205.9 reduce-scatter.8
  1445.3 173.7 all-gather.14
  2031.9 224.2 all-reduce.86
  2259.8 207.8 reduce-scatter.6
  2471.3 206.8 reduce-scatter.10
where the time goes:
time: 2730 us; the launch traced here: 2700 us
  waiting for transfers between devices  1510 us (55%)
  local copies, waits for them, and re-layouts  548 us (20%)
  matrix products  263 us (10%)
  blocking collectives  200 us (7%)
  other arithmetic  171 us (6%)
    slice x141, local copies, waits for them, and re-layouts, linear_scan(): return lax.associative_scan(combine_pair, (decay, drive), axis=1)  324 us
    reduce_scatter x1, waiting for transfers between devices, on_device(): lax.psum_scatter(in_term.astype(jnp.bfloat16), 'tp', scatter_dimension=2,...  210 us
    reduce_scatter x1, waiting for transfers between devices, on_device(): lax.psum_scatter((project_back(grad_gate, w_gate) + project_back(grad_up,...  206 us
    reduce_scatter x1, waiting for transfers between devices, on_device(): lax.psum_scatter(project(mixer_out, w_out).astype(jnp.bfloat16), 'tp', sc...  205 us
    reduce_scatter x1, waiting for transfers between devices, on_device(): lax.psum_scatter(project(hidden, w_down).astype(jnp.bfloat16), 'tp', scat...  194 us
    all_gather x1, waiting for transfers between devices, on_device(): full_tokens = lax.all_gather(tokens, 'tp', axis=2, tiled=True)  181 us
    all_gather x1, waiting for transfers between devices, on_device(): mlp_in = lax.all_gather(mlp_shard, 'tp', axis=2, tiled=True)  173 us
    pad x72, local copies, waits for them, and re-layouts, linear_scan(): return lax.associative_scan(combine_pair, (decay, drive), axis=1)  154 us
  transfers between devices with their start and end apart: 9, of which 9 were waited for; matrix products, arithmetic and copies ran while one was open for 8% of the time, Pallas kernels for 0%

commit v1 on v0

v1 whole, which is shorter than its diff:
```python
import functools

import jax
import jax.numpy as jnp
import numpy as np
from jax import lax
from jax.experimental import pallas as pl
from jax.experimental.pallas import tpu as pltpu
from jax.sharding import PartitionSpec as P

EPS = 1e-06
F32, BF16 = jnp.float32, jnp.bfloat16
VMEM_LIMIT = 56 * 1024 * 1024


def params(**more):
    return pltpu.CompilerParams(vmem_limit_bytes=VMEM_LIMIT, **more)


def sigmoid(v):
    return 1.0 / (1.0 + jnp.exp(-v))


def ring_of(mesh):
    count = mesh.shape["tp"]
    try:
        coords = [tuple(d.coords) for d in mesh.devices[0]]
        ys = len({c[1] for c in coords})
    except (AttributeError, TypeError):
        ys = 2 if count % 2 == 0 else 1
    zs = count // ys
    if zs * ys != count or zs % 2 or ys < 2:
        return list(range(count))
    cycle = [(z, 0) for z in range(zs)]
    for turn, z in enumerate(reversed(range(zs))):
        across = range(1, ys) if turn % 2 == 0 else reversed(range(1, ys))
        cycle += [(z, y) for y in across]
    return [z * ys + y for z, y in cycle]


class Net:
    def __init__(self, mesh):
        self.seq, self.tp = mesh.shape["seq"], mesh.shape["tp"]
        self.cycle = ring_of(mesh)
        self.bits = [1 << b for b in range(self.seq.bit_length() - 1)]

    def places(self):
        s, t = lax.axis_index("seq"), lax.axis_index("tp")
        where = np.zeros(self.tp, np.int32)
        for i, index in enumerate(self.cycle):
            where[index] = i
        pos = jnp.asarray(where)[t]
        steps = jnp.arange(self.tp, dtype=jnp.int32)
        table = jnp.asarray(np.array(self.cycle, np.int32))
        self.ahead = table[(pos + steps) % self.tp]
        self.behind = table[(pos - steps) % self.tp]
        return s, t

    def shift(self, x, k):
        n = self.tp
        return lax.ppermute(x, "tp", [(self.cycle[i], self.cycle[(i + k) % n]) for i in range(n)])

    def swap(self, x, bit):
        return lax.ppermute(x, "seq", [(i, i ^ bit) for i in range(self.seq)])

    def ring_gather(self, x):
        n = self.tp
        out = [x] + [None] * (n - 1)
        full = (n - 1) // 2
        fore = back = x
        for d in range(1, full + 1):
            fore = out[d] = self.shift(fore, 1)
            back = out[n - d] = self.shift(back, -1)
        if n % 2 == 0:
            half = x.shape[0] // 2
            out[n // 2] = jnp.concatenate([self.shift(fore[:half], 1), self.shift(back[half:], -1)], 0)
        return out

    def ring_scatter(self, chunk):
        n = self.tp
        full = (n - 1) // 2
        fore, back = [], []
        if n % 2 == 0:
            far = chunk(n // 2, [])
            half = far.shape[0] // 2
            up, down = self.shift(far[:half], 1), self.shift(far[half:], -1)
            fore = [jnp.concatenate([up, jnp.zeros_like(down)], 0)]
            back = [jnp.concatenate([jnp.zeros_like(up), down], 0)]
        for d in range(full, 0, -1):
            fore = [self.shift(chunk(n - d, fore), 1)]
            back = [self.shift(chunk(d, back), -1)]
        return chunk(0, fore + back)

    def quad_gather(self, x):
        out = [x] + [None] * (self.seq - 1)
        for bit in reversed(self.bits):
            for j in range(0, self.seq, 2 * bit):
                if out[j] is not None:
                    out[j ^ bit] = self.swap(out[j], bit)
        return out

    def quad_scatter(self, parts):
        parts = list(parts)
        for bit in self.bits[:-1]:
            for j in range(0, self.seq, 2 * bit):
                moved = self.swap(parts[j ^ bit], bit)
                if j == 0:
                    first = moved
                    parts[0] = (parts[0].astype(F32) + moved.astype(F32)).astype(BF16)
                else:
                    parts[j] = (parts[j].astype(F32) + moved.astype(F32)).astype(BF16)
        return [parts[0], self.swap(parts[self.bits[-1]], self.bits[-1])]

    def quad_total(self, x):
        for bit in self.bits:
            order = [j ^ bit for j in range(self.seq)]
            moved = self.swap(x, bit)
            x = x + jnp.stack([moved[j] for j in order], 0)
        return x


SMEM_SPEC = pl.BlockSpec(memory_space=pltpu.SMEM)
VMEM_SPEC = pl.BlockSpec(memory_space=pltpu.VMEM)


def split_rows(x, order, pos_n):
    slots, _, cols = x.shape
    count = order.shape[0]

    def body(order_ref, x_ref, *outs):
        for k in range(count):
            start = pl.multiple_of(order_ref[k] * pos_n, pos_n)
            outs[k][...] = x_ref[:, pl.ds(start, pos_n), :]

    return pl.pallas_call(
        body,
        out_shape=[jax.ShapeDtypeStruct((slots, pos_n, cols), x.dtype)] * count,
        in_specs=[SMEM_SPEC, VMEM_SPEC],
        out_specs=[VMEM_SPEC] * count,
        compiler_params=params(),
    )(order, x)


def join_rows(chunks, order, dtype):
    slots, pos_n, cols = chunks[0].shape
    count = len(chunks)

    def body(order_ref, *refs):
        out = refs[-1]
        for k in range(count):
            start = pl.multiple_of(order_ref[k] * pos_n, pos_n)
            out[:, pl.ds(start, pos_n), :] = refs[k][...].astype(dtype)

    return pl.pallas_call(
        body,
        out_shape=jax.ShapeDtypeStruct((slots, count * pos_n, cols), dtype),
        in_specs=[SMEM_SPEC] + [VMEM_SPEC] * count,
        out_specs=VMEM_SPEC,
        compiler_params=params(),
    )(order, *chunks)


def norm_tokens(chunks, order, gain):
    slots, pos_n, cols = chunks[0].shape
    count = len(chunks)
    rows, width = slots * pos_n, count * cols

    def body(order_ref, gain_ref, *refs):
        x_ref, n_ref = refs[-2:]
        total = jnp.zeros((rows, 1), F32)
        for k in range(count):
            c = refs[k][...].astype(F32).reshape(rows, cols)
            total += jnp.sum(c * c, axis=-1, keepdims=True)
        r = lax.rsqrt(total / width + EPS)
        for k in range(count):
            c = refs[k][...].reshape(rows, cols)
            at = pl.ds(pl.multiple_of(order_ref[k] * cols, cols), cols)
            x_ref[:, at] = c
            n_ref[:, at] = (c.astype(F32) * r * gain_ref[:, at]).astype(BF16)

    return pl.pallas_call(
        body,
        out_shape=[jax.ShapeDtypeStruct((rows, width), BF16)] * 2,
        in_specs=[SMEM_SPEC, VMEM_SPEC] + [VMEM_SPEC] * count,
        out_specs=[VMEM_SPEC] * 2,
        compiler_params=params(),
    )(order, gain.reshape(1, width), *chunks)


def mask_rows(chunks, order, live):
    slots, pos_n, cols = chunks[0].shape
    count = len(chunks)
    rows, width = slots * pos_n, count * cols

    def body(order_ref, live_ref, *refs):
        x_ref = refs[-1]
        for k in range(count):
            c = refs[k][...].astype(F32).reshape(rows, cols)
            at = pl.ds(pl.multiple_of(order_ref[k] * cols, cols), cols)
            x_ref[:, at] = (c * live_ref[...]).astype(BF16)

    return pl.pallas_call(
        body,
        out_shape=jax.ShapeDtypeStruct((rows, width), BF16),
        in_specs=[SMEM_SPEC, VMEM_SPEC] + [VMEM_SPEC] * count,
        out_specs=VMEM_SPEC,
        compiler_params=params(),
    )(order, live, *chunks)


def split_columns(x, order, slots, pos_n, cols):
    count = order.shape[0]

    def body(order_ref, x_ref, *outs):
        for k in range(count):
            at = pl.ds(pl.multiple_of(order_ref[k] * cols, cols), cols)
            outs[k][...] = x_ref[:, at].reshape(slots, pos_n, cols)

    return pl.pallas_call(
        body,
        out_shape=[jax.ShapeDtypeStruct((slots, pos_n, cols), x.dtype)] * count,
        in_specs=[SMEM_SPEC, VMEM_SPEC],
        out_specs=[VMEM_SPEC] * count,
        compiler_params=params(),
    )(order, x)


def tile_scan(decay, drive):
    place = lax.broadcasted_iota(jnp.int32, decay.shape, 0)
    for step in (1, 2, 4):
        inside = place >= step
        before_decay = jnp.where(inside, pltpu.roll(decay, step, 0), 1.0)
        before_drive = jnp.where(inside, pltpu.roll(drive, step, 0), 0.0)
        drive = drive + decay * before_drive
        decay = decay * before_decay
    return decay, drive


def tile_scan_up(decay, drive):
    place = lax.broadcasted_iota(jnp.int32, decay.shape, 0)
    for step in (1, 2, 4):
        inside = place < 8 - step
        before_decay = jnp.where(inside, pltpu.roll(decay, 8 - step, 0), 1.0)
        before_drive = jnp.where(inside, pltpu.roll(drive, 8 - step, 0), 0.0)
        drive = drive + decay * before_drive
        decay = decay * before_decay
    return decay, drive


def gates(pre_in, pre_fg, bound):
    sig_f = sigmoid(pre_fg)
    forget = bound + (1.0 - bound) * sig_f
    sig_in = sigmoid(pre_in)
    act_in = pre_in * sig_in
    slope_in = sig_in * (1.0 + pre_in * (1.0 - sig_in))
    keep = (1.0 - bound) * (1.0 - sig_f)
    return sig_f, forget, act_in, slope_in, keep


def scan_ends(pre, bound, pos_n):
    wide = pre.shape[1] // 3
    blocks = pre.shape[0] // pos_n

    def body(in_ref, fg_ref, bound_ref, decay_ref, end_ref):
        low = bound_ref[...]

        def one(i, carry):
            at = pl.ds(pl.multiple_of(i * 8, 8), 8)
            _, forget, act, _, keep = gates(in_ref[at, :], fg_ref[at, :], low)
            decay, local = tile_scan(forget, act * keep)
            a, h = carry
            return a * decay[7:8, :], decay[7:8, :] * h + local[7:8, :]

        a, h = lax.fori_loop(0, pos_n // 8, one, (jnp.ones((1, wide), F32), jnp.zeros((1, wide), F32)))
        decay_ref[0] = a
        end_ref[0] = h

    return pl.pallas_call(
        body,
        grid=(blocks,),
        out_shape=[jax.ShapeDtypeStruct((blocks, 1, wide), F32)] * 2,
        in_specs=[
            pl.BlockSpec((pos_n, wide), lambda b: (b, 0)),
            pl.BlockSpec((pos_n, wide), lambda b: (b, 1)),
            pl.BlockSpec((1, wide), lambda b: (0, 0)),
        ],
        out_specs=[pl.BlockSpec((1, 1, wide), lambda b: (b, 0, 0))] * 2,
        compiler_params=params(),
    )(pre, pre, bound)


def scan_heads(place, decay, end, reverse):
    behind, count, slots, wide = decay.shape

    def body(place_ref, decay_ref, end_ref, head_ref):
        s, own = place_ref[0], place_ref[1]

        def one(i, state):
            step = count * behind - 1 - i if reverse else i
            block, t = step // behind, step % behind
            j = lax.bitwise_xor(s, block)

            @pl.when(t == own)
            def _():
                head_ref[j] = state

            d = place_ref[2 + t]
            return decay_ref[d, j] * state + end_ref[d, j]

        lax.fori_loop(0, count * behind, one, jnp.zeros((slots, wide), F32))

    return pl.pallas_call(
        body,
        out_shape=jax.ShapeDtypeStruct((count, slots, wide), F32),
        in_specs=[SMEM_SPEC, VMEM_SPEC, VMEM_SPEC],
        out_specs=VMEM_SPEC,
        compiler_params=params(),
    )(place, decay, end)


def scan_states(pre, bound, gain, head, pos_n):
    wide = pre.shape[1] // 3
    blocks = pre.shape[0] // pos_n

    def body(in_ref, fg_ref, og_ref, bound_ref, gain_ref, head_ref, state_ref, mix_ref, sum_ref):
        low = bound_ref[...]

        def one(i, h):
            at = pl.ds(pl.multiple_of(i * 8, 8), 8)
            _, forget, act, _, keep = gates(in_ref[at, :], fg_ref[at, :], low)
            decay, local = tile_scan(forget, act * keep)
            state = local + decay * h
            state_ref[at, :] = state
            square = jnp.sum(state * state, axis=-1, keepdims=True)
            sum_ref[at, :] = jnp.broadcast_to(square, (8, 128))
            return state[7:8, :]

        lax.fori_loop(0, pos_n // 8, one, head_ref[0])
        og = og_ref[...]
        mix_ref[...] = (state_ref[...] * gain_ref[...] * (og * sigmoid(og))).astype(BF16)

    row = pl.BlockSpec((1, wide), lambda b: (0, 0))
    block = pl.BlockSpec((pos_n, wide), lambda b: (b, 0))
    return pl.pallas_call(
        body,
        grid=(blocks,),
        out_shape=[
            jax.ShapeDtypeStruct((blocks * pos_n, wide), F32),
            jax.ShapeDtypeStruct((blocks * pos_n, wide), BF16),
            jax.ShapeDtypeStruct((blocks * pos_n, 128), F32),
        ],
        in_specs=[
            block,
            pl.BlockSpec((pos_n, wide), lambda b: (b, 1)),
            pl.BlockSpec((pos_n, wide), lambda b: (b, 2)),
            row,
            row,
            pl.BlockSpec((1, 1, wide), lambda b: (b, 0, 0)),
        ],
        out_specs=[block, block, pl.BlockSpec((pos_n, 128), lambda b: (b, 0))],
        compiler_params=params(),
    )(pre, pre, pre, bound, gain, head)


def back_ends(pre, bound, local, pos_n):
    wide = local.shape[1]
    blocks = local.shape[0] // pos_n
    tiles = pos_n // 8

    def body(fg_ref, local_ref, bound_ref, end_ref):
        low = bound_ref[...]

        def one(i, g):
            at = pl.ds(pl.multiple_of((tiles - 1 - i) * 8, 8), 8)
            forget = low + (1.0 - low) * sigmoid(fg_ref[at, :])
            decay, part = tile_scan_up(forget, forget * local_ref[at, :])
            return decay[0:1, :] * g + part[0:1, :]

        end_ref[0] = lax.fori_loop(0, tiles, one, jnp.zeros((1, wide), F32))

    return pl.pallas_call(
        body,
        grid=(blocks,),
        out_shape=jax.ShapeDtypeStruct((blocks, 1, wide), F32),
        in_specs=[
            pl.BlockSpec((pos_n, wide), lambda b: (b, 1)),
            pl.BlockSpec((pos_n, wide), lambda b: (b, 0)),
            pl.BlockSpec((1, wide), lambda b: (0, 0)),
        ],
        out_specs=pl.BlockSpec((1, 1, wide), lambda b: (b, 0, 0)),
        compiler_params=params(),
    )(pre, local, bound)


def back_states(pre, bound, local, state, head, tail, pos_n):
    wide = local.shape[1]
    blocks = local.shape[0] // pos_n
    pairs = pos_n // 16

    def body(in_ref, fg_ref, bound_ref, local_ref, state_ref, head_ref, tail_ref, gin_ref, gfg_ref, low_ref):
        low = bound_ref[...]
        place = lax.broadcasted_iota(jnp.int32, (8, wide), 0)

        def half(tile, g, total):
            at = pl.ds(pl.multiple_of(tile * 8, 8), 8)
            sig_f, forget, act, slope, keep = gates(in_ref[at, :], fg_ref[at, :], low)
            loc = local_ref[at, :]
            decay, part = tile_scan_up(forget, forget * loc)
            whole = part + decay * g
            after = jnp.where(place == 7, g, pltpu.roll(whole, 7, 0))
            g_state = loc + after
            now = state_ref[at, :]
            last = jnp.maximum(tile * 8 - 1, 0)
            first = jnp.where(tile == 0, head_ref[0], state_ref[pl.ds(last, 1), :])
            before = jnp.where(place == 0, first, pltpu.roll(now, 1, 0))
            g_forget = g_state * (before - act)
            total = total + g_forget * (1.0 - sig_f)
            return g_state * keep * slope, g_forget * keep * sig_f, whole[0:1, :], total

        def one(i, carry):
            g, total = carry
            pair = pairs - 1 - i
            in_2, fg_2, g, total = half(2 * pair + 1, g, total)
            in_1, fg_1, g, total = half(2 * pair, g, total)
            at = pl.ds(pl.multiple_of(pair * 16, 16), 16)
            gin_ref[at, :] = jnp.concatenate([in_1, in_2], 0).astype(BF16)
            gfg_ref[at, :] = jnp.concatenate([fg_1, fg_2], 0).astype(BF16)
            return g, total

        _, total = lax.fori_loop(0, pairs, one, (tail_ref[0], jnp.zeros((8, wide), F32)))
        low_ref[0] = jnp.sum(total, axis=0, keepdims=True)

    row = pl.BlockSpec((1, wide), lambda b: (0, 0))
    block = pl.BlockSpec((pos_n, wide), lambda b: (b, 0))
    edge = pl.BlockSpec((1, 1, wide), lambda b: (b, 0, 0))
    return pl.pallas_call(
        body,
        grid=(blocks,),
        out_shape=[
            jax.ShapeDtypeStruct((blocks * pos_n, wide), BF16),
            jax.ShapeDtypeStruct((blocks * pos_n, wide), BF16),
            jax.ShapeDtypeStruct((blocks, 1, wide), F32),
        ],
        in_specs=[block, pl.BlockSpec((pos_n, wide), lambda b: (b, 1)), row, block, block, edge, edge],
        out_specs=[block, block, edge],
        compiler_params=params(),
    )(pre, pre, bound, local, state, head, tail)


def dot_nt(a, b):
    return lax.dot_general(a, b, (((1,), (1,)), ((), ())), preferred_element_type=F32)


def dot_nn(a, b):
    return lax.dot_general(a, b, (((1,), (0,)), ((), ())), preferred_element_type=F32)


def dot_tn(a, b):
    return lax.dot_general(a, b, (((0,), (0,)), ((), ())), preferred_element_type=F32)


def on_device(
    net,
    tokens,
    cotangent,
    lengths,
    in_gain,
    w_input,
    w_forget,
    w_output_gate,
    lower_bound,
    mix_gain,
    w_out,
    mlp_gain,
    w_gate,
    w_up,
    w_down,
):
    s, t = net.places()
    n_seq, n_tp = net.seq, net.tp
    slots, group, cols = tokens.shape
    width = cols * n_tp
    pos_n = group // n_tp
    rows = slots * pos_n
    dq = cols // n_seq
    fq = w_down.shape[0] // n_seq
    chan, hid = dq * n_tp, fq * n_tp
    order = [j for j in range(n_seq)]

    def quarter_t(w, q):
        return lax.dynamic_slice_in_dim(w, s * q, q, 1).T

    mix_w = jnp.concatenate(
        [quarter_t(w, dq) for w in (w_input, w_forget, w_output_gate)]
        + [lax.dynamic_slice_in_dim(w_out, s * dq, dq, 0)],
        0,
    )
    gate_w = jnp.concatenate([quarter_t(w_gate, fq), quarter_t(w_up, fq)], 0)
    down_w = lax.dynamic_slice_in_dim(w_down, s * fq, fq, 0)
    small = jnp.stack([lax.dynamic_slice_in_dim(v, s * dq, dq) for v in (lower_bound, mix_gain)], 0)

    def to_rows(x):
        pieces = split_rows(x, net.ahead, pos_n)
        return [pieces[0]] + [net.shift(pieces[k], k) for k in range(1, n_tp)]

    def from_rows(x, dtype):
        pieces = split_columns(x, net.ahead, slots, pos_n, cols)
        moved = [pieces[0]] + [net.shift(pieces[k], k) for k in range(1, n_tp)]
        return join_rows(moved, net.behind, dtype)

    def live_of(j):
        where = lax.bitwise_xor(s, j) * group + t * pos_n + jnp.arange(pos_n, dtype=jnp.int32)
        return (where[None, :] < lengths[:, None]).astype(F32).reshape(rows, 1)

    live = live_of(0)
    tok, normed_own = norm_tokens(to_rows(tokens), net.behind, in_gain)
    normed = jnp.concatenate(net.quad_gather(normed_own), 0)

    gathered_small = [small] + [net.shift(small, k) for k in range(1, n_tp)]
    bound = jnp.concatenate([g[0] for g in gathered_small], 0).reshape(1, chan)
    gain = jnp.concatenate([g[1] for g in gathered_small], 0).reshape(1, chan)
    gathered_gain = jnp.stack([mlp_gain] + [net.shift(mlp_gain, k) for k in range(1, n_tp)], 0)
    mlp_full = jnp.zeros((n_tp, cols), F32).at[net.behind].set(gathered_gain).reshape(1, width)

    mix_all = net.ring_gather(mix_w)
    w3 = jnp.concatenate([w[i * dq : (i + 1) * dq] for i in range(3) for w in mix_all], 0)
    wo = jnp.concatenate([w[3 * dq :] for w in mix_all], 0)
    gate_all = net.ring_gather(gate_w)
    wg = jnp.concatenate([w[:fq] for w in gate_all], 0)
    wu = jnp.concatenate([w[fq:] for w in gate_all], 0)
    wd = jnp.concatenate(net.ring_gather(down_w), 0)

    pre = dot_nt(normed, w3)
    decay, end = scan_ends(pre, bound, pos_n)

    place = jnp.concatenate([jnp.stack([s, t]), jnp.zeros((n_tp,), jnp.int32).at[net.behind].set(jnp.arange(n_tp, dtype=jnp.int32))])

    def spread(v):
        lead = v.shape[:-1]
        out = [v]
        for k in range(1, n_tp):
            moved = net.shift(v, k).reshape(lead + (n_tp, dq))
            out.append(jnp.roll(moved, k, axis=-2).reshape(v.shape))
        return jnp.stack(out, 0)

    both = spread(jnp.stack([decay, end], 0).reshape(2, n_seq, slots, chan))
    decays, ends = both[:, 0], both[:, 1]
    head = scan_heads(place, decays, ends, False).reshape(n_seq * slots, 1, chan)
    state, mix, squares = scan_states(pre, bound, gain, head, pos_n)
    total = net.quad_total(squares[:, 0].reshape(n_seq, rows))
    r_mix = lax.rsqrt(total / width + EPS).reshape(n_seq * rows, 1)
    part = dot_nn(mix, wo).astype(BF16).reshape(n_seq, rows, width)
    branch = sum(p.astype(F32) for p in net.quad_scatter([part[j] for j in order]))
    resid = tok.astype(F32) + r_mix[:rows] * branch
    r_mlp = lax.rsqrt(jnp.mean(resid * resid, axis=-1, keepdims=True) + EPS)
    scaled = resid * r_mlp
    mlp_in = jnp.concatenate(net.quad_gather((scaled * mlp_full).astype(BF16)), 0)

    gate_pre = dot_nt(mlp_in, wg)
    up_pre = dot_nt(mlp_in, wu)
    sig_g = sigmoid(gate_pre)
    act_g = gate_pre * sig_g
    slope_g = sig_g * (1.0 + gate_pre * (1.0 - sig_g))
    hidden = (act_g * up_pre).astype(BF16)
    part = dot_nn(hidden, wd).astype(BF16).reshape(n_seq, rows, width)
    ffn = sum(p.astype(F32) for p in net.quad_scatter([part[j] for j in order]))
    mixed = from_rows((live * (resid + ffn)).astype(BF16), BF16)

    cot = mask_rows(to_rows(cotangent), net.behind, live)
    grad_out = jnp.concatenate(net.quad_gather(cot), 0)
    grad_hidden = dot_nt(grad_out, wd)
    grad_gate = (grad_hidden * up_pre * slope_g).astype(BF16)
    grad_up = (grad_hidden * act_g).astype(BF16)
    part = (dot_nn(grad_gate, wg) + dot_nn(grad_up, wu)).astype(BF16).reshape(n_seq, rows, width)
    grad_mlp_in = sum(p.astype(F32) for p in net.quad_scatter([part[j] for j in order]))

    def reduce_rows(pairs):
        def chunk(d, add):
            out = jnp.concatenate(
                [dot_tn(left[:, d * q : (d + 1) * q], right) for left, right, q in pairs], 0
            )
            for a in add:
                out = out + a.astype(F32)
            return out.astype(BF16)

        return net.ring_scatter(chunk)

    def whole_rows(x):
        blocks = net.quad_gather(x)
        out = jnp.zeros((n_seq,) + x.shape, F32)
        for j in order:
            out = lax.dynamic_update_index_in_dim(out, blocks[j].astype(F32), lax.bitwise_xor(s, j), 0)
        return out

    grad_w_down = whole_rows(reduce_rows([(hidden, grad_out, fq)])).reshape(n_seq * fq, width)
    grad_gu = whole_rows(reduce_rows([(grad_gate, mlp_in, fq), (grad_up, mlp_in, fq)]))
    grad_w_gate = grad_gu[:, :fq].reshape(n_seq * fq, width).T
    grad_w_up = grad_gu[:, fq:].reshape(n_seq * fq, width).T

    grad_mlp_gain = jnp.sum(grad_mlp_in * scaled, axis=0)
    grad_scaled = grad_mlp_in * mlp_full
    inner = jnp.sum(resid * grad_scaled, axis=-1, keepdims=True)
    grad_resid = cot.astype(F32) + r_mlp * grad_scaled - resid * r_mlp**3 * inner / width
    grad_branch = jnp.concatenate(net.quad_gather(grad_resid.astype(BF16)), 0)

    grad_mix = dot_nt(grad_branch, wo)
    pre_og = pre[:, 2 * chan :]
    sig_o = sigmoid(pre_og)
    act_o = pre_og * sig_o
    slope_o = sig_o * (1.0 + pre_og * (1.0 - sig_o))
    state_norm = state * r_mix
    grad_mix_gain = jnp.sum(grad_mix * state_norm * act_o, axis=0)
    grad_og = (grad_mix * state_norm * gain * slope_o).astype(BF16)
    grad_norm = grad_mix * gain * act_o
    inner = net.quad_total(jnp.sum(state * grad_norm, axis=-1).reshape(n_seq, rows)).reshape(-1, 1)
    grad_local = r_mix * grad_norm - state * (r_mix**3 * inner / width)
    back_end = spread(back_ends(pre, bound, grad_local, pos_n).reshape(n_seq, slots, chan))
    tail = scan_heads(place, decays, back_end, True).reshape(n_seq * slots, 1, chan)
    grad_in, grad_fg, low_sums = back_states(pre, bound, grad_local, state, head, tail, pos_n)
    mixer_out = (mix.astype(F32) * r_mix).astype(BF16)
    grad_3 = jnp.concatenate([grad_in, grad_fg, grad_og], 1)
    part = dot_nn(grad_3, w3).astype(BF16).reshape(n_seq, rows, width)
    grad_normed = sum(p.astype(F32) for p in net.quad_scatter([part[j] for j in order]))

    grad_mw = whole_rows(
        reduce_rows(
            [(grad_3[:, i * chan : (i + 1) * chan], normed, dq) for i in range(3)]
            + [(mixer_out, grad_branch, dq)]
        )
    )
    grads_3 = [grad_mw[:, i * dq : (i + 1) * dq].reshape(n_seq * dq, width).T for i in range(3)]
    grad_w_out = grad_mw[:, 3 * dq :].reshape(n_seq * dq, width)

    x = tok.astype(F32)
    r_in = lax.rsqrt(jnp.mean(x * x, axis=-1, keepdims=True) + EPS)
    grad_in_gain = jnp.sum(grad_normed * x * r_in, axis=0)
    scaled_g = grad_normed * in_gain
    inner = jnp.sum(x * scaled_g, axis=-1, keepdims=True)
    grad_tok = grad_resid + r_in * scaled_g - x * r_in**3 * inner / width
    grad_tokens = from_rows(grad_tok.astype(BF16), F32)

    full = lax.psum(jnp.stack([grad_in_gain, grad_mlp_gain], 0), ("seq", "tp"))
    mine = lax.dynamic_slice_in_dim(full, t * cols, cols, 1)
    sums = jnp.stack([jnp.sum(low_sums, axis=(0, 1)), grad_mix_gain], 0).reshape(2, n_tp, dq)
    chans = sums[:, 0]
    for k in range(1, n_tp):
        chans = chans + net.shift(sums[:, (n_tp - k) % n_tp], k)
    chans = whole_rows(chans)
    return (
        mixed,
        grad_tokens,
        mine[0],
        grads_3[0],
        grads_3[1],
        grads_3[2],
        chans[:, 0].reshape(-1),
        chans[:, 1].reshape(-1),
        grad_w_out,
        mine[1],
        grad_w_gate,
        grad_w_up,
        grad_w_down,
    )


def solution(mesh):
    return jax.shard_map(
        functools.partial(on_device, Net(mesh)),
        mesh=mesh,
        in_specs=(
            P(None, "seq", "tp"),
            P(None, "seq", "tp"),
            P(),
            P(),
            P(None, "tp"),
            P(None, "tp"),
            P(None, "tp"),
            P("tp"),
            P("tp"),
            P("tp", None),
            P("tp"),
            P(None, "tp"),
            P(None, "tp"),
            P("tp", None),
        ),
        out_specs=(
            P(None, "seq", "tp"),
            P(None, "seq", "tp"),
            P("tp"),
            P(None, "tp"),
            P(None, "tp"),
            P(None, "tp"),
            P("tp"),
            P("tp"),
            P("tp", None),
            P("tp"),
            P(None, "tp"),
            P(None, "tp"),
            P("tp", None),
        ),
        check_vma=False,
    )
```

time: 2730 us -> 1270 us (0.47)
  waiting for transfers between devices: 1510 us -> 394 us
  local copies, waits for them, and re-layouts: 548 us -> 131 us
  starting transfers between devices: 0.77 us -> 234 us
  blocking collectives: 200 us -> 39.1 us
  Pallas kernels: 0 us -> 89 us
  other arithmetic: 171 us -> 96.9 us
    reduce_scatter x4 -> x0, waiting for transfers between devices: 816 us -> none  [the longest x1 210 us: on_device(): lax.psum_scatter(in_term.astype(jnp.bfloat16), 'tp', scatter_dimension=2,...]
    all_gather x4 -> x0, waiting for transfers between devices: 566 us -> none  [the longest x1 181 us: on_device(): full_tokens = lax.all_gather(tokens, 'tp', axis=2, tiled=True)]
    ppermute x0 -> x151, waiting for transfers between devices: none -> 394 us  [the longest x111 334 us: shift(): lax.ppermute(x, 'tp', [(self.cycle[i], self.cycle[(i + k) % n]) for i in...]
    slice x142 -> x40, local copies, waits for them, and re-layouts: 326 us -> 28 us  [the longest x1 10.7 us: on_device(): grad_w_up = grad_gu[:, fq:].reshape(n_seq * fq, width).T]
    ppermute x0 -> x151, starting transfers between devices: none -> 234 us  [the longest x111 216 us: shift(): lax.ppermute(x, 'tp', [(self.cycle[i], self.cycle[(i + k) % n]) for i in...]
    pad x72 -> x0, local copies, waits for them, and re-layouts: 154 us -> none  [linear_scan(): return lax.associative_scan(combine_pair, (decay, drive), axis=1)]
    psum x1 -> x0, waiting for transfers between devices: 122 us -> none  [on_device(): lax.psum(grad_w_input.astype(jnp.bfloat16), 'seq').astype(jnp.float32)]
    psum x5 -> x1, blocking collectives: 146 us -> 39.1 us  [on_device(): full = lax.psum(jnp.stack([grad_in_gain, grad_mlp_gain], 0), ('seq', 'tp'))]
  transfers between devices with their start and end apart: 9 -> 151, of which waited for: 9 -> 42; matrix products, arithmetic and copies ran while one was open for 8% -> 28% of each run, Pallas kernels for 0% -> 7%
where the time goes in v1:
time: 1270 us; the launch traced here: 1260 us
  waiting for transfers between devices  394 us (31%)
  matrix products  274 us (22%)
  starting transfers between devices  234 us (18%)
  local copies, waits for them, and re-layouts  131 us (10%)
  other arithmetic  96.9 us (8%)
  Pallas kernels  89 us (7%)
  blocking collectives  39.1 us (3%)
    ppermute x111, waiting for transfers between devices, shift(): lax.ppermute(x, 'tp', [(self.cycle[i], self.cycle[(i + k) % n]) for i in...  334 us
    ppermute x111, starting transfers between devices, shift(): lax.ppermute(x, 'tp', [(self.cycle[i], self.cycle[(i + k) % n]) for i in...  216 us
    dot_general x56, matrix products, dot_tn(): lax.dot_general(a, b, (((0,), (0,)), ((), ())), preferred_element_type=F32)  140 us
    dot_general x5, matrix products, dot_nt(): lax.dot_general(a, b, (((1,), (1,)), ((), ())), preferred_element_type=F32)  68.8 us
    dot_general x5, matrix products, dot_nn(): lax.dot_general(a, b, (((1,), (0,)), ((), ())), preferred_element_type=F32)  65 us
    unnamed x357, local copies, waits for them, and re-layouts  64.9 us
    ppermute x40, waiting for transfers between devices, swap(): return lax.ppermute(x, 'seq', [(i, i ^ bit) for i in range(self.seq)])  60 us
    psum x1, blocking collectives, on_device(): full = lax.psum(jnp.stack([grad_in_gain, grad_mlp_gain], 0), ('seq', 'tp'))  39.1 us
  transfers between devices with their start and end apart: 151, of which 42 were waited for; matrix products, arithmetic and copies ran while one was open for 28% of the time, Pallas kernels for 7%

profile of v1, /device:TPU:0, one launch (start us, length us, event | category | flops | bytes accessed | tf_op | source)
XLA Modules:
  0.0 1261.1 jit_solution(18357552001447090816)
XLA Ops:
  60.0 17.6 %collective-permute-start.78 = (bf16[3,128,256]{2,1,0:T(8,128)(2,1)}, bf16[3,128,256]{2,1,0:T(8,128)(2,1)S(1)}, u32[]{:S(2)}, u32[]{:S(2)}) collective-permute-start(bf16[3,128,256]{2,1,0:T(8,128)(2,1)} %get-tuple-element.83), channel_id=1, source_target_pairs={{0,3},{2,1},{4,0},{6,2},{7,4},{5,6},{3,7},{1,5},{8,11},{10,9},{12,... | collective-permute-start | bytes 589832 | tf_op jit(solution)/shard_map/ppermute | solution.py:61
  85.6 15.7 %collective-permute-start.2 = (bf16[3,128,256]{2,1,0:T(8,128)(2,1)}, bf16[3,128,256]{2,1,0:T(8,128)(2,1)S(1)}, u32[]{:S(2)}, u32[]{:S(2)}) collective-permute-start(bf16[3,128,256]{2,1,0:T(8,128)(2,1)} %get-tuple-element.58), channel_id=1, source_target_pairs={{0,6},{2,7},{4,5},{6,3},{7,1},{5,0},{3,2},{1,4},{8,14},{10,15},{12... | collective-permute-start | bytes 589832 | tf_op jit(solution)/shard_map/ppermute | solution.py:61
  125.2 25.4 %collective-permute-done.5.refs_6_ = bf16[3,128,256]{2,1,0:T(8,128)(2,1)} collective-permute-done((bf16[3,128,256]{2,1,0:T(8,128)(2,1)}, bf16[3,128,256]{2,1,0:T(8,128)(2,1)}, u32[]{:S(2)}, u32[]{:S(2)}) %collective-permute-start.5) | collective-permute-done | bytes 196640 | tf_op jit(solution)/shard_map/ppermute | solution.py:61
  170.8 21.4 %collective-permute-done.56 = bf16[176,2048]{1,0:T(8,128)(2,1)} collective-permute-done((bf16[176,2048]{1,0:T(8,128)(2,1)}, bf16[176,2048]{1,0:T(8,128)(2,1)}, u32[]{:S(2)}, u32[]{:S(2)}) %collective-permute-start.56) | collective-permute-done | bytes 720928 | tf_op jit(solution)/shard_map/ppermute | solution.py:61
  214.5 12.4 collective-permute-done.11
  230.1 12.3 collective-permute-done.57
  246.7 22.6 %collective-permute-done.58 = bf16[88,2048]{1,0:T(8,128)(2,1)S(1)} collective-permute-done((bf16[88,2048]{1,0:T(8,128)(2,1)S(1)}, bf16[88,2048]{1,0:T(8,128)(2,1)S(1)}, u32[]{:S(2)}, u32[]{:S(2)}) %collective-permute-start.58) | collective-permute-done | bytes 360480 | tf_op jit(solution)/shard_map/ppermute | solution.py:61
  292.0 22.6 %collective-permute-done.17 = bf16[128,2048]{1,0:T(8,128)(2,1)S(1)} collective-permute-done((bf16[128,2048]{1,0:T(8,128)(2,1)S(1)}, bf16[128,2048]{1,0:T(8,128)(2,1)S(1)}, u32[]{:S(2)}, u32[]{:S(2)}) %collective-permute-start.17) | collective-permute-done | bytes 524320 | tf_op jit(solution)/shard_map/ppermute | solution.py:61
  318.6 12.6 fusion.202.in_ref.fg_ref.og_ref
  369.2 25.0 %shard_map.259 = (f32[1536,512]{1,0:T(8,128)}, bf16[1536,512]{1,0:T(8,128)(2,1)}, f32[1536,128]{1,0:T(8,128)}) custom-call(f32[1536,1536]{1,0:T(8,128)} %fusion.202.in_ref.fg_ref.og_ref, f32[1536,1536]{1,0:T(8,128)} %fusion.202.in_ref.fg_ref.og_ref, f32[1536,1536]{1,0:T(8,128)} %fusion.202.in_ref.fg_ref.og_ref, f32[1,512]{1,0:T(1,128)} %bitcast.434, ...), custom_call_target="tpu_custom_call" | custom-call | tf_op jit(solution)/shard_map/pallas_call | solution.py:344
  419.2 23.8 %collective-permute-done.49 = bf16[352,2048]{1,0:T(8,128)(2,1)S(1)} collective-permute-done((bf16[352,2048]{1,0:T(8,128)(2,1)}, bf16[352,2048]{1,0:T(8,128)(2,1)S(1)}, u32[]{:S(2)}, u32[]{:S(2)}) %collective-permute-start.49) | collective-permute-done | bytes 1441824 | tf_op jit(solution)/shard_map/ppermute | solution.py:61
  475.5 18.5 %collective-permute-done.45 = bf16[384,2048]{1,0:T(8,128)(2,1)} collective-permute-done((bf16[384,2048]{1,0:T(8,128)(2,1)}, bf16[384,2048]{1,0:T(8,128)(2,1)}, u32[]{:S(2)}, u32[]{:S(2)}) %collective-permute-start.45) | collective-permute-done | bytes 1572896 | tf_op jit(solution)/shard_map/ppermute | solution.py:64
  515.9 22.8 %multiply_convert_fusion.1 = (bf16[1536,1408]{0,1:T(8,128)(2,1)S(1)}, bf16[1536,1408]{0,1:T(8,128)(2,1)}, bf16[1536,1408]{0,1:T(8,128)(2,1)}) fusion(f32[1536,1408]{0,1:T(8,128)} %fusion.204, f32[1536,1408]{0,1:T(8,128)} %fusion.203, bf16[1536,2048]{1,0:T(8,128)(2,1)} %copy-done.25, bf16[1408,2048]{1,0:T(8,128)(2,1)} %get-tuple-element.170), kind=kOutput, calls=%fused_computation.6 | convolution fusion | flops 8890810368 | bytes 42336256 | tf_op jit(solution)/shard_map/dot_general | solution.py:451
  538.7 17.8 %fusion.205 = f32[1536,2048]{1,0:T(8,128)} fusion(bf16[1536,1408]{0,1:T(8,128)(2,1)} %get-tuple-element.150, bf16[1408,2048]{1,0:T(8,128)(2,1)} %get-tuple-element.171), kind=kOutput, calls=%fused_computation.464 | convolution fusion | flops 8858370048 | bytes 22675456 | tf_op jit(solution)/shard_map/dot_general | solution.py:455
  601.7 15.8 %add_convert_fusion = bf16[1536,2048]{1,0:T(8,128)(2,1)S(1)} fusion(f32[1536,2048]{1,0:T(8,128)} %fusion.205, bf16[1536,1408]{0,1:T(8,128)(2,1)} %copy-done.121, bf16[1408,2048]{1,0:T(8,128)(2,1)} %get-tuple-element.170), kind=kOutput, calls=%fused_computation.4 | convolution fusion | flops 8864661504 | bytes 28966912 | tf_op jit(solution)/shard_map/dot_general | solution.py:455
  628.5 19.0 %collective-permute-done.144 = bf16[88,2048]{1,0:T(8,128)(2,1)S(1)} collective-permute-done((bf16[88,2048]{1,0:T(8,128)(2,1)S(1)}, bf16[88,2048]{1,0:T(8,128)(2,1)S(1)}, u32[]{:S(2)}, u32[]{:S(2)}) %collective-permute-start.144) | collective-permute-done | bytes 360480 | tf_op jit(solution)/shard_map/ppermute | solution.py:61
  691.5 30.0 %collective-permute-done.146 = bf16[176,2048]{1,0:T(8,128)(2,1)S(1)} collective-permute-done((bf16[176,2048]{1,0:T(8,128)(2,1)S(1)}, bf16[176,2048]{1,0:T(8,128)(2,1)S(1)}, u32[]{:S(2)}, u32[]{:S(2)}) %collective-permute-start.146) | collective-permute-done | bytes 720928 | tf_op jit(solution)/shard_map/ppermute | solution.py:61
  764.1 28.5 %collective-permute-done.65 = bf16[384,2048]{1,0:T(8,128)(2,1)S(1)} collective-permute-done((bf16[384,2048]{1,0:T(8,128)(2,1)S(1)}, bf16[384,2048]{1,0:T(8,128)(2,1)S(1)}, u32[]{:S(2)}, u32[]{:S(2)}) %collective-permute-start.65) | collective-permute-done | bytes 1572896 | tf_op jit(solution)/shard_map/ppermute | solution.py:64
  851.3 21.9 %collective-permute-done.136 = bf16[352,2048]{1,0:T(8,128)(2,1)} collective-permute-done((bf16[352,2048]{1,0:T(8,128)(2,1)}, bf16[352,2048]{1,0:T(8,128)(2,1)}, u32[]{:S(2)}, u32[]{:S(2)}) %collective-permute-start.136) | collective-permute-done | bytes 1441824 | tf_op jit(solution)/shard_map/ppermute | solution.py:61
  983.3 13.0 %shard_map.266 = (bf16[1536,512]{1,0:T(8,128)(2,1)}, bf16[1536,512]{1,0:T(8,128)(2,1)}, f32[12,1,512]{2,1,0:T(1,128)}) custom-call(f32[1536,1536]{1,0:T(8,128)} %fusion.202.in_ref.fg_ref.og_ref, f32[1536,1536]{1,0:T(8,128)} %fusion.202.in_ref.fg_ref.og_ref, f32[1,512]{1,0:T(1,128)} %bitcast.436, f32[1536,512]{1,0:T(8,128)} %get-tuple-element.152.local_ref, ...), custom_call_target="tpu_custom_call" | custom-call | tf_op jit(solution)/shard_map/pallas_call | solution.py:436
  1001.5 13.8 %convolution_convert_fusion = bf16[1536,2048]{1,0:T(8,128)(2,1)S(1)} fusion(bf16[1536,2048]{1,0:T(8,128)(2,1)} %copy-done.107, bf16[1536,512]{1,0:T(8,128)(2,1)S(1)} %copy-done.10, bf16[1536,512]{1,0:T(8,128)(2,1)} %get-tuple-element.87, bf16[1536,512]{1,0:T(8,128)(2,1)} %get-tuple-element.86), kind=kOutput, calls=%fused_computation.10 | convolution fusion | flops 9680977920 | bytes 17301504 | tf_op jit(solution)/shard_map/dot_general | solution.py:455
  1089.7 16.3 %collective-permute-done.113 = bf16[256,2048]{1,0:T(8,128)(2,1)S(1)} collective-permute-done((bf16[256,2048]{1,0:T(8,128)(2,1)S(1)}, bf16[256,2048]{1,0:T(8,128)(2,1)S(1)}, u32[]{:S(2)}, u32[]{:S(2)}) %collective-permute-start.113) | collective-permute-done | bytes 1048608 | tf_op jit(solution)/shard_map/ppermute | solution.py:61
  1117.2 14.0 %collective-permute-done.114 = bf16[256,2048]{1,0:T(8,128)(2,1)S(1)} collective-permute-done((bf16[256,2048]{1,0:T(8,128)(2,1)S(1)}, bf16[256,2048]{1,0:T(8,128)(2,1)S(1)}, u32[]{:S(2)}, u32[]{:S(2)}) %collective-permute-start.114) | collective-permute-done | bytes 1048608 | tf_op jit(solution)/shard_map/ppermute | solution.py:61
  1197.6 39.1 %psum.7 = f32[2,2048]{1,0:T(2,128)} all-reduce(f32[2,2048]{1,0:T(2,128)S(1)} %pad_maximum_fusion.21), channel_id=1, replica_groups=mesh['seq'=4,'tp'=8] {'seq','tp'}, use_global_device_ids=true, to_apply=%region_9.10 | all-reduce | flops 4096 | bytes 32768 | tf_op jit(solution)/shard_map/psum | solution.py:642
  (926 shorter events, 775.8 us)
Async XLA Ops:
  106.2 54.8 %collective-permute-start.10 = (bf16[256,2048]{1,0:T(8,128)(2,1)}, bf16[256,2048]{1,0:T(8,128)(2,1)S(1)}, u32[]{:S(2)}, u32[]{:S(2)}) collective-permute-start(bf16[256,2048]{1,0:T(8,128)(2,1)} %pad_maximum_fusion.4), channel_id=1, source_target_pairs={{0,2},{2,4},{4,6},{6,7},{7,5},{5,3},{3,1},{1,0},{8,10},{10,12},{12... | collective-permute-start | bytes 3145736 | tf_op jit(solution)/shard_map/ppermute | solution.py:61
  106.2 53.2 %collective-permute-start.55 = (bf16[176,2048]{1,0:T(8,128)(2,1)S(1)}, bf16[176,2048]{1,0:T(8,128)(2,1)}, u32[]{:S(2)}, u32[]{:S(2)}) collective-permute-start(bf16[176,2048]{1,0:T(8,128)(2,1)S(1)} %get-tuple-element.140), channel_id=1, source_target_pairs={{0,2},{2,4},{4,6},{6,7},{7,5},{5,3},{3,1},{1,0},{8,10},{10,12},{12... | collective-permute-start | bytes 2162696 | tf_op jit(solution)/shard_map/ppermute | solution.py:61
  150.6 52.6 %collective-permute-start.47 = (bf16[352,2048]{1,0:T(8,128)(2,1)}, bf16[352,2048]{1,0:T(8,128)(2,1)}, u32[]{:S(2)}, u32[]{:S(2)}) collective-permute-start(bf16[352,2048]{1,0:T(8,128)(2,1)} %pad_maximum_fusion.3), channel_id=1, source_target_pairs={{0,2},{2,4},{4,6},{6,7},{7,5},{5,3},{3,1},{1,0},{8,10},{10,12},{12... | collective-permute-start | bytes 4325384 | tf_op jit(solution)/shard_map/ppermute | solution.py:61
  159.4 51.0 %collective-permute-start.7 = (bf16[384,2048]{1,0:T(8,128)(2,1)}, bf16[384,2048]{1,0:T(8,128)(2,1)}, u32[]{:S(2)}, u32[]{:S(2)}) collective-permute-start(bf16[384,2048]{1,0:T(8,128)(2,1)} %get-tuple-element.64), channel_id=1, source_target_pairs={{0,8},{8,0},{16,24},{24,16},{1,9},{9,1},{17,25},{25,17},{2,10},{10... | collective-permute-start | bytes 4718600 | tf_op jit(solution)/shard_map/ppermute | solution.py:64
  159.4 51.6 %collective-permute-start.8 = (bf16[384,2048]{1,0:T(8,128)(2,1)}, bf16[384,2048]{1,0:T(8,128)(2,1)}, u32[]{:S(2)}, u32[]{:S(2)}) collective-permute-start(bf16[384,2048]{1,0:T(8,128)(2,1)} %get-tuple-element.64), channel_id=1, source_target_pairs={{0,16},{8,24},{16,0},{24,8},{1,17},{9,25},{17,1},{25,9},{2,18},{10... | collective-permute-start | bytes 4718600 | tf_op jit(solution)/shard_map/ppermute | solution.py:64
  211.0 69.6 %collective-permute-start.9 = (bf16[384,2048]{1,0:T(8,128)(2,1)}, bf16[384,2048]{1,0:T(8,128)(2,1)S(1)}, u32[]{:S(2)}, u32[]{:S(2)}) collective-permute-start(bf16[384,2048]{1,0:T(8,128)(2,1)} %collective-permute-done.8), channel_id=1, source_target_pairs={{0,8},{8,0},{16,24},{24,16},{1,9},{9,1},{17,25},{25,17},{2,10},{10... | collective-permute-start | bytes 4718600 | tf_op jit(solution)/shard_map/ppermute | solution.py:64
  226.8 51.4 %collective-permute-start.12 = (bf16[256,2048]{1,0:T(8,128)(2,1)S(1)}, bf16[256,2048]{1,0:T(8,128)(2,1)S(1)}, u32[]{:S(2)}, u32[]{:S(2)}) collective-permute-start(bf16[256,2048]{1,0:T(8,128)(2,1)S(1)} %collective-permute-done.11), channel_id=1, source_target_pairs={{0,2},{2,4},{4,6},{6,7},{7,5},{5,3},{3,1},{1,0},{8,10},{10,12},{12... | collective-permute-start | bytes 3145736 | tf_op jit(solution)/shard_map/ppermute | solution.py:61
  230.0 49.3 %collective-permute-start.16 = (bf16[256,2048]{1,0:T(8,128)(2,1)S(1)}, bf16[256,2048]{1,0:T(8,128)(2,1)S(1)}, u32[]{:S(2)}, u32[]{:S(2)}) collective-permute-start(bf16[256,2048]{1,0:T(8,128)(2,1)S(1)} %collective-permute-done.15), channel_id=1, source_target_pairs={{0,1},{2,0},{4,2},{6,4},{7,6},{5,7},{3,5},{1,3},{8,9},{10,8},{12,1... | collective-permute-start | bytes 3145736 | tf_op jit(solution)/shard_map/ppermute | solution.py:61
  269.3 91.9 %collective-permute-start.51 = (bf16[352,2048]{1,0:T(8,128)(2,1)}, bf16[352,2048]{1,0:T(8,128)(2,1)}, u32[]{:S(2)}, u32[]{:S(2)}) collective-permute-start(bf16[352,2048]{1,0:T(8,128)(2,1)} %pad_maximum_fusion.3), channel_id=1, source_target_pairs={{0,1},{2,0},{4,2},{6,4},{7,6},{5,7},{3,5},{1,3},{8,9},{10,8},{12,1... | collective-permute-start | bytes 4325384 | tf_op jit(solution)/shard_map/ppermute | solution.py:61
  275.1 86.1 %collective-permute-start.81 = (bf16[384,2048]{1,0:T(8,128)(2,1)}, bf16[384,2048]{1,0:T(8,128)(2,1)}, u32[]{:S(2)}, u32[]{:S(2)}) collective-permute-start(bf16[384,2048]{1,0:T(8,128)(2,1)} %shard_map.263), channel_id=1, source_target_pairs={{0,16},{8,24},{16,0},{24,8},{1,17},{9,25},{17,1},{25,9},{2,18},{10... | collective-permute-start | bytes 4718600 | tf_op jit(solution)/shard_map/ppermute | solution.py:64
  360.9 52.8 %collective-permute-start.80 = (bf16[384,2048]{1,0:T(8,128)(2,1)}, bf16[384,2048]{1,0:T(8,128)(2,1)S(1)}, u32[]{:S(2)}, u32[]{:S(2)}) collective-permute-start(bf16[384,2048]{1,0:T(8,128)(2,1)} %shard_map.263), channel_id=1, source_target_pairs={{0,8},{8,0},{16,24},{24,16},{1,9},{9,1},{17,25},{25,17},{2,10},{10... | collective-permute-start | bytes 4718600 | tf_op jit(solution)/shard_map/ppermute | solution.py:64
  363.2 52.0 %collective-permute-start.82 = (bf16[384,2048]{1,0:T(8,128)(2,1)}, bf16[384,2048]{1,0:T(8,128)(2,1)}, u32[]{:S(2)}, u32[]{:S(2)}) collective-permute-start(bf16[384,2048]{1,0:T(8,128)(2,1)} %collective-permute-done.81), channel_id=1, source_target_pairs={{0,8},{8,0},{16,24},{24,16},{1,9},{9,1},{17,25},{25,17},{2,10},{10... | collective-permute-start | bytes 4718600 | tf_op jit(solution)/shard_map/ppermute | solution.py:64
  618.0 68.8 %collective-permute-start.84 = (bf16[384,2048]{1,0:T(8,128)(2,1)S(1)}, bf16[384,2048]{1,0:T(8,128)(2,1)S(1)}, u32[]{:S(2)}, u32[]{:S(2)}) collective-permute-start(bf16[384,2048]{1,0:T(8,128)(2,1)S(1)} %get-tuple-element.163), channel_id=1, source_target_pairs={{0,8},{8,0},{16,24},{24,16},{1,9},{9,1},{17,25},{25,17},{2,10},{10... | collective-permute-start | bytes 4718600 | tf_op jit(solution)/shard_map/ppermute | solution.py:64
  618.6 139.8 %collective-permute-start.83 = (bf16[384,2048]{1,0:T(8,128)(2,1)S(1)}, bf16[384,2048]{1,0:T(8,128)(2,1)S(1)}, u32[]{:S(2)}, u32[]{:S(2)}) collective-permute-start(bf16[384,2048]{1,0:T(8,128)(2,1)S(1)} %get-tuple-element.162), channel_id=1, source_target_pairs={{0,8},{8,0},{16,24},{24,16},{1,9},{9,1},{17,25},{25,17},{2,10},{10... | collective-permute-start | bytes 4718600 | tf_op jit(solution)/shard_map/ppermute | solution.py:64
  674.6 61.1 %collective-permute-start.134 = (bf16[352,2048]{1,0:T(8,128)(2,1)S(1)}, bf16[352,2048]{1,0:T(8,128)(2,1)S(1)}, u32[]{:S(2)}, u32[]{:S(2)}) collective-permute-start(bf16[352,2048]{1,0:T(8,128)(2,1)S(1)} %copy-done.64), channel_id=1, source_target_pairs={{0,1},{2,0},{4,2},{6,4},{7,6},{5,7},{3,5},{1,3},{8,9},{10,8},{12,1... | collective-permute-start | bytes 4325384 | tf_op jit(solution)/shard_map/ppermute | solution.py:61
  684.0 57.5 %collective-permute-start.130 = (bf16[352,2048]{1,0:T(8,128)(2,1)}, bf16[352,2048]{1,0:T(8,128)(2,1)}, u32[]{:S(2)}, u32[]{:S(2)}) collective-permute-start(bf16[352,2048]{1,0:T(8,128)(2,1)} %fusion.21), channel_id=1, source_target_pairs={{0,2},{2,4},{4,6},{6,7},{7,5},{5,3},{3,1},{1,0},{8,10},{10,12},{12... | collective-permute-start | bytes 4325384 | tf_op jit(solution)/shard_map/ppermute | solution.py:61
  753.6 51.6 %collective-permute-start.135 = (bf16[352,2048]{1,0:T(8,128)(2,1)}, bf16[352,2048]{1,0:T(8,128)(2,1)}, u32[]{:S(2)}, u32[]{:S(2)}) collective-permute-start(bf16[352,2048]{1,0:T(8,128)(2,1)} %fusion.23), channel_id=1, source_target_pairs={{0,1},{2,0},{4,2},{6,4},{7,6},{5,7},{3,5},{1,3},{8,9},{10,8},{12,1... | collective-permute-start | bytes 4325384 | tf_op jit(solution)/shard_map/ppermute | solution.py:61
  758.3 70.2 %collective-permute-start.131 = (bf16[352,2048]{1,0:T(8,128)(2,1)}, bf16[352,2048]{1,0:T(8,128)(2,1)}, u32[]{:S(2)}, u32[]{:S(2)}) collective-permute-start(bf16[352,2048]{1,0:T(8,128)(2,1)} %fusion.20), channel_id=1, source_target_pairs={{0,2},{2,4},{4,6},{6,7},{7,5},{5,3},{3,1},{1,0},{8,10},{10,12},{12... | collective-permute-start | bytes 4325384 | tf_op jit(solution)/shard_map/ppermute | solution.py:61
  762.7 48.4 %collective-permute-start.149 = (bf16[176,2048]{1,0:T(8,128)(2,1)}, bf16[176,2048]{1,0:T(8,128)(2,1)S(1)}, u32[]{:S(2)}, u32[]{:S(2)}) collective-permute-start(bf16[176,2048]{1,0:T(8,128)(2,1)} %get-tuple-element.253), channel_id=1, source_target_pairs={{0,16},{8,24},{16,0},{24,8},{1,17},{9,25},{17,1},{25,9},{2,18},{10... | collective-permute-start | bytes 2162696 | tf_op jit(solution)/shard_map/ppermute | solution.py:64
  883.4 188.8 %collective-permute-start.138 = (bf16[352,2048]{1,0:T(8,128)(2,1)}, bf16[352,2048]{1,0:T(8,128)(2,1)}, u32[]{:S(2)}, u32[]{:S(2)}) collective-permute-start(bf16[352,2048]{1,0:T(8,128)(2,1)} %get-tuple-element.132), channel_id=1, source_target_pairs={{0,16},{8,24},{16,0},{24,8},{1,17},{9,25},{17,1},{25,9},{2,18},{10... | collective-permute-start | bytes 4325384 | tf_op jit(solution)/shard_map/ppermute | solution.py:64
  1070.8 69.3 %collective-permute-start.98 = (bf16[384,2048]{1,0:T(8,128)(2,1)}, bf16[384,2048]{1,0:T(8,128)(2,1)S(1)}, u32[]{:S(2)}, u32[]{:S(2)}) collective-permute-start(bf16[384,2048]{1,0:T(8,128)(2,1)} %get-tuple-element.160), channel_id=1, source_target_pairs={{0,8},{8,0},{16,24},{24,16},{1,9},{9,1},{17,25},{25,17},{2,10},{10... | collective-permute-start | bytes 4718600 | tf_op jit(solution)/shard_map/ppermute | solution.py:64
  1172.1 70.1 %collective-permute-start.116 = (bf16[256,2048]{1,0:T(8,128)(2,1)S(1)}, bf16[256,2048]{1,0:T(8,128)(2,1)S(1)}, u32[]{:S(2)}, u32[]{:S(2)}) collective-permute-start(bf16[256,2048]{1,0:T(8,128)(2,1)S(1)} %get-tuple-element.136), channel_id=1, source_target_pairs={{0,8},{8,0},{16,24},{24,16},{1,9},{9,1},{17,25},{25,17},{2,10},{10... | collective-permute-start | bytes 3145736 | tf_op jit(solution)/shard_map/ppermute | solution.py:64
  1172.1 70.0 %collective-permute-start.117 = (bf16[256,2048]{1,0:T(8,128)(2,1)S(1)}, bf16[256,2048]{1,0:T(8,128)(2,1)S(1)}, u32[]{:S(2)}, u32[]{:S(2)}) collective-permute-start(bf16[256,2048]{1,0:T(8,128)(2,1)S(1)} %get-tuple-element.136), channel_id=1, source_target_pairs={{0,16},{8,24},{16,0},{24,8},{1,17},{9,25},{17,1},{25,9},{2,18},{10... | collective-permute-start | bytes 3145736 | tf_op jit(solution)/shard_map/ppermute | solution.py:64
  1184.5 53.6 %collective-permute-start.105 = (bf16[3,128,256]{2,1,0:T(8,128)(2,1)}, bf16[3,128,256]{2,1,0:T(8,128)(2,1)S(1)}, u32[]{:S(2)}, u32[]{:S(2)}) collective-permute-start(bf16[3,128,256]{2,1,0:T(8,128)(2,1)} %get-tuple-element.93), channel_id=1, source_target_pairs={{0,5},{2,3},{4,1},{6,0},{7,2},{5,4},{3,6},{1,7},{8,13},{10,11},{12... | collective-permute-start | bytes 589832 | tf_op jit(solution)/shard_map/ppermute | solution.py:61
  (269 other events, 5163.5 us)

commit v2 on v0

v2 whole, which is shorter than its diff:
```python
import functools

import jax
import jax.numpy as jnp
import numpy as np
from jax import lax
from jax.experimental import pallas as pl
from jax.experimental.pallas import tpu as pltpu
from jax.sharding import PartitionSpec as P

EPS = 1e-06
F32, BF16 = jnp.float32, jnp.bfloat16
VMEM_LIMIT = 56 * 1024 * 1024


def params(**more):
    return pltpu.CompilerParams(vmem_limit_bytes=VMEM_LIMIT, **more)


def sigmoid(v):
    return 1.0 / (1.0 + jnp.exp(-v))


def fast_sigmoid(v):
    d = 1.0 + jnp.exp(jnp.minimum(-v, 80.0))
    r = pl.reciprocal(d, approx=True)
    return r * (2.0 - d * r)


def ring_of(mesh):
    count = mesh.shape["tp"]
    try:
        coords = [tuple(d.coords) for d in mesh.devices[0]]
        ys = len({c[1] for c in coords})
    except (AttributeError, TypeError):
        ys = 2 if count % 2 == 0 else 1
    zs = count // ys
    if zs * ys != count or zs % 2 or ys < 2:
        return list(range(count))
    cycle = [(z, 0) for z in range(zs)]
    for turn, z in enumerate(reversed(range(zs))):
        across = range(1, ys) if turn % 2 == 0 else reversed(range(1, ys))
        cycle += [(z, y) for y in across]
    return [z * ys + y for z, y in cycle]


class Net:
    def __init__(self, mesh):
        self.seq, self.tp = mesh.shape["seq"], mesh.shape["tp"]
        self.cycle = ring_of(mesh)
        self.bits = [1 << b for b in range(self.seq.bit_length() - 1)]
        self.tp_bits = [1 << b for b in range(self.tp.bit_length() - 1)]

    def places(self):
        s, t = lax.axis_index("seq"), lax.axis_index("tp")
        where = np.zeros(self.tp, np.int32)
        for i, index in enumerate(self.cycle):
            where[index] = i
        pos = jnp.asarray(where)[t]
        steps = [[self.cycle[(i - d) % self.tp] for d in range(self.tp)] for i in where]
        self.order = lax.dynamic_index_in_dim(jnp.asarray(np.array(steps, np.int32)), t, 0, False)
        self.behind = [self.order[d] for d in range(self.tp)]
        self.inverse = (pos - jnp.asarray(where)) % self.tp
        return s, t

    def shift(self, x, k):
        n = self.tp
        return lax.ppermute(x, "tp", [(self.cycle[i], self.cycle[(i + k) % n]) for i in range(n)])

    def cross(self, x, bit):
        return lax.ppermute(x, "tp", [(i, i ^ bit) for i in range(self.tp)])

    def swap(self, x, bit):
        return lax.ppermute(x, "seq", [(i, i ^ bit) for i in range(self.seq)])

    def halves(self, size):
        half = size // 2
        return half // 16 * 16 if size >= 32 else half

    def gather_first(self, x):
        out = [x] + [None] * (self.seq - 1)
        for bit in reversed(self.bits):
            out[bit] = self.swap(x, bit)
        return out

    def gather_rest(self, out):
        out = list(out)
        for j in range(self.seq):
            if out[j] is None:
                out[j] = self.swap(out[j & (j - 1)], j & -j)
        return out

    def quad_far_part(self, parts):
        parts = list(parts)
        for bit in self.bits[:-1]:
            for j in reversed(range(0, len(parts), 2 * bit)):
                moved = self.swap(parts[j ^ bit], bit)
                parts[j] = (parts[j].astype(F32) + moved.astype(F32)).astype(BF16)
        return parts[0]

    def quad_near(self, parts):
        half = self.seq // 2
        far = self.quad_far_part(parts[half:])
        return [self.quad_far_part(parts[:half]), far]

    def quad_far(self, near):
        return [near[0], self.swap(near[1], self.bits[-1])]

    def total_step(self, x, bit):
        moved = self.swap(x, bit)
        return x + jnp.stack([moved[j ^ bit] for j in range(self.seq)], 0)

    def total_near(self, x):
        for bit in self.bits[:-1]:
            x = self.total_step(x, bit)
        return x

    def total_far(self, x):
        return self.total_step(x, self.bits[-1])


def after(x, *others):
    return lax.optimization_barrier((x,) + others)[0]


def hold(*trees):
    return lax.optimization_barrier(trees)


class RingGather:
    def __init__(self, net, x):
        self.net, self.size = net, x.shape[0]
        n = net.tp
        self.blocks = [[(x, 0)]] + [None] * (n - 1)
        self.full = (n - 1) // 2
        self.made = 0
        self.came = (x, x)

    def done(self):
        return self.made == self.net.tp // 2

    def sends(self):
        if self.done():
            return ()
        fore, back = self.came
        if self.made < self.full:
            return fore, back
        half = self.net.halves(self.size)
        return fore[:half], back[half:]

    def launch(self, sends):
        if self.done():
            return
        net, n = self.net, self.net.tp
        self.made += 1
        d = self.made
        self.came = net.shift(sends[0], 1), net.shift(sends[1], -1)
        if d <= self.full:
            self.blocks[d], self.blocks[n - d] = [(self.came[0], 0)], [(self.came[1], 0)]
        else:
            self.blocks[d] = [(self.came[0], 0), (self.came[1], net.halves(self.size))]

    def finish(self):
        while not self.done():
            self.launch(self.sends())

    def rows(self, start, q):
        out = []
        for block in self.blocks:
            whole = jnp.concatenate([a for a, _ in block], 0) if len(block) > 1 else block[0][0]
            out.append(whole[start : start + q])
        return out


class RingScatter:
    def __init__(self, net, chunk):
        self.net, self.chunk = net, chunk
        self.d = net.tp // 2
        self.came = ()
        self.half = net.halves(chunk(self.d).shape[0]) if net.tp % 2 == 0 else 0

    def done(self):
        return self.d == 0

    def plus(self, own, part, start):
        if part is None:
            return own
        rest = own.shape[0] - start - part.shape[0]
        return (own.astype(F32) + jnp.pad(part.astype(F32), ((start, rest), (0, 0)))).astype(BF16)

    def sends(self):
        if self.done():
            return ()
        n, d = self.net.tp, self.d
        if 2 * d == n:
            far = self.chunk(d)
            return far[: self.half], far[self.half :]
        fore, back = self.came if self.came else (None, None)
        return self.plus(self.chunk(n - d), fore, 0), self.plus(self.chunk(d), back, self.start())

    def start(self):
        return self.half if 2 * (self.d + 1) == self.net.tp else 0

    def launch(self, sends):
        if self.done():
            return
        self.d -= 1
        self.came = self.net.shift(sends[0], 1), self.net.shift(sends[1], -1)

    def result(self):
        while not self.done():
            self.launch(self.sends())
        own = self.chunk(0)
        start = self.start()
        return self.plus(self.plus(own, self.came[0], 0), self.came[1], start)


SMEM_SPEC = pl.BlockSpec(memory_space=pltpu.SMEM)
VMEM_SPEC = pl.BlockSpec(memory_space=pltpu.VMEM)


def norm_tokens(blocks, gain, rows):
    count, _, cols = blocks.shape
    width = count * cols

    def body(gain_ref, in_ref, x_ref, n_ref):
        total = jnp.zeros((rows, 1), F32)
        for k in range(count):
            c = in_ref[k, :rows].astype(F32)
            total += jnp.sum(c * c, axis=-1, keepdims=True)
        r = lax.rsqrt(total / width + EPS)
        for k in range(count):
            c = in_ref[k, :rows]
            at = slice(k * cols, (k + 1) * cols)
            x_ref[:, at] = c
            n_ref[:, at] = (c.astype(F32) * r * gain_ref[:, at]).astype(BF16)

    return pl.pallas_call(
        body,
        out_shape=[jax.ShapeDtypeStruct((rows, width), BF16)] * 2,
        in_specs=[VMEM_SPEC] * 2,
        out_specs=[VMEM_SPEC] * 2,
        compiler_params=params(),
    )(gain.reshape(1, width), blocks)


def mask_rows(blocks, live):
    count, rows, cols = blocks.shape
    width = count * cols

    def body(live_ref, in_ref, x_ref):
        for k in range(count):
            at = slice(k * cols, (k + 1) * cols)
            x_ref[:, at] = (in_ref[k].astype(F32) * live_ref[...]).astype(BF16)

    return pl.pallas_call(
        body,
        out_shape=jax.ShapeDtypeStruct((rows, width), BF16),
        in_specs=[VMEM_SPEC] * 2,
        out_specs=VMEM_SPEC,
        compiler_params=params(),
    )(live, blocks)


def tile_scan(decay, drive):
    place = lax.broadcasted_iota(jnp.int32, decay.shape, 0)
    for step in (1, 2, 4):
        inside = place >= step
        before_decay = jnp.where(inside, pltpu.roll(decay, step, 0), 1.0)
        before_drive = jnp.where(inside, pltpu.roll(drive, step, 0), 0.0)
        drive = drive + decay * before_drive
        decay = decay * before_decay
    return decay, drive


def tile_scan_up(decay, drive):
    place = lax.broadcasted_iota(jnp.int32, decay.shape, 0)
    for step in (1, 2, 4):
        inside = place < 8 - step
        before_decay = jnp.where(inside, pltpu.roll(decay, 8 - step, 0), 1.0)
        before_drive = jnp.where(inside, pltpu.roll(drive, 8 - step, 0), 0.0)
        drive = drive + decay * before_drive
        decay = decay * before_decay
    return decay, drive


def gates(pre_in, pre_fg, bound):
    sig_f = fast_sigmoid(pre_fg)
    forget = bound + (1.0 - bound) * sig_f
    sig_in = fast_sigmoid(pre_in)
    act_in = pre_in * sig_in
    slope_in = sig_in * (1.0 + pre_in * (1.0 - sig_in))
    keep = (1.0 - bound) * (1.0 - sig_f)
    return sig_f, forget, act_in, slope_in, keep


class Weights:
    def __init__(self):
        self.arrays, self.takes, self.shapes = [], [], []

    def add(self, ring, parts, stride, canonical):
        held, n = len(self.shapes), ring.net.tp
        width = ring.blocks[0][0][0].shape[1]
        self.shapes.append((len(parts) * n * stride, width))
        if stride % 16:
            for start, at in parts:
                rows = ring.rows(start, stride)
                whole = jnp.stack(rows, 0)
                if canonical:
                    whole = whole[ring.net.inverse]
                self.takes.append((len(self.arrays), 0, n * stride, held, None, at))
                self.arrays.append(whole.reshape(n * stride, width))
            return
        seen = {id(a): i for i, a in enumerate(self.arrays)}
        for d, block in enumerate(ring.blocks):
            for array, first in block:
                if id(array) not in seen:
                    seen[id(array)] = len(self.arrays)
                    self.arrays.append(array)
                for start, at in parts:
                    low, high = max(start, first), min(start + stride, first + array.shape[0])
                    if low < high:
                        place = (d, stride) if canonical else None
                        row = at + (low - start) + (0 if canonical else d * stride)
                        self.takes.append((seen[id(array)], low - first, high - low, held, place, row))

    def copies(self, order_ref, refs, held, sems):
        out = []
        for k, (source, first, size, to, place, row) in enumerate(self.takes):
            if place is not None:
                row = pl.multiple_of(order_ref[place[0]] * place[1] + row, 16)
            out.append(
                pltpu.make_async_copy(refs[source].at[pl.ds(first, size)], held[to].at[pl.ds(row, size)], sems.at[k])
            )
        return out


def step_kernel(body, order, count, rows, blocks, weights, ins, outs, width, cost, onto=()):
    any_spec = pl.BlockSpec(memory_space=pl.ANY)
    n_x, n_w, n_in, n_out = len(blocks), len(weights.arrays), len(ins), len(outs)
    n_part = count if width else 0
    n_held, n_onto = len(weights.shapes), len(onto)

    def kernel(order_ref, *refs):
        refs = list(refs)

        def take(k):
            out = refs[:k]
            del refs[:k]
            return out

        x_refs, w_refs, in_refs, _ = take(n_x), take(n_w), take(n_in), take(n_onto)
        out_refs, part_refs = take(n_out), take(n_part)
        held, w_sems = take(n_held), take(1)[0]
        xs, x_sems = take(2) if n_x else (None, None)
        kept, part_sems = take(2) if n_part else (None, None)
        j = pl.program_id(0)
        loads = weights.copies(order_ref, w_refs, held, w_sems)
        x_loads = [pltpu.make_async_copy(x_refs[k], xs.at[k], x_sems.at[k]) for k in range(n_x)]

        @pl.when(j == 0)
        def _():
            for load in loads + x_loads:
                load.start()
            for load in loads:
                load.wait()

        for k in range(n_x):

            @pl.when(j == k)
            def _(k=k):
                x_loads[k].wait()

        x = xs[j] if n_x else None
        part = body(x, held, in_refs, out_refs)
        stores = [pltpu.make_async_copy(kept.at[k % 2], part_refs[k], part_sems.at[k]) for k in range(n_part)]
        for k in range(n_part):

            @pl.when(j == k)
            def _(k=k):
                if k >= 2:
                    stores[k - 2].wait()
                kept[k % 2] = part
                stores[k].start()
                if k == n_part - 1:
                    for store in stores[max(k - 1, 0) :]:
                        store.wait()

    scratch = [pltpu.VMEM(shape, BF16) for shape in weights.shapes]
    scratch.append(pltpu.SemaphoreType.DMA((max(len(weights.takes), 1),)))
    if n_x:
        scratch += [pltpu.VMEM((n_x,) + blocks[0].shape, BF16), pltpu.SemaphoreType.DMA((n_x,))]
    if n_part:
        scratch += [pltpu.VMEM((2, rows, width), BF16), pltpu.SemaphoreType.DMA((n_part,))]
    out = pl.pallas_call(
        kernel,
        grid=(count,),
        out_shape=[shape for shape, _ in outs] + [jax.ShapeDtypeStruct((rows, width), BF16)] * n_part,
        in_specs=[SMEM_SPEC] + [any_spec] * (n_x + n_w) + [spec for _, spec in ins] + [any_spec] * n_onto,
        out_specs=[spec for _, spec in outs] + [any_spec] * n_part,
        input_output_aliases={1 + n_x + n_w + n_in + i: i for i in range(n_onto)},
        scratch_shapes=scratch,
        compiler_params=params(),
        cost_estimate=pl.CostEstimate(flops=cost // 1000, bytes_accessed=1024, transcendentals=0),
    )(order, *blocks, *weights.arrays, *[a for a, _ in ins], *onto)
    return list(out[:n_out]), list(out[n_out:])


def shape_of(*shape, dtype=F32):
    return jax.ShapeDtypeStruct(shape, dtype)


def by_block(rows, wide, first=0, column=0):
    return pl.BlockSpec((rows, wide), lambda b: (b + first, column))


def whole_row(wide):
    return pl.BlockSpec((1, wide), lambda b: (0, 0))


def by_slot(slots, wide, first=0):
    return pl.BlockSpec((1, slots, wide), lambda b: (b + first, 0, 0))


def columns(wide):
    return [slice(c, min(c + 256, wide)) for c in range(0, wide, 256)]


def mixer_in(order, blocks, weights, bound, slots, pos_n):
    count, (rows, depth), wide = len(blocks), blocks[0].shape, bound.shape[1]

    def body(x, held, ins, outs):
        pre_ref, all_ref, decay_ref, end_ref = outs
        low = ins[0][...]
        all_ref[...] = x
        pre_ref[...] = dot_nt(x, held[0][...])

        def one(i, carry):
            out = []
            for k in range(slots):
                at = pl.ds(pl.multiple_of(k * pos_n + i * 8, 8), 8)
                _, forget, act, _, keep = gates(pre_ref[at, :wide], pre_ref[at, wide : 2 * wide], low)
                decay, local = tile_scan(forget, act * keep)
                a, h = carry[k]
                out.append((a * decay[7:8, :], decay[7:8, :] * h + local[7:8, :]))
            return tuple(out)

        start = (jnp.ones((1, wide), F32), jnp.zeros((1, wide), F32))
        ends = lax.fori_loop(0, pos_n // 8, one, (start,) * slots)
        for k in range(slots):
            decay_ref[0, k : k + 1] = ends[k][0]
            end_ref[0, k : k + 1] = ends[k][1]

    outs = [
        (shape_of(count * rows, 3 * wide), by_block(rows, 3 * wide)),
        (shape_of(count * rows, depth, dtype=BF16), by_block(rows, depth)),
        (shape_of(count, slots, wide), by_slot(slots, wide)),
        (shape_of(count, slots, wide), by_slot(slots, wide)),
    ]
    return step_kernel(
        body, order, count, rows, blocks, weights, [(bound, whole_row(wide))], outs, 0, 6 * count * rows * wide * depth
    )[0]


def scan_heads(place, before, whole, reverse):
    count, slots, wide = whole[0].shape

    def body(place_ref, pa_ref, pb_ref, wa_ref, wb_ref, head_ref):
        state = jnp.zeros((slots, wide), F32)
        for i in range(count):
            j = lax.bitwise_xor(place_ref[0], count - 1 - i if reverse else i)
            head_ref[j] = pa_ref[j] * state + pb_ref[j]
            state = wa_ref[j] * state + wb_ref[j]

    return pl.pallas_call(
        body,
        out_shape=shape_of(count, slots, wide),
        in_specs=[SMEM_SPEC] + [VMEM_SPEC] * 4,
        out_specs=VMEM_SPEC,
        compiler_params=params(),
    )(place, *before, *whole)


def mixer_out(order, pre, bound, gain, head, weights, pos_n):
    wide = bound.shape[1]
    count, slots, _ = head.shape
    rows = slots * pos_n
    depth = weights.shapes[0][1]

    def body(x, held, ins, outs):
        pre_ref, bound_ref, gain_ref, head_ref = ins
        state_ref, mix_ref, sum_ref = outs
        low = bound_ref[...]

        def one(i, carry):
            out = []
            for k in range(slots):
                at = pl.ds(pl.multiple_of(k * pos_n + i * 8, 8), 8)
                _, forget, act, _, keep = gates(pre_ref[at, :wide], pre_ref[at, wide : 2 * wide], low)
                decay, local = tile_scan(forget, act * keep)
                state = local + decay * carry[k]
                state_ref[at, :] = state
                square = state * state
                sum_ref[at, :] = sum(square[:, c : c + 128] for c in range(0, wide, 128))
                out.append(state[7:8, :])
            return tuple(out)

        lax.fori_loop(0, pos_n // 8, one, tuple(head_ref[0, k : k + 1] for k in range(slots)))
        og = pre_ref[:, 2 * wide :]
        mix = (state_ref[...] * gain_ref[...] * (og * fast_sigmoid(og))).astype(BF16)
        mix_ref[...] = mix
        return dot_nn(mix, held[0][...]).astype(BF16)

    ins = [
        (pre, by_block(rows, 3 * wide)),
        (bound, whole_row(wide)),
        (gain, whole_row(wide)),
        (head, by_slot(slots, wide)),
    ]
    outs = [
        (shape_of(count * rows, wide), by_block(rows, wide)),
        (shape_of(count * rows, wide, dtype=BF16), by_block(rows, wide)),
        (shape_of(count * rows, 128), by_block(rows, 128)),
    ]
    return step_kernel(body, order, count, rows, [], weights, ins, outs, depth, 2 * count * rows * wide * depth)


def feed_forward(order, blocks, weights, first, count, onto=()):
    (rows, depth), wide = blocks[0].shape, weights.shapes[0][0]

    def body(x, held, ins, outs):
        hid_ref, slope_ref, act_ref, all_ref = outs
        all_ref[...] = x
        for at in columns(wide):
            gate = dot_nt(x, held[0][at, :])
            up = dot_nt(x, held[1][at, :])
            sig = fast_sigmoid(gate)
            act = gate * sig
            hid_ref[:, at] = (act * up).astype(BF16)
            slope_ref[:, at] = (up * (sig * (1.0 + gate * (1.0 - sig)))).astype(BF16)
            act_ref[:, at] = act.astype(BF16)

    outs = [(shape_of(count * rows, wide, dtype=BF16), by_block(rows, wide, first))] * 3
    outs = outs + [(shape_of(count * rows, depth, dtype=BF16), by_block(rows, depth, first))]
    cost = 4 * len(blocks) * rows * wide * depth
    return step_kernel(body, order, len(blocks), rows, blocks, weights, [], outs, 0, cost, onto)[0]


def down_parts(order, hidden, weights, rows):
    wide, depth = weights.shapes[0]
    count = hidden.shape[0] // rows

    def body(x, held, ins, outs):
        return dot_nn(ins[0][...], held[0][...]).astype(BF16)

    return step_kernel(
        body, order, count, rows, [], weights, [(hidden, by_block(rows, wide))], [], depth, 2 * count * rows * wide * depth
    )[1]


def back_hidden(order, g, weights, slope, act, rows):
    wide, depth = weights.shapes[0]
    count = g.shape[0] // rows

    def body(x, held, ins, outs):
        g_ref, slope_ref, act_ref = ins
        for at in columns(wide):
            hid = dot_nt(g_ref[...], held[0][at, :])
            outs[0][:, at] = (hid * slope_ref[:, at].astype(F32)).astype(BF16)
            outs[1][:, at] = (hid * act_ref[:, at].astype(F32)).astype(BF16)

    block = by_block(rows, wide)
    ins = [(g, by_block(rows, depth)), (slope, block), (act, block)]
    outs = [(shape_of(count * rows, wide, dtype=BF16), block)] * 2
    return step_kernel(body, order, count, rows, [], weights, ins, outs, 0, 2 * count * rows * wide * depth)[0]


def back_pair(order, a, b, weights, rows, first, count):
    wide, depth = weights.shapes[0]

    def body(x, held, ins, outs):
        return (dot_nn(ins[0][...], held[0][...]) + dot_nn(ins[1][...], held[1][...])).astype(BF16)

    block = by_block(rows, wide, first)
    return step_kernel(
        body, order, count, rows, [], weights, [(a, block), (b, block)], [], depth, 4 * count * rows * wide * depth
    )[1]


def back_mixer(order, blocks, weights, pre, state, mix, r_mix, gain):
    count, (rows, depth), wide = len(blocks), blocks[0].shape, gain.shape[1]

    def body(x, held, ins, outs):
        og_ref, state_ref, mix_ref, r_ref, gain_ref = ins
        norm_ref, og_out, mix_out, all_ref, inner_ref, sum_ref = outs
        all_ref[...] = x
        mix_out[...] = (mix_ref[...].astype(F32) * r_ref[...]).astype(BF16)
        g = dot_nt(x, held[0][...])
        og, state = og_ref[...], state_ref[...]
        sig = fast_sigmoid(og)
        act = og * sig
        g_state = g * (state * r_ref[...])
        sum_ref[0] = jnp.sum((g_state * act).reshape(rows // 8, 8, wide), 0)
        og_out[...] = (g_state * gain_ref[...] * (sig * (1.0 + og * (1.0 - sig)))).astype(BF16)
        norm = g * gain_ref[...] * act
        norm_ref[...] = norm
        inner = state * norm
        inner_ref[...] = sum(inner[:, c : c + 128] for c in range(0, wide, 128))

    ins = [
        (pre, pl.BlockSpec((rows, wide), lambda b: (b, 2))),
        (state, by_block(rows, wide)),
        (mix, by_block(rows, wide)),
        (r_mix, by_block(rows, 1)),
        (gain, whole_row(wide)),
    ]
    outs = [
        (shape_of(count * rows, wide), by_block(rows, wide)),
        (shape_of(count * rows, wide, dtype=BF16), by_block(rows, wide)),
        (shape_of(count * rows, wide, dtype=BF16), by_block(rows, wide)),
        (shape_of(count * rows, depth, dtype=BF16), by_block(rows, depth)),
        (shape_of(count * rows, 128), by_block(rows, 128)),
        (shape_of(count, 8, wide), by_slot(8, wide)),
    ]
    return step_kernel(body, order, count, rows, blocks, weights, ins, outs, 0, 2 * count * rows * wide * depth)[0]


def back_ends(pre, bound, norm, state, r_mix, coef, slots, pos_n):
    wide = norm.shape[1]
    rows = slots * pos_n
    count = norm.shape[0] // rows
    tiles = pos_n // 8

    def body(fg_ref, norm_ref, state_ref, r_ref, coef_ref, bound_ref, end_ref):
        low = bound_ref[...]

        def one(i, carry):
            out = []
            for k in range(slots):
                at = pl.ds(pl.multiple_of(k * pos_n + (tiles - 1 - i) * 8, 8), 8)
                local = r_ref[at, :] * norm_ref[at, :] - coef_ref[at, :] * state_ref[at, :]
                forget = low + (1.0 - low) * fast_sigmoid(fg_ref[at, :])
                decay, part = tile_scan_up(forget, forget * local)
                out.append(decay[0:1, :] * carry[k] + part[0:1, :])
            return tuple(out)

        ends = lax.fori_loop(0, tiles, one, (jnp.zeros((1, wide), F32),) * slots)
        for k in range(slots):
            end_ref[0, k : k + 1] = ends[k]

    block = by_block(rows, wide)
    return pl.pallas_call(
        body,
        grid=(count,),
        out_shape=shape_of(count, slots, wide),
        in_specs=[
            pl.BlockSpec((rows, wide), lambda b: (b, 1)),
            block,
            block,
            by_block(rows, 1),
            by_block(rows, 1),
            whole_row(wide),
        ],
        out_specs=by_slot(slots, wide),
        compiler_params=params(),
    )(pre, norm, state, r_mix, coef, bound)


def back_states(order, pre, bound, norm, state, g_og, r_mix, coef, head, tail, weights, pos_n, first, count):
    wide = norm.shape[1]
    slots = head.shape[1]
    rows = slots * pos_n
    pairs = pos_n // 16
    depth = weights.shapes[0][1]

    def body(x, held, ins, outs):
        in_ref, fg_ref, bound_ref, norm_ref, state_ref, og_ref, r_ref, coef_ref, head_ref, tail_ref = ins
        gin_ref, gfg_ref, low_ref = outs
        low = bound_ref[...]
        place = lax.broadcasted_iota(jnp.int32, (8, wide), 0)
        low_ref[0] = jnp.zeros((8, wide), F32)

        def half(k, tile, g):
            at = pl.ds(pl.multiple_of(k * pos_n + tile * 8, 8), 8)
            sig_f, forget, act, slope, keep = gates(in_ref[at, :], fg_ref[at, :], low)
            now = state_ref[at, :]
            local = r_ref[at, :] * norm_ref[at, :] - coef_ref[at, :] * now
            decay, part = tile_scan_up(forget, forget * local)
            whole = part + decay * g
            g_state = local + jnp.where(place == 7, g, pltpu.roll(whole, 7, 0))
            last = jnp.maximum(k * pos_n + tile * 8 - 1, 0)
            entry = jnp.where(tile == 0, head_ref[0, k : k + 1], state_ref[pl.ds(last, 1), :])
            before = jnp.where(place == 0, entry, pltpu.roll(now, 1, 0))
            g_forget = g_state * (before - act)
            return g_state * keep * slope, g_forget * keep * sig_f, whole[0:1, :], g_forget * (1.0 - sig_f)

        def one(i, carry):
            pair = pairs - 1 - i
            out, total = [], low_ref[0]
            for k in range(slots):
                in_2, fg_2, g, low_2 = half(k, 2 * pair + 1, carry[k])
                in_1, fg_1, g, low_1 = half(k, 2 * pair, g)
                at = pl.ds(pl.multiple_of(k * pos_n + pair * 16, 16), 16)
                gin_ref[at, :] = jnp.concatenate([in_1, in_2], 0).astype(BF16)
                gfg_ref[at, :] = jnp.concatenate([fg_1, fg_2], 0).astype(BF16)
                total = total + low_1 + low_2
                out.append(g)
            low_ref[0] = total
            return tuple(out)

        lax.fori_loop(0, pairs, one, tuple(tail_ref[0, k : k + 1] for k in range(slots)))
        part = dot_nn(gin_ref[...], held[0][:wide]) + dot_nn(gfg_ref[...], held[0][wide : 2 * wide])
        return (part + dot_nn(og_ref[...], held[0][2 * wide :])).astype(BF16)

    block, edge, one_lane = by_block(rows, wide, first), by_slot(slots, wide, first), by_block(rows, 1, first)
    ins = [
        (pre, block),
        (pre, by_block(rows, wide, first, 1)),
        (bound, whole_row(wide)),
        (norm, block),
        (state, block),
        (g_og, block),
        (r_mix, one_lane),
        (coef, one_lane),
        (head, edge),
        (tail, edge),
    ]
    outs = [(shape_of(count * rows, wide, dtype=BF16), by_block(rows, wide))] * 2
    outs = outs + [(shape_of(count, 8, wide), by_slot(8, wide))]
    return step_kernel(body, order, count, rows, [], weights, ins, outs, depth, 6 * count * rows * wide * depth)


def order_rows(blocks, place):
    count = len(blocks)
    q, width = blocks[0].shape
    tile = 512

    def body(place_ref, *refs):
        out_ref = refs[count]
        for j in range(count):
            at = pl.multiple_of(lax.bitwise_xor(place_ref[0], j) * q, 16)
            out_ref[pl.ds(at, q), :] = refs[j][...].astype(F32)

    return pl.pallas_call(
        body,
        grid=(width // tile,),
        out_shape=shape_of(count * q, width),
        in_specs=[SMEM_SPEC] + [pl.BlockSpec((q, tile), lambda i: (0, i))] * count,
        out_specs=pl.BlockSpec((count * q, tile), lambda i: (0, i)),
        compiler_params=params(),
    )(place, *blocks)


def turn_rows(blocks, place):
    count = len(blocks)
    q, width = blocks[0].shape
    tile = 256

    def body(place_ref, *refs):
        out_ref, held = refs[count], refs[count + 1]
        for j in range(count):
            held[lax.bitwise_xor(place_ref[0], j)] = refs[j][...].astype(F32)
        out_ref[...] = held[...].reshape(count * q, tile).T

    return pl.pallas_call(
        body,
        grid=(width // tile,),
        out_shape=shape_of(width, count * q),
        in_specs=[SMEM_SPEC] + [pl.BlockSpec((q, tile), lambda i: (0, i))] * count,
        out_specs=pl.BlockSpec((tile, count * q), lambda i: (i, 0)),
        scratch_shapes=[pltpu.VMEM((count, q, tile), F32)],
        compiler_params=params(),
    )(place, *blocks)


def dot_nt(a, b):
    return lax.dot_general(a, b, (((1,), (1,)), ((), ())), preferred_element_type=F32)


def dot_nn(a, b):
    return lax.dot_general(a, b, (((1,), (0,)), ((), ())), preferred_element_type=F32)


def dot_tn(a, b):
    return lax.dot_general(a, b, (((0,), (0,)), ((), ())), preferred_element_type=F32)


def on_device(
    net,
    tokens,
    cotangent,
    lengths,
    in_gain,
    w_input,
    w_forget,
    w_output_gate,
    lower_bound,
    mix_gain,
    w_out,
    mlp_gain,
    w_gate,
    w_up,
    w_down,
):
    s, t = net.places()
    n_seq, n_tp = net.seq, net.tp
    slots, group, cols = tokens.shape
    width = cols * n_tp
    pos_n = group // n_tp
    rows = slots * pos_n
    dq = cols // n_seq
    fq = w_down.shape[0] // n_seq
    chan, hid = dq * n_tp, fq * n_tp
    place = s.reshape(1)
    order = net.order

    def quarter_t(w, q):
        return lax.dynamic_slice_in_dim(w, s * q, q, 1).T

    def by_owner(x):
        return x.reshape(slots, n_tp, pos_n, cols).transpose(1, 0, 2, 3).reshape(n_tp, rows, cols)

    def to_owner(x):
        return lax.all_to_all(x, "tp", 0, 0, tiled=True)

    def in_place(x):
        return x.reshape(n_tp, slots, pos_n, cols).transpose(1, 0, 2, 3).reshape(tokens.shape)

    def total(terms):
        return sum(p.astype(F32) for p in terms)

    where = s * group + t * pos_n + jnp.arange(pos_n, dtype=jnp.int32)
    live = (where[None, :] < lengths[:, None]).astype(F32).reshape(rows, 1)

    small = jnp.concatenate(
        [lax.dynamic_slice_in_dim(v, s * dq, dq) for v in (lower_bound, mix_gain)] + [mlp_gain], 0
    )
    terms, rest = [], small
    for _ in range(3):
        terms.append(hold(rest.astype(BF16))[0])
        rest = rest - terms[-1].astype(F32)
    terms = jnp.pad(jnp.concatenate(terms, 0), (0, 16 * cols - 3 * small.shape[0])).reshape(1, 16, cols)
    token_blocks = to_owner(jnp.concatenate([by_owner(tokens), jnp.broadcast_to(terms, (n_tp, 16, cols))], 1))
    small = token_blocks[:, rows:].reshape(n_tp, 16 * cols)[:, : 3 * small.shape[0]].astype(F32).reshape(n_tp, 3, -1)
    small = small[:, 0] + small[:, 1] + small[:, 2]
    bound = small[:, :dq].reshape(1, chan)
    gain = small[:, dq : 2 * dq].reshape(1, chan)
    mlp_full = small[:, 2 * dq :].reshape(1, width)
    mix_w = jnp.concatenate(
        [quarter_t(w, dq) for w in (w_input, w_forget, w_output_gate)]
        + [lax.dynamic_slice_in_dim(w_out, s * dq, dq, 0)],
        0,
    )
    tok, normed_own = norm_tokens(token_blocks, in_gain, rows)
    mix_ring = RingGather(net, after(mix_w, normed_own))
    mix_ring.launch(mix_ring.sends())
    normed = net.gather_rest(net.gather_first(normed_own))
    mix_ring.finish()
    w3, wo = Weights(), Weights()
    w3.add(mix_ring, [(i * dq, i * chan) for i in range(3)], dq, True)
    wo.add(mix_ring, [(3 * dq, 0)], dq, True)
    gate_w = jnp.concatenate([quarter_t(w_gate, fq), quarter_t(w_up, fq)], 0)
    gate_ring = RingGather(net, after(gate_w, *mix_ring.came))
    gate_ring.launch(gate_ring.sends())

    pre, normed_all, decay, end = mixer_in(order, normed, w3, bound, slots, pos_n)

    def spread(pair, reverse):
        def joined(earlier, later):
            return earlier[0] * later[0], later[0] * earlier[1] + later[1]

        whole = pair
        before = (jnp.ones_like(pair[0]), jnp.zeros_like(pair[1]))
        for bit in net.tp_bits:
            moved = net.cross(jnp.stack(whole, 0), bit)
            moved = (moved[0], moved[1])
            upper = (jnp.bitwise_and(t, bit) != 0) != reverse
            ahead, behind = joined(moved, whole), joined(whole, moved)
            longer = joined(moved, before)
            before = tuple(jnp.where(upper, a, b) for a, b in zip(longer, before))
            whole = tuple(jnp.where(upper, a, b) for a, b in zip(ahead, behind))
        return before, whole

    (decay, end), gate_ring.came = hold((decay, end), gate_ring.came)
    head = scan_heads(place, *spread((decay, end), False), False)
    head, sends, cot_sent = hold(head, gate_ring.sends(), by_owner(cotangent))
    gate_ring.launch(sends)
    cot_blocks = to_owner(cot_sent)
    (state, mix, squares), parts = mixer_out(order, pre, bound, gain, head, wo, pos_n)
    parts, sum_all = hold(parts, jnp.sum(squares, -1).reshape(n_seq, rows))
    sum_all = net.total_near(sum_all)
    near, sum_all = hold(net.quad_near(parts), sum_all)
    branch, sum_all = net.quad_far(near), net.total_far(sum_all)
    branch, sum_all, gate_ring.came = hold(branch, sum_all, gate_ring.came)
    gate_ring.launch(gate_ring.sends())
    r_mix = lax.rsqrt(sum_all / width + EPS).reshape(n_seq * rows, 1)
    branch = total(branch)
    resid = tok.astype(F32) + r_mix[:rows] * branch
    r_mlp = lax.rsqrt(jnp.mean(resid * resid, axis=-1, keepdims=True) + EPS)
    scaled = resid * r_mlp
    mlp_own = (scaled * mlp_full).astype(BF16)
    mlp_in = net.gather_first(mlp_own)
    cot = mask_rows(after(cot_blocks, mlp_own), live)
    half = n_seq // 2
    mlp_in, gate_ring.came, cot = hold(mlp_in, gate_ring.came, cot)
    gate_ring.launch(gate_ring.sends())
    gate_ring.finish()
    mlp_in = net.gather_rest(mlp_in)
    grad_out = net.gather_first(cot)
    wgu = Weights()
    wgu.add(gate_ring, [(0, 0)], fq, False)
    wgu.add(gate_ring, [(fq, 0)], fq, False)
    down_w = lax.dynamic_slice_in_dim(w_down, s * fq, fq, 0)
    mlp_in, down_w, _ = hold(mlp_in, down_w, gate_ring.came)

    down_ring = RingGather(net, down_w)
    down_ring.launch(down_ring.sends())
    some = feed_forward(order, mlp_in[:half], wgu, 0, n_seq)
    some, down_ring.came, far_in = hold(some, down_ring.came, mlp_in[half:])
    down_ring.launch(down_ring.sends())
    hidden, slope_up, act, mlp_all = feed_forward(order, far_in, wgu, half, n_seq, some)
    hidden, down_ring.came, grad_out = hold(hidden, down_ring.came, grad_out)
    down_ring.launch(down_ring.sends())
    grad_out = net.gather_rest(grad_out)
    grad_out, hidden, sends = hold(grad_out, hidden, down_ring.sends())
    down_ring.launch(sends)
    down_ring.finish()
    grad_all = jnp.concatenate(grad_out, 0)

    def ring_sum(wholes, canonical, *others):
        def chunk(d):
            out = []
            for w in wholes:
                q = w.shape[0] // n_tp
                if canonical:
                    out.append(lax.dynamic_slice_in_dim(w, net.behind[d] * q, q, 0))
                else:
                    out.append(w[d * q : (d + 1) * q])
            return jnp.concatenate(out, 0) if len(out) > 1 else out[0]

        return RingScatter(net, chunk)

    def to_output(blocks, turned):
        q = blocks[0].shape[0]
        if q % 16 == 0:
            return turn_rows(blocks, place) if turned else order_rows(blocks, place)
        out = jnp.zeros((n_seq, q, width), F32)
        for j in range(n_seq):
            out = lax.dynamic_update_index_in_dim(out, blocks[j].astype(F32), lax.bitwise_xor(s, j), 0)
        out = out.reshape(n_seq * q, width)
        return out.T if turned else out

    dw_down = dot_tn(hidden, grad_all).astype(BF16)
    down_sum = ring_sum([dw_down], False)
    wd = Weights()
    wd.add(down_ring, [(0, 0)], fq, False)
    sends, grad_all, _ = hold(down_sum.sends(), grad_all, down_ring.came)
    down_sum.launch(sends)
    grad_gate, grad_up = back_hidden(order, grad_all, wd, slope_up, act, rows)
    grad_gate, down_sum.came = hold(grad_gate, down_sum.came)
    sends, grad_gate = hold(down_sum.sends(), grad_gate)
    down_sum.launch(sends)
    dw_gate = dot_tn(grad_gate, mlp_all).astype(BF16)
    dw_gate, down_sum.came = hold(dw_gate, down_sum.came)
    sends, grad_up = hold(down_sum.sends(), grad_up)
    down_sum.launch(sends)
    dw_up = dot_tn(grad_up, mlp_all).astype(BF16)
    dw_up, down_sum.came = hold(dw_up, down_sum.came)
    sends, grad_gate = hold(down_sum.sends(), grad_gate)
    down_sum.launch(sends)
    far = back_pair(order, grad_gate, grad_up, wgu, rows, half, half)
    far, down_sum.came = hold(far, down_sum.came)
    near_far = net.quad_far_part(far)
    down_own = down_sum.result()
    gu_sum = ring_sum([dw_gate, dw_up], False)
    near_far, down_own, grad_gate, sends = hold(near_far, down_own, grad_gate, gu_sum.sends())
    gu_sum.launch(sends)
    moved_far = net.swap(near_far, net.bits[-1])
    parts = back_pair(order, grad_gate, grad_up, wgu, rows, 0, half)
    parts, gu_sum.came = hold(parts, gu_sum.came)
    near_own = net.quad_far_part(parts)
    sends, near_own, hidden = hold(gu_sum.sends(), near_own, hidden)
    gu_sum.launch(sends)
    ffn_parts = down_parts(order, hidden, wd, rows)
    moved_far, near_own, ffn_parts = hold(moved_far, near_own, ffn_parts)
    grad_mlp_in = total([near_own, moved_far])

    grad_mlp_gain = jnp.sum(grad_mlp_in * scaled, axis=0)
    grad_scaled = grad_mlp_in * mlp_full
    inner = jnp.sum(resid * grad_scaled, axis=-1, keepdims=True)
    grad_resid = cot.astype(F32) + r_mlp * grad_scaled - resid * r_mlp**3 * inner / width
    branch_own = grad_resid.astype(BF16)
    grad_branch = net.gather_first(branch_own)
    branch_own, gu_sum.came = hold(branch_own, gu_sum.came)
    sends = hold(gu_sum.sends())[0]
    gu_sum.launch(sends)
    down_blocks = net.gather_first(after(down_own, *sends))

    grad_branch, gu_sum.came, down_blocks = hold(grad_branch, gu_sum.came, down_blocks)
    grad_branch, down_blocks = net.gather_rest(grad_branch), net.gather_rest(down_blocks)
    sends, grad_branch = hold(gu_sum.sends(), grad_branch)
    gu_sum.launch(sends)
    g_norm, grad_og, mixed_out, branch_all, inner_lanes, gain_sums = back_mixer(
        order, grad_branch, wo, pre, state, mix, r_mix, gain
    )
    inner = net.total_far(net.total_near(jnp.sum(inner_lanes, -1).reshape(n_seq, rows))).reshape(-1, 1)
    ffn = net.quad_far(net.quad_near([after(p, inner) for p in ffn_parts]))
    coef = r_mix**3 * inner / width
    back_end = back_ends(pre, bound, g_norm, state, r_mix, coef, slots, pos_n)
    dw_out = dot_tn(after(mixed_out, back_end), branch_all).astype(BF16)
    dw_og = dot_tn(after(grad_og, dw_out), normed_all).astype(BF16)
    back_end, gu_sum.came, dw_og = hold(back_end, gu_sum.came, dw_og)
    tail = scan_heads(place, *spread((decay, back_end), True), True)
    gu_own = gu_sum.result()
    mixed = (live * (resid + total(ffn))).astype(BF16)
    mixed_sent = mixed.reshape(rows, n_tp, cols).transpose(1, 0, 2)
    first_sum = ring_sum([dw_out, dw_og], True)
    tail, gu_own, mixed_sent, sends = hold(tail, gu_own, mixed_sent, first_sum.sends())
    first_sum.launch(sends)
    mixed_got = to_owner(mixed_sent)

    def back(start, tail):
        return back_states(
            order, pre, bound, g_norm, state, grad_og, r_mix, coef, head, tail, w3, pos_n, start, half
        )

    (far_in, far_fg, far_low), far = back(half, tail)
    far, far_in, first_sum.came = hold(far, far_in, first_sum.came)
    near_far = net.quad_far_part(far)
    near_far, sends, tail = hold(near_far, first_sum.sends(), tail)
    moved_far = net.swap(near_far, net.bits[-1])
    first_sum.launch(sends)
    (grad_in, grad_fg, low_sums), parts = back(0, tail)
    near_own = net.quad_far_part(parts)
    low_sums = low_sums + far_low
    grad_in, grad_fg = (jnp.concatenate([a, b], 0) for a, b in ((grad_in, far_in), (grad_fg, far_fg)))
    near_own, first_sum.came, grad_in = hold(near_own, first_sum.came, grad_in)
    sends, grad_in = hold(first_sum.sends(), grad_in)
    first_sum.launch(sends)
    dw_in = dot_tn(grad_in, normed_all).astype(BF16)
    dw_fg = dot_tn(after(grad_fg, dw_in), normed_all).astype(BF16)
    last_sum = ring_sum([dw_in, dw_fg], True)
    dw_fg, first_sum.came, last_sends, moved_far = hold(dw_fg, first_sum.came, last_sum.sends(), moved_far)
    first_sum.launch(first_sum.sends())
    last_sum.launch(last_sends)
    moved = [near_own, moved_far]
    gu_blocks = net.gather_first(after(gu_own, moved_far))
    grad_w_down = to_output(down_blocks, False)

    grad_normed = total(moved)
    x = tok.astype(F32)
    r_in = lax.rsqrt(jnp.mean(x * x, axis=-1, keepdims=True) + EPS)
    grad_in_gain = jnp.sum(grad_normed * x * r_in, axis=0)
    scaled_g = grad_normed * in_gain
    inner = jnp.sum(x * scaled_g, axis=-1, keepdims=True)
    grad_tok = grad_resid + r_in * scaled_g - x * r_in**3 * inner / width

    gains = jnp.stack([grad_in_gain, grad_mlp_gain], 0)
    high = hold(gains.astype(BF16))[0]
    low = (gains - high.astype(F32)).astype(BF16)
    extra = jnp.concatenate([high, low, jnp.zeros((12, width), BF16)], 0)
    sent = jnp.concatenate([grad_tok.astype(BF16), extra], 0).reshape(-1, n_tp, cols).transpose(1, 0, 2)
    sent, first_sum.came, last_sum.came = hold(sent, first_sum.came, last_sum.came)
    got = to_owner(sent)
    first_own = first_sum.result()
    last_own = last_sum.result()
    first_blocks = net.gather_rest(net.gather_first(first_own))
    gu_blocks = net.gather_rest(gu_blocks)
    last_blocks = net.gather_rest(net.gather_first(last_own))
    grad_w_gate = to_output([b[:fq] for b in gu_blocks], False).T
    grad_w_up = to_output([b[fq:] for b in gu_blocks], False).T
    grad_w_out = to_output([b[:dq] for b in first_blocks], False)
    grad_w_og = to_output([b[dq:] for b in first_blocks], True)
    grad_w_in = to_output([b[:dq] for b in last_blocks], True)
    grad_w_fg = to_output([b[dq:] for b in last_blocks], True)
    mine = jnp.sum(got[:, rows : rows + 4].astype(F32), 0)
    mine = mine[:2] + mine[2:]
    sums = jnp.stack([jnp.sum(low_sums, axis=(0, 1)), jnp.sum(gain_sums, axis=(0, 1))], 0).reshape(2, n_tp, dq)
    for bit in reversed(net.tp_bits):
        sums = sums.reshape(2, 2, bit, dq)
        upper = jnp.bitwise_and(t, bit) != 0
        keep = jnp.where(upper, sums[:, 1], sums[:, 0])
        send = jnp.where(upper, sums[:, 0], sums[:, 1])
        sums = keep + net.cross(send, bit)
    chans = sums.reshape(1, 2, dq)
    for bit in net.bits:
        chans = jnp.concatenate([chans, net.swap(chans, bit)], 0)
        mine = mine + net.swap(mine, bit)
    chans = chans[lax.bitwise_xor(s, jnp.arange(n_seq, dtype=jnp.int32))]
    return (
        in_place(mixed_got),
        in_place(got[:, :rows]).astype(F32),
        mine[0],
        grad_w_in,
        grad_w_fg,
        grad_w_og,
        chans[:, 0].reshape(-1),
        chans[:, 1].reshape(-1),
        grad_w_out,
        mine[1],
        grad_w_gate,
        grad_w_up,
        grad_w_down,
    )


def solution(mesh):
    return jax.shard_map(
        functools.partial(on_device, Net(mesh)),
        mesh=mesh,
        in_specs=(
            P(None, "seq", "tp"),
            P(None, "seq", "tp"),
            P(),
            P(),
            P(None, "tp"),
            P(None, "tp"),
            P(None, "tp"),
            P("tp"),
            P("tp"),
            P("tp", None),
            P("tp"),
            P(None, "tp"),
            P(None, "tp"),
            P("tp", None),
        ),
        out_specs=(
            P(None, "seq", "tp"),
            P(None, "seq", "tp"),
            P("tp"),
            P(None, "tp"),
            P(None, "tp"),
            P(None, "tp"),
            P("tp"),
            P("tp"),
            P("tp", None),
            P("tp"),
            P(None, "tp"),
            P(None, "tp"),
            P("tp", None),
        ),
        check_vma=False,
    )
```

time: 2730 us -> 1020 us (0.37)
  waiting for transfers between devices: 1510 us -> 395 us
  local copies, waits for them, and re-layouts: 548 us -> 81.9 us
  Pallas kernels: 0 us -> 252 us
  matrix products: 263 us -> 60.8 us
  blocking collectives: 200 us -> 0 us
  starting transfers between devices: 0.77 us -> 130 us
  other arithmetic: 171 us -> 84.3 us
    reduce_scatter x4 -> x0, waiting for transfers between devices: 816 us -> none  [the longest x1 210 us: on_device(): lax.psum_scatter(in_term.astype(jnp.bfloat16), 'tp', scatter_dimension=2,...]
    all_gather x4 -> x0, waiting for transfers between devices: 566 us -> none  [the longest x1 181 us: on_device(): full_tokens = lax.all_gather(tokens, 'tp', axis=2, tiled=True)]
    ppermute x0 -> x109, waiting for transfers between devices: none -> 352 us  [the longest x56 185 us: shift(): lax.ppermute(x, 'tp', [(self.cycle[i], self.cycle[(i + k) % n]) for i in...]
    slice x142 -> x33, local copies, waits for them, and re-layouts: 326 us -> 27 us  [the longest x4 9.12 us: on_device(): grad_w_up = to_output([b[fq:] for b in gu_blocks], False).T]
    pallas_call x0 -> x23, Pallas kernels: none -> 252 us  [the longest x11 198 us: step_kernel(): pl.pallas_call(kernel, grid=(count,), out_shape=[shape for shape, _ in ou...]
    dot_general x21 -> x7, matrix products: 263 us -> 60.8 us  [dot_tn(): lax.dot_general(a, b, (((0,), (0,)), ((), ())), preferred_element_type=F32)]
    pad x72 -> x0, local copies, waits for them, and re-layouts: 154 us -> none  [linear_scan(): return lax.associative_scan(combine_pair, (decay, drive), axis=1)]
    psum x5 -> x0, blocking collectives: 146 us -> none  [the longest x4 139 us: row_total(): return lax.psum(values, 'tp')]
  transfers between devices with their start and end apart: 9 -> 113, of which waited for: 9 -> 46; matrix products, arithmetic and copies ran while one was open for 8% -> 19% of each run, Pallas kernels for 0% -> 21%
where the time goes in v2:
time: 1020 us; the launch traced here: 1010 us
  waiting for transfers between devices  395 us (39%)
  Pallas kernels  252 us (25%)
  starting transfers between devices  130 us (13%)
  other arithmetic  84.3 us (8%)
  local copies, waits for them, and re-layouts  81.9 us (8%)
  matrix products  60.8 us (6%)
    pallas_call x11, Pallas kernels, step_kernel(): pl.pallas_call(kernel, grid=(count,), out_shape=[shape for shape, _ in ou...  198 us
    ppermute x56, waiting for transfers between devices, shift(): lax.ppermute(x, 'tp', [(self.cycle[i], self.cycle[(i + k) % n]) for i in...  185 us
    ppermute x44, waiting for transfers between devices, swap(): return lax.ppermute(x, 'seq', [(i, i ^ bit) for i in range(self.seq)])  142 us
    ppermute x56, starting transfers between devices, shift(): lax.ppermute(x, 'tp', [(self.cycle[i], self.cycle[(i + k) % n]) for i in...  75.9 us
    dot_general x7, matrix products, dot_tn(): lax.dot_general(a, b, (((0,), (0,)), ((), ())), preferred_element_type=F32)  60.8 us
    all_to_all x4, waiting for transfers between devices, to_owner(): return lax.all_to_all(x, 'tp', 0, 0, tiled=True)  43.2 us
    convert_element_type x25, other arithmetic, plus(): (own.astype(F32) + jnp.pad(part.astype(F32), ((start, rest), (0, 0)))).as...  33.5 us
    unnamed x230, local copies, waits for them, and re-layouts  27.8 us
  transfers between devices with their start and end apart: 113, of which 46 were waited for; matrix products, arithmetic and copies ran while one was open for 19% of the time, Pallas kernels for 21%

profile of v2, /device:TPU:0, one launch (start us, length us, event | category | flops | bytes accessed | tf_op | source)
XLA Modules:
  0.0 1012.0 jit_solution(14321802925803554222)
XLA Ops:
  25.2 28.0 %all-to-all-done.in_ref = bf16[8,400,256]{2,1,0:T(8,128)(2,1)} async-done(((bf16[8,400,256]{2,1,0:T(8,128)(2,1)}), bf16[8,400,256]{2,1,0:T(8,128)(2,1)}, u32[]{:S(2)}, u32[]{:S(2)}) %all-to-all-start) | async-done | bytes 1638432 | tf_op jit(solution)/shard_map/all_to_all | solution.py:824
  59.1 21.9 %collective-permute-done.7.refs_12_.refs_8_ = bf16[256,2048]{1,0:T(8,128)(2,1)S(1)} collective-permute-done((bf16[256,2048]{1,0:T(8,128)(2,1)}, bf16[256,2048]{1,0:T(8,128)(2,1)S(1)}, u32[]{:S(2)}, u32[]{:S(2)}) %collective-permute-start.7) | collective-permute-done | bytes 1048608 | tf_op jit(solution)/shard_map/ppermute | solution.py:68
  84.6 19.6 %collective-permute-done.8.refs_11_.refs_7_ = bf16[256,2048]{1,0:T(8,128)(2,1)S(1)} collective-permute-done((bf16[256,2048]{1,0:T(8,128)(2,1)S(1)}, bf16[256,2048]{1,0:T(8,128)(2,1)S(1)}, u32[]{:S(2)}, u32[]{:S(2)}) %collective-permute-start.8) | collective-permute-done | bytes 1048608 | tf_op jit(solution)/shard_map/ppermute | solution.py:68
  106.8 22.2 %collective-permute-done.9.refs_10_.refs_6_ = bf16[256,2048]{1,0:T(8,128)(2,1)S(1)} collective-permute-done((bf16[256,2048]{1,0:T(8,128)(2,1)S(1)}, bf16[256,2048]{1,0:T(8,128)(2,1)S(1)}, u32[]{:S(2)}, u32[]{:S(2)}) %collective-permute-start.9) | collective-permute-done | bytes 1048608 | tf_op jit(solution)/shard_map/ppermute | solution.py:68
  150.0 24.1 %shard_map.247 = (f32[1536,1536]{1,0:T(8,128)}, bf16[1536,2048]{1,0:T(8,128)(2,1)}, f32[4,3,512]{2,1,0:T(4,128)}, f32[4,3,512]{2,1,0:T(4,128)}) custom-call(s32[8]{0:T(128)} %get-tuple-element.561.order_ref, bf16[384,2048]{1,0:T(8,128)(2,1)} %get-tuple-element.222.refs_0_, bf16[384,2048]{1,0:T(8,128)(2,1)} %collective-permute-done.refs_1_, ...), custom_call_target="tpu_custom_call" | custom-call | flops 9663676 | bytes 1024 | tf_op jit(solution)/shard_map/pallas_call | solution.py:395
  196.9 17.4 %shard_map.249 = (f32[1536,512]{1,0:T(8,128)}, bf16[1536,512]{1,0:T(8,128)(2,1)}, f32[1536,128]{1,0:T(8,128)}, bf16[384,2048]{1,0:T(8,128)(2,1)}, bf16[384,2048]...) custom-call(s32[8]{0:T(128)} %get-tuple-element.561.order_ref, ...), custom_call_target="tpu_custom_call" | custom-call | flops 3221225 | bytes 1024 | tf_op jit(solution)/shard_map/pallas_call | solution.py:395
  233.0 28.2 %collective-permute-done.20 = f32[4,384]{1,0:T(4,128)S(1)} collective-permute-done((f32[4,384]{1,0:T(4,128)S(1)}, f32[4,384]{1,0:T(4,128)S(1)}, u32[]{:S(2)}, u32[]{:S(2)}) %collective-permute-start.20) | collective-permute-done | bytes 6176 | tf_op jit(solution)/shard_map/ppermute | solution.py:74
  279.9 15.2 %all-to-all-done.1.in_ref = bf16[8,384,256]{2,1,0:T(8,128)(2,1)} async-done(((bf16[8,384,256]{2,1,0:T(8,128)(2,1)}), bf16[8,384,256]{2,1,0:T(8,128)(2,1)}, u32[]{:S(2)}, u32[]{:S(2)}) %all-to-all-start.1) | async-done | bytes 1572896 | tf_op jit(solution)/shard_map/all_to_all | solution.py:824
  298.2 15.7 %collective-permute-done.25.refs_5_.refs_3_ = bf16[352,2048]{1,0:T(8,128)(2,1)} collective-permute-done((bf16[352,2048]{1,0:T(8,128)(2,1)}, bf16[352,2048]{1,0:T(8,128)(2,1)}, u32[]{:S(2)}, u32[]{:S(2)}) %collective-permute-start.25) | collective-permute-done | bytes 1441824 | tf_op jit(solution)/shard_map/ppermute | solution.py:68
  349.0 19.1 %shard_map.251 = (bf16[1536,1408]{1,0:T(8,128)(2,1)}, bf16[1536,1408]{1,0:T(8,128)(2,1)}, bf16[1536,1408]{1,0:T(8,128)(2,1)}, bf16[1536,2048]{1,0:T(8,128)(2,1)}) custom-call(s32[8]{0:T(128)} %get-tuple-element.561.order_ref, bf16[384,2048]{1,0:T(8,128)(2,1)} %multiply_convert_fusion.1.refs_0_, bf16[384,2048]{1,0:T(8,128)(2,1)} %collective-permute-done.23.refs_1_, ...), custom_call_target="tpu_custom_call" | custom-call | flops 8858370 | bytes 1024 | tf_op jit(solution)/shard_map/pallas_call | solution.py:395
  370.6 19.2 %shard_map.252 = (bf16[1536,1408]{1,0:T(8,128)(2,1)}, bf16[1536,1408]{1,0:T(8,128)(2,1)}, bf16[1536,1408]{1,0:T(8,128)(2,1)}, bf16[1536,2048]{1,0:T(8,128)(2,1)}) custom-call(s32[8]{0:T(128)} %get-tuple-element.561.order_ref, ...), custom_call_target="tpu_custom_call", output_to_operand_aliasing={{0}: (12, {}), {1}: (13, {}), {2}: (14, {}), {3}: (15, {})} | custom-call | flops 8858370 | bytes 1024 | tf_op jit(solution)/shard_map/pallas_call | solution.py:395
  392.1 16.5 %collective-permute-done.38.refs_6_ = bf16[176,2048]{1,0:T(8,128)(2,1)S(1)} collective-permute-done((bf16[176,2048]{1,0:T(8,128)(2,1)S(1)}, bf16[176,2048]{1,0:T(8,128)(2,1)S(1)}, u32[]{:S(2)}, u32[]{:S(2)}) %collective-permute-start.38) | collective-permute-done | bytes 720928 | tf_op jit(solution)/shard_map/ppermute | solution.py:68
  429.0 17.5 %shard_map.253 = (bf16[1536,1408]{1,0:T(8,128)(2,1)}, bf16[1536,1408]{1,0:T(8,128)(2,1)}) custom-call(s32[8]{0:T(128)} %get-tuple-element.561.order_ref, bf16[176,2048]{1,0:T(8,128)(2,1)} %copy-done.19, bf16[176,2048]{1,0:T(8,128)(2,1)} %copy-done.26, bf16[176,2048]{1,0:T(8,128)(2,1)} %copy-done.28, bf16[176,2048]{1,0:T(8,128)(2,1)} %copy-done.25, ...), custom_call_target="tpu_custom_call" | custom-call | flops 8858370 | bytes 1024 | tf_op jit(solution)/shard_map/pallas_call | solution.py:395
  450.4 14.3 %convolution_convert_fusion.1 = bf16[1408,2048]{1,0:T(8,128)(2,1)} fusion(bf16[1536,1408]{1,0:T(8,128)(2,1)} %get-tuple-element.326.refs_9_, bf16[1536,2048]{1,0:T(8,128)(2,1)} %get-tuple-element.303), kind=kOutput, calls=%fused_computation.2 | convolution fusion | flops 8861253632 | bytes 16384000 | tf_op jit(solution)/shard_map/dot_general | solution.py:785
  485.5 17.7 %shard_map.254 = (bf16[384,2048]{1,0:T(8,128)(2,1)}, bf16[384,2048]{1,0:T(8,128)(2,1)}) custom-call(s32[8]{0:T(128)} %get-tuple-element.561.order_ref, bf16[352,2048]{1,0:T(8,128)(2,1)} %pad_maximum_fusion.3.refs_2_.refs_0_, bf16[352,2048]{1,0:T(8,128)(2,1)} %collective-permute-done.11.refs_3_.refs_1_, ...), custom_call_target="tpu_custom_call" | custom-call | flops 8858370 | bytes 1024 | tf_op jit(solution)/shard_map/pallas_call | solution.py:395
  515.6 17.7 %shard_map.255 = (bf16[384,2048]{1,0:T(8,128)(2,1)}, bf16[384,2048]{1,0:T(8,128)(2,1)}) custom-call(s32[8]{0:T(128)} %get-tuple-element.561.order_ref, bf16[352,2048]{1,0:T(8,128)(2,1)} %pad_maximum_fusion.3.refs_2_.refs_0_, bf16[352,2048]{1,0:T(8,128)(2,1)} %collective-permute-done.11.refs_3_.refs_1_, ...), custom_call_target="tpu_custom_call" | custom-call | flops 8858370 | bytes 1024 | tf_op jit(solution)/shard_map/pallas_call | solution.py:395
  540.1 16.6 %shard_map.256 = (bf16[384,2048]{1,0:T(8,128)(2,1)}, bf16[384,2048]{1,0:T(8,128)(2,1)}, bf16[384,2048]{1,0:T(8,128)(2,1)}, bf16[384,2048]{1,0:T(8,128)(2,1)}) custom-call(s32[8]{0:T(128)} %get-tuple-element.561.order_ref, bf16[176,2048]{1,0:T(8,128)(2,1)} %copy-done.19, bf16[176,2048]{1,0:T(8,128)(2,1)} %copy-done.26, bf16[176,2048]{1,0:T(8,128)(2,1)} %copy-done.28, ...), custom_call_target="tpu_custom_call" | custom-call | flops 8858370 | bytes 1024 | tf_op jit(solution)/shard_map/pallas_call | solution.py:395
  582.8 29.1 %collective-permute-done.55.refs_2_ = bf16[384,2048]{1,0:T(8,128)(2,1)} collective-permute-done((bf16[384,2048]{1,0:T(8,128)(2,1)S(1)}, bf16[384,2048]{1,0:T(8,128)(2,1)}, u32[]{:S(2)}, u32[]{:S(2)}) %collective-permute-start.55) | collective-permute-done | bytes 1572896 | tf_op jit(solution)/shard_map/ppermute | solution.py:74
  611.9 15.0 %collective-permute-done.61.refs_2_ = bf16[176,2048]{1,0:T(8,128)(2,1)S(1)} collective-permute-done((bf16[176,2048]{1,0:T(8,128)(2,1)S(1)}, bf16[176,2048]{1,0:T(8,128)(2,1)S(1)}, u32[]{:S(2)}, u32[]{:S(2)}) %collective-permute-start.61) | collective-permute-done | bytes 720928 | tf_op jit(solution)/shard_map/ppermute | solution.py:74
  712.3 20.6 %collective-permute-done.72 = bf16[384,2048]{1,0:T(8,128)(2,1)} collective-permute-done((bf16[384,2048]{1,0:T(8,128)(2,1)}, bf16[384,2048]{1,0:T(8,128)(2,1)}, u32[]{:S(2)}, u32[]{:S(2)}) %collective-permute-start.72) | collective-permute-done | bytes 1572896 | tf_op jit(solution)/shard_map/ppermute | solution.py:74
  739.2 17.5 %shard_map.260 = (bf16[768,512]{1,0:T(8,128)(2,1)}, bf16[768,512]{1,0:T(8,128)(2,1)}, f32[2,8,512]{2,1,0:T(8,128)}, bf16[384,2048]{1,0:T(8,128)(2,1)}, bf16[384,2048]{1,0:T(8,128)(2,1)}) custom-call(s32[8]{0:T(128)} %get-tuple-element.561.order_ref, bf16[256,2048]{1,0:T(8,128)(2,1)} %pad_maximum_fusion.4.refs_4_.refs_0_, bf16[256,2048]{1,0:T(8,128)(2,1)} %copy-done.7, ...), custom_call_target="tpu_custom_call" | custom-call | flops 4831838 | bytes 1024 | tf_op jit(solution)/shard_map/pallas_call | solution.py:395
  767.2 17.4 %shard_map.261 = (bf16[768,512]{1,0:T(8,128)(2,1)}, bf16[768,512]{1,0:T(8,128)(2,1)}, f32[2,8,512]{2,1,0:T(8,128)}, bf16[384,2048]{1,0:T(8,128)(2,1)}, bf16[384,2048]{1,0:T(8,128)(2,1)}) custom-call(s32[8]{0:T(128)} %get-tuple-element.561.order_ref, bf16[256,2048]{1,0:T(8,128)(2,1)} %pad_maximum_fusion.4.refs_4_.refs_0_, bf16[256,2048]{1,0:T(8,128)(2,1)} %copy-done.7, ...), custom_call_target="tpu_custom_call" | custom-call | flops 4831838 | bytes 1024 | tf_op jit(solution)/shard_map/pallas_call | solution.py:395
  817.2 29.7 %collective-permute-done.104 = f32[2,2,64]{2,1,0:T(2,128)S(1)} collective-permute-done((f32[2,2,64]{2,1,0:T(2,128)S(1)}, f32[2,2,64]{2,1,0:T(2,128)S(1)}, u32[]{:S(2)}, u32[]{:S(2)}) %collective-permute-start.104) | collective-permute-done | bytes 1056 | tf_op jit(solution)/shard_map/ppermute | solution.py:74
  919.0 26.1 %collective-permute-done.89 = bf16[128,2048]{1,0:T(8,128)(2,1)S(1)} collective-permute-done((bf16[128,2048]{1,0:T(8,128)(2,1)S(1)}, bf16[128,2048]{1,0:T(8,128)(2,1)S(1)}, u32[]{:S(2)}, u32[]{:S(2)}) %collective-permute-start.89) | collective-permute-done | bytes 524320 | tf_op jit(solution)/shard_map/ppermute | solution.py:68
  (626 shorter events, 517.7 us)
Async XLA Ops:
  7.4 45.8 %all-to-all-start = ((bf16[8,400,256]{2,1,0:T(8,128)(2,1)}), bf16[8,400,256]{2,1,0:T(8,128)(2,1)}, u32[]{:S(2)}, u32[]{:S(2)}) async-start(bf16[8,400,256]{2,1,0:T(8,128)(2,1)} %pad_maximum_fusion), calls=%async_computation | async-start | bytes 3276800 | tf_op jit(solution)/shard_map/all_to_all | solution.py:824
  83.1 53.1 %collective-permute-start.1 = (bf16[384,2048]{1,0:T(8,128)(2,1)}, bf16[384,2048]{1,0:T(8,128)(2,1)}, u32[]{:S(2)}, u32[]{:S(2)}) collective-permute-start(bf16[384,2048]{1,0:T(8,128)(2,1)} %get-tuple-element.222.refs_0_), channel_id=1, source_target_pairs={{0,16},{8,24},{16,0},{24,8},{1,17},{9,25},{17,1},{25,9},{2,18},{10... | collective-permute-start | bytes 4718600 | tf_op jit(solution)/shard_map/ppermute | solution.py:74
  224.4 43.1 %collective-permute-start.19 = (bf16[384,2048]{1,0:T(8,128)(2,1)}, bf16[384,2048]{1,0:T(8,128)(2,1)}, u32[]{:S(2)}, u32[]{:S(2)}) collective-permute-start(bf16[384,2048]{1,0:T(8,128)(2,1)} %add_convert_fusion.6), channel_id=1, source_target_pairs={{0,16},{8,24},{16,0},{24,8},{1,17},{9,25},{17,1},{25,9},{2,18},{10... | collective-permute-start | bytes 4718600 | tf_op jit(solution)/shard_map/ppermute | solution.py:74
  226.3 41.3 %collective-permute-start.22 = (bf16[352,2048]{1,0:T(8,128)(2,1)}, bf16[352,2048]{1,0:T(8,128)(2,1)}, u32[]{:S(2)}, u32[]{:S(2)}) collective-permute-start(bf16[352,2048]{1,0:T(8,128)(2,1)} %collective-permute-done.12.refs_10_.refs_8_), channel_id=1, source_target_pairs={{0,1},{2,0},{4,2},{6,4},{7,6},{5,7},{3,5},{1,3},{8,9},{10,8},{12,1... | collective-permute-start | bytes 4325384 | tf_op jit(solution)/shard_map/ppermute | solution.py:68
  228.5 66.6 %all-to-all-start.1 = ((bf16[8,384,256]{2,1,0:T(8,128)(2,1)}), bf16[8,384,256]{2,1,0:T(8,128)(2,1)}, u32[]{:S(2)}, u32[]{:S(2)}) async-start(bf16[8,384,256]{2,1,0:T(8,128)(2,1)} %bitcast.274), calls=%async_computation.1 | async-start | bytes 3145728 | tf_op jit(solution)/shard_map/all_to_all | solution.py:824
  274.5 42.3 %collective-permute-start.23 = (bf16[384,2048]{1,0:T(8,128)(2,1)}, bf16[384,2048]{1,0:T(8,128)(2,1)}, u32[]{:S(2)}, u32[]{:S(2)}) collective-permute-start(bf16[384,2048]{1,0:T(8,128)(2,1)} %multiply_convert_fusion.1.refs_0_), channel_id=1, source_target_pairs={{0,8},{8,0},{16,24},{24,16},{1,9},{9,1},{17,25},{25,17},{2,10},{10... | collective-permute-start | bytes 4718600 | tf_op jit(solution)/shard_map/ppermute | solution.py:74
  274.5 42.3 %collective-permute-start.24 = (bf16[384,2048]{1,0:T(8,128)(2,1)}, bf16[384,2048]{1,0:T(8,128)(2,1)}, u32[]{:S(2)}, u32[]{:S(2)}) collective-permute-start(bf16[384,2048]{1,0:T(8,128)(2,1)} %multiply_convert_fusion.1.refs_0_), channel_id=1, source_target_pairs={{0,16},{8,24},{16,0},{24,8},{1,17},{9,25},{17,1},{25,9},{2,18},{10... | collective-permute-start | bytes 4718600 | tf_op jit(solution)/shard_map/ppermute | solution.py:74
  275.0 41.8 %collective-permute-start.26 = (bf16[352,2048]{1,0:T(8,128)(2,1)}, bf16[352,2048]{1,0:T(8,128)(2,1)}, u32[]{:S(2)}, u32[]{:S(2)}) collective-permute-start(bf16[352,2048]{1,0:T(8,128)(2,1)} %collective-permute-done.22.refs_9_.refs_7_), channel_id=1, source_target_pairs={{0,1},{2,0},{4,2},{6,4},{7,6},{5,7},{3,5},{1,3},{8,9},{10,8},{12,1... | collective-permute-start | bytes 4325384 | tf_op jit(solution)/shard_map/ppermute | solution.py:68
  327.6 62.3 %collective-permute-start.34 = (bf16[384,2048]{1,0:T(8,128)(2,1)S(1)}, bf16[384,2048]{1,0:T(8,128)(2,1)}, u32[]{:S(2)}, u32[]{:S(2)}) collective-permute-start(bf16[384,2048]{1,0:T(8,128)(2,1)S(1)} %copy-done.10), channel_id=1, source_target_pairs={{0,8},{8,0},{16,24},{24,16},{1,9},{9,1},{17,25},{25,17},{2,10},{10... | collective-permute-start | bytes 4718600 | tf_op jit(solution)/shard_map/ppermute | solution.py:74
  327.9 62.0 %collective-permute-start.35 = (bf16[384,2048]{1,0:T(8,128)(2,1)S(1)}, bf16[384,2048]{1,0:T(8,128)(2,1)}, u32[]{:S(2)}, u32[]{:S(2)}) collective-permute-start(bf16[384,2048]{1,0:T(8,128)(2,1)S(1)} %copy-done.10), channel_id=1, source_target_pairs={{0,16},{8,24},{16,0},{24,8},{1,17},{9,25},{17,1},{25,9},{2,18},{10... | collective-permute-start | bytes 4718600 | tf_op jit(solution)/shard_map/ppermute | solution.py:74
  579.1 47.7 %collective-permute-start.58 = (bf16[352,2048]{1,0:T(8,128)(2,1)S(1)}, bf16[352,2048]{1,0:T(8,128)(2,1)S(1)}, u32[]{:S(2)}, u32[]{:S(2)}) collective-permute-start(bf16[352,2048]{1,0:T(8,128)(2,1)S(1)} %add_convert_fusion.13), channel_id=1, source_target_pairs={{0,2},{2,4},{4,6},{6,7},{7,5},{5,3},{3,1},{1,0},{8,10},{10,12},{12... | collective-permute-start | bytes 4325384 | tf_op jit(solution)/shard_map/ppermute | solution.py:68
  580.2 47.8 %collective-permute-start.59 = (bf16[352,2048]{1,0:T(8,128)(2,1)S(1)}, bf16[352,2048]{1,0:T(8,128)(2,1)S(1)}, u32[]{:S(2)}, u32[]{:S(2)}) collective-permute-start(bf16[352,2048]{1,0:T(8,128)(2,1)S(1)} %add_convert_fusion.12), channel_id=1, source_target_pairs={{0,1},{2,0},{4,2},{6,4},{7,6},{5,7},{3,5},{1,3},{8,9},{10,8},{12,1... | collective-permute-start | bytes 4325384 | tf_op jit(solution)/shard_map/ppermute | solution.py:68
  581.2 45.6 %collective-permute-start.61 = (bf16[176,2048]{1,0:T(8,128)(2,1)S(1)}, bf16[176,2048]{1,0:T(8,128)(2,1)S(1)}, u32[]{:S(2)}, u32[]{:S(2)}) collective-permute-start(bf16[176,2048]{1,0:T(8,128)(2,1)S(1)} %copy-done.30), channel_id=1, source_target_pairs={{0,16},{8,24},{16,0},{24,8},{1,17},{9,25},{17,1},{25,9},{2,18},{10... | collective-permute-start | bytes 2162696 | tf_op jit(solution)/shard_map/ppermute | solution.py:74
  665.9 46.4 %collective-permute-start.70 = (bf16[384,2048]{1,0:T(8,128)(2,1)}, bf16[384,2048]{1,0:T(8,128)(2,1)}, u32[]{:S(2)}, u32[]{:S(2)}) collective-permute-start(bf16[384,2048]{1,0:T(8,128)(2,1)} %get-tuple-element.378), channel_id=1, source_target_pairs={{0,8},{8,0},{16,24},{24,16},{1,9},{9,1},{17,25},{25,17},{2,10},{10... | collective-permute-start | bytes 4718600 | tf_op jit(solution)/shard_map/ppermute | solution.py:74
  757.6 91.1 %all-to-all-start.2 = ((bf16[8,384,256]{2,1,0:T(8,128)(2,1)}), bf16[8,384,256]{2,1,0:T(8,128)(2,1)S(1)}, u32[]{:S(2)}, u32[]{:S(2)}) async-start(bf16[8,384,256]{2,1,0:T(8,128)(2,1)} %bitcast.261), calls=%async_computation.2 | async-start | bytes 3145728 | tf_op jit(solution)/shard_map/all_to_all | solution.py:824
  788.6 61.4 %collective-permute-start.76 = (bf16[384,2048]{1,0:T(8,128)(2,1)}, bf16[384,2048]{1,0:T(8,128)(2,1)}, u32[]{:S(2)}, u32[]{:S(2)}) collective-permute-start(bf16[384,2048]{1,0:T(8,128)(2,1)} %get-tuple-element.397), channel_id=1, source_target_pairs={{0,8},{8,0},{16,24},{24,16},{1,9},{9,1},{17,25},{25,17},{2,10},{10... | collective-permute-start | bytes 4718600 | tf_op jit(solution)/shard_map/ppermute | solution.py:74
  810.5 42.4 %collective-permute-start.77 = (bf16[128,2048]{1,0:T(8,128)(2,1)}, bf16[128,2048]{1,0:T(8,128)(2,1)}, u32[]{:S(2)}, u32[]{:S(2)}) collective-permute-start(bf16[128,2048]{1,0:T(8,128)(2,1)} %add_convert_fusion.39), channel_id=1, source_target_pairs={{0,2},{2,4},{4,6},{6,7},{7,5},{5,3},{3,1},{1,0},{8,10},{10,12},{12... | collective-permute-start | bytes 1572872 | tf_op jit(solution)/shard_map/ppermute | solution.py:68
  810.5 42.3 %collective-permute-start.78 = (bf16[128,2048]{1,0:T(8,128)(2,1)}, bf16[128,2048]{1,0:T(8,128)(2,1)}, u32[]{:S(2)}, u32[]{:S(2)}) collective-permute-start(bf16[128,2048]{1,0:T(8,128)(2,1)} %add_convert_fusion.38), channel_id=1, source_target_pairs={{0,1},{2,0},{4,2},{6,4},{7,6},{5,7},{3,5},{1,3},{8,9},{10,8},{12,1... | collective-permute-start | bytes 1572872 | tf_op jit(solution)/shard_map/ppermute | solution.py:68
  812.6 60.2 %collective-permute-start.81 = (bf16[384,2048]{1,0:T(8,128)(2,1)}, bf16[384,2048]{1,0:T(8,128)(2,1)S(1)}, u32[]{:S(2)}, u32[]{:S(2)}) collective-permute-start(bf16[384,2048]{1,0:T(8,128)(2,1)} %add_convert_fusion.1), channel_id=1, source_target_pairs={{0,16},{8,24},{16,0},{24,8},{1,17},{9,25},{17,1},{25,9},{2,18},{10... | collective-permute-start | bytes 4718600 | tf_op jit(solution)/shard_map/ppermute | solution.py:74
  873.0 45.5 %collective-permute-start.106 = (bf16[352,2048]{1,0:T(8,128)(2,1)}, bf16[352,2048]{1,0:T(8,128)(2,1)}, u32[]{:S(2)}, u32[]{:S(2)}) collective-permute-start(bf16[352,2048]{1,0:T(8,128)(2,1)} %add_convert_fusion.8), channel_id=1, source_target_pairs={{0,16},{8,24},{16,0},{24,8},{1,17},{9,25},{17,1},{25,9},{2,18},{10... | collective-permute-start | bytes 4325384 | tf_op jit(solution)/shard_map/ppermute | solution.py:74
  891.0 66.8 %collective-permute-start.105 = (bf16[352,2048]{1,0:T(8,128)(2,1)}, bf16[352,2048]{1,0:T(8,128)(2,1)}, u32[]{:S(2)}, u32[]{:S(2)}) collective-permute-start(bf16[352,2048]{1,0:T(8,128)(2,1)} %add_convert_fusion.8), channel_id=1, source_target_pairs={{0,8},{8,0},{16,24},{24,16},{1,9},{9,1},{17,25},{25,17},{2,10},{10... | collective-permute-start | bytes 4325384 | tf_op jit(solution)/shard_map/ppermute | solution.py:74
  896.5 98.5 %all-to-all-start.3 = ((bf16[8,400,256]{2,1,0:T(8,128)(2,1)}), bf16[8,400,256]{2,1,0:T(8,128)(2,1)S(1)}, u32[]{:S(2)}, u32[]{:S(2)}) async-start(bf16[8,400,256]{2,1,0:T(8,128)(2,1)} %bitcast.259), calls=%async_computation.3 | async-start | bytes 3276800 | tf_op jit(solution)/shard_map/all_to_all | solution.py:824
  917.7 53.1 %collective-permute-start.99 = (bf16[128,2048]{1,0:T(8,128)(2,1)}, bf16[128,2048]{1,0:T(8,128)(2,1)S(1)}, u32[]{:S(2)}, u32[]{:S(2)}) collective-permute-start(bf16[128,2048]{1,0:T(8,128)(2,1)} %collective-permute-done.98), channel_id=1, source_target_pairs={{0,8},{8,0},{16,24},{24,16},{1,9},{9,1},{17,25},{25,17},{2,10},{10... | collective-permute-start | bytes 1572872 | tf_op jit(solution)/shard_map/ppermute | solution.py:74
  918.5 65.3 %collective-permute-start.107 = (bf16[352,2048]{1,0:T(8,128)(2,1)}, bf16[352,2048]{1,0:T(8,128)(2,1)S(1)}, u32[]{:S(2)}, u32[]{:S(2)}) collective-permute-start(bf16[352,2048]{1,0:T(8,128)(2,1)} %collective-permute-done.106), channel_id=1, source_target_pairs={{0,8},{8,0},{16,24},{24,16},{1,9},{9,1},{17,25},{25,17},{2,10},{10... | collective-permute-start | bytes 4325384 | tf_op jit(solution)/shard_map/ppermute | solution.py:74
  (195 other events, 3082.7 us)

commit v3 on v2

--- a/solution.py
+++ b/solution.py
@@ -11,6 +11,8 @@
 EPS = 1e-06
 F32, BF16 = jnp.float32, jnp.bfloat16
 VMEM_LIMIT = 56 * 1024 * 1024
+NO_COST = pl.CostEstimate(flops=1, bytes_accessed=1, transcendentals=0)
+LONG = pl.CostEstimate(flops=10**12, bytes_accessed=10**9, transcendentals=0)
 
 
 def params(**more):
@@ -83,12 +85,22 @@
             out[bit] = self.swap(x, bit)
         return out
 
-    def gather_rest(self, out):
+    def gather_rest(self, out, end=None):
         out = list(out)
-        for j in range(self.seq):
+        for j in range(end or self.seq):
             if out[j] is None:
                 out[j] = self.swap(out[j & (j - 1)], j & -j)
         return out
+
+    def gather_near(self, x):
+        out = [x]
+        for bit in self.bits[:-1]:
+            out = out + [self.swap(y, bit) for y in out]
+        return out
+
+    def halved(self, x):
+        half = x.shape[0] // 2
+        return [x[:half], x[half:]]
 
     def quad_far_part(self, parts):
         parts = list(parts)
@@ -173,33 +185,46 @@
 
 
 class RingScatter:
-    def __init__(self, net, chunk):
-        self.net, self.chunk = net, chunk
+    def __init__(self, net, wholes, canonical):
+        self.net, self.wholes, self.canonical = net, wholes, canonical
+        self.sizes = [w.shape[0] // net.tp for w in wholes]
+        self.size = sum(self.sizes)
         self.d = net.tp // 2
         self.came = ()
-        self.half = net.halves(chunk(self.d).shape[0]) if net.tp % 2 == 0 else 0
+        self.half = net.halves(self.size) if net.tp % 2 == 0 else 0
 
     def done(self):
         return self.d == 0
 
-    def plus(self, own, part, start):
-        if part is None:
-            return own
-        rest = own.shape[0] - start - part.shape[0]
-        return (own.astype(F32) + jnp.pad(part.astype(F32), ((start, rest), (0, 0)))).astype(BF16)
+    def make(self, outs):
+        net = self.net
+        made = []
+        for d, low, high, adds in outs:
+            rows = []
+            for w, q in zip(self.wholes, self.sizes):
+                at = net.behind[d] * q if self.canonical else d * q
+                rows.append(lax.dynamic_slice_in_dim(w, at, q, 0))
+            whole = jnp.concatenate(rows, 0)[low:high]
+            for part, start in adds:
+                first = start - low
+                part = jnp.pad(part.astype(F32), ((first, high - low - first - part.shape[0]), (0, 0)))
+                whole = whole.astype(F32) + part
+            made.append(whole.astype(BF16))
+        return made
+
+    def adds(self, which):
+        if not self.came:
+            return []
+        after_half = which == 1 and 2 * (self.d + 1) == self.net.tp
+        return [(self.came[which], self.half if after_half else 0)]
 
     def sends(self):
         if self.done():
             return ()
         n, d = self.net.tp, self.d
         if 2 * d == n:
-            far = self.chunk(d)
-            return far[: self.half], far[self.half :]
-        fore, back = self.came if self.came else (None, None)
-        return self.plus(self.chunk(n - d), fore, 0), self.plus(self.chunk(d), back, self.start())
-
-    def start(self):
-        return self.half if 2 * (self.d + 1) == self.net.tp else 0
+            return self.make([(d, 0, self.half, []), (d, self.half, self.size, [])])
+        return self.make([(n - d, 0, self.size, self.adds(0)), (d, 0, self.size, self.adds(1))])
 
     def launch(self, sends):
         if self.done():
@@ -210,9 +235,7 @@
     def result(self):
         while not self.done():
             self.launch(self.sends())
-        own = self.chunk(0)
-        start = self.start()
-        return self.plus(self.plus(own, self.came[0], 0), self.came[1], start)
+        return self.make([(0, 0, self.size, self.adds(0) + self.adds(1))])[0]
 
 
 SMEM_SPEC = pl.BlockSpec(memory_space=pltpu.SMEM)
@@ -241,6 +264,7 @@
         in_specs=[VMEM_SPEC] * 2,
         out_specs=[VMEM_SPEC] * 2,
         compiler_params=params(),
+        cost_estimate=NO_COST,
     )(gain.reshape(1, width), blocks)
 
 
@@ -259,6 +283,7 @@
         in_specs=[VMEM_SPEC] * 2,
         out_specs=VMEM_SPEC,
         compiler_params=params(),
+        cost_estimate=NO_COST,
     )(live, blocks)
 
 
@@ -335,9 +360,10 @@
         return out
 
 
-def step_kernel(body, order, count, rows, blocks, weights, ins, outs, width, cost, onto=()):
+def step_kernel(body, order, count, rows, blocks, weights, ins, outs, width, onto=(), long=True):
     any_spec = pl.BlockSpec(memory_space=pl.ANY)
-    n_x, n_w, n_in, n_out = len(blocks), len(weights.arrays), len(ins), len(outs)
+    pieces = [(j, i, sum(a.shape[0] for a in block[:i]), a) for j, block in enumerate(blocks) for i, a in enumerate(block)]
+    n_x, n_w, n_in, n_out = len(pieces), len(weights.arrays), len(ins), len(outs)
     n_part = count if width else 0
     n_held, n_onto = len(weights.shapes), len(onto)
 
@@ -356,7 +382,10 @@
         kept, part_sems = take(2) if n_part else (None, None)
         j = pl.program_id(0)
         loads = weights.copies(order_ref, w_refs, held, w_sems)
-        x_loads = [pltpu.make_async_copy(x_refs[k], xs.at[k], x_sems.at[k]) for k in range(n_x)]
+        x_loads = [
+            pltpu.make_async_copy(x_refs[k], xs.at[at, pl.ds(start, a.shape[0])], x_sems.at[k])
+            for k, (at, _, start, a) in enumerate(pieces)
+        ]
 
         @pl.when(j == 0)
         def _():
@@ -367,7 +396,7 @@
 
         for k in range(n_x):
 
-            @pl.when(j == k)
+            @pl.when(j == pieces[k][0])
             def _(k=k):
                 x_loads[k].wait()
 
@@ -389,7 +418,7 @@
     scratch = [pltpu.VMEM(shape, BF16) for shape in weights.shapes]
     scratch.append(pltpu.SemaphoreType.DMA((max(len(weights.takes), 1),)))
     if n_x:
-        scratch += [pltpu.VMEM((n_x,) + blocks[0].shape, BF16), pltpu.SemaphoreType.DMA((n_x,))]
+        scratch += [pltpu.VMEM((len(blocks), rows, pieces[0][3].shape[1]), BF16), pltpu.SemaphoreType.DMA((n_x,))]
     if n_part:
         scratch += [pltpu.VMEM((2, rows, width), BF16), pltpu.SemaphoreType.DMA((n_part,))]
     out = pl.pallas_call(
@@ -401,8 +430,8 @@
         input_output_aliases={1 + n_x + n_w + n_in + i: i for i in range(n_onto)},
         scratch_shapes=scratch,
         compiler_params=params(),
-        cost_estimate=pl.CostEstimate(flops=cost // 1000, bytes_accessed=1024, transcendentals=0),
-    )(order, *blocks, *weights.arrays, *[a for a, _ in ins], *onto)
+        cost_estimate=LONG if long else NO_COST,
+    )(order, *[a for _, _, _, a in pieces], *weights.arrays, *[a for a, _ in ins], *onto)
     return list(out[:n_out]), list(out[n_out:])
 
 
@@ -458,7 +487,7 @@
         (shape_of(count, slots, wide), by_slot(slots, wide)),
     ]
     return step_kernel(
-        body, order, count, rows, blocks, weights, [(bound, whole_row(wide))], outs, 0, 6 * count * rows * wide * depth
+        body, order, count, rows, [[x] for x in blocks], weights, [(bound, whole_row(wide))], outs, 0
     )[0]
 
 
@@ -478,10 +507,11 @@
         in_specs=[SMEM_SPEC] + [VMEM_SPEC] * 4,
         out_specs=VMEM_SPEC,
         compiler_params=params(),
+        cost_estimate=NO_COST,
     )(place, *before, *whole)
 
 
-def mixer_out(order, pre, bound, gain, head, weights, pos_n):
+def mixer_out(order, pre, bound, gain, head, weights, pos_n, first, steps, onto=(), long=True):
     wide = bound.shape[1]
     count, slots, _ = head.shape
     rows = slots * pos_n
@@ -512,20 +542,20 @@
         return dot_nn(mix, held[0][...]).astype(BF16)
 
     ins = [
-        (pre, by_block(rows, 3 * wide)),
+        (pre, by_block(rows, 3 * wide, first)),
         (bound, whole_row(wide)),
         (gain, whole_row(wide)),
-        (head, by_slot(slots, wide)),
+        (head, by_slot(slots, wide, first)),
     ]
     outs = [
-        (shape_of(count * rows, wide), by_block(rows, wide)),
-        (shape_of(count * rows, wide, dtype=BF16), by_block(rows, wide)),
-        (shape_of(count * rows, 128), by_block(rows, 128)),
+        (shape_of(count * rows, wide), by_block(rows, wide, first)),
+        (shape_of(count * rows, wide, dtype=BF16), by_block(rows, wide, first)),
+        (shape_of(count * rows, 128), by_block(rows, 128, first)),
     ]
-    return step_kernel(body, order, count, rows, [], weights, ins, outs, depth, 2 * count * rows * wide * depth)
-
-
-def feed_forward(order, blocks, weights, first, count, onto=()):
+    return step_kernel(body, order, steps, rows, [], weights, ins, outs, depth, onto, long)
+
+
+def feed_forward(order, blocks, weights, first, count, onto=(), long=True):
     (rows, depth), wide = blocks[0].shape, weights.shapes[0][0]
 
     def body(x, held, ins, outs):
@@ -542,8 +572,7 @@
 
     outs = [(shape_of(count * rows, wide, dtype=BF16), by_block(rows, wide, first))] * 3
     outs = outs + [(shape_of(count * rows, depth, dtype=BF16), by_block(rows, depth, first))]
-    cost = 4 * len(blocks) * rows * wide * depth
-    return step_kernel(body, order, len(blocks), rows, blocks, weights, [], outs, 0, cost, onto)[0]
+    return step_kernel(body, order, len(blocks), rows, [[x] for x in blocks], weights, [], outs, 0, onto, long)[0]
 
 
 def down_parts(order, hidden, weights, rows):
@@ -554,7 +583,7 @@
         return dot_nn(ins[0][...], held[0][...]).astype(BF16)
 
     return step_kernel(
-        body, order, count, rows, [], weights, [(hidden, by_block(rows, wide))], [], depth, 2 * count * rows * wide * depth
+        body, order, count, rows, [], weights, [(hidden, by_block(rows, wide))], [], depth
     )[1]
 
 
@@ -572,7 +601,7 @@
     block = by_block(rows, wide)
     ins = [(g, by_block(rows, depth)), (slope, block), (act, block)]
     outs = [(shape_of(count * rows, wide, dtype=BF16), block)] * 2
-    return step_kernel(body, order, count, rows, [], weights, ins, outs, 0, 2 * count * rows * wide * depth)[0]
+    return step_kernel(body, order, count, rows, [], weights, ins, outs, 0)[0]
 
 
 def back_pair(order, a, b, weights, rows, first, count):
@@ -583,12 +612,12 @@
 
     block = by_block(rows, wide, first)
     return step_kernel(
-        body, order, count, rows, [], weights, [(a, block), (b, block)], [], depth, 4 * count * rows * wide * depth
+        body, order, count, rows, [], weights, [(a, block), (b, block)], [], depth
     )[1]
 
 
-def back_mixer(order, blocks, weights, pre, state, mix, r_mix, gain):
-    count, (rows, depth), wide = len(blocks), blocks[0].shape, gain.shape[1]
+def back_mixer(order, blocks, rows, weights, pre, state, mix, r_mix, gain):
+    count, depth, wide = len(blocks), blocks[0][0].shape[1], gain.shape[1]
 
     def body(x, held, ins, outs):
         og_ref, state_ref, mix_ref, r_ref, gain_ref = ins
@@ -622,7 +651,7 @@
         (shape_of(count * rows, 128), by_block(rows, 128)),
         (shape_of(count, 8, wide), by_slot(8, wide)),
     ]
-    return step_kernel(body, order, count, rows, blocks, weights, ins, outs, 0, 2 * count * rows * wide * depth)[0]
+    return step_kernel(body, order, count, rows, blocks, weights, ins, outs, 0)[0]
 
 
 def back_ends(pre, bound, norm, state, r_mix, coef, slots, pos_n):
@@ -663,10 +692,11 @@
         ],
         out_specs=by_slot(slots, wide),
         compiler_params=params(),
+        cost_estimate=NO_COST,
     )(pre, norm, state, r_mix, coef, bound)
 
 
-def back_states(order, pre, bound, norm, state, g_og, r_mix, coef, head, tail, weights, pos_n, first, count):
+def back_states(order, pre, bound, norm, state, g_og, r_mix, coef, head, tail, weights, pos_n, first, count, long=True):
     wide = norm.shape[1]
     slots = head.shape[1]
     rows = slots * pos_n
@@ -727,7 +757,95 @@
     ]
     outs = [(shape_of(count * rows, wide, dtype=BF16), by_block(rows, wide))] * 2
     outs = outs + [(shape_of(count, 8, wide), by_slot(8, wide))]
-    return step_kernel(body, order, count, rows, [], weights, ins, outs, depth, 6 * count * rows * wide * depth)
+    return step_kernel(body, order, count, rows, [], weights, ins, outs, depth, (), long)
+
+
+def joined(refs):
+    return jnp.concatenate([r[...].astype(F32) for r in refs], 0)
+
+
+def whole_kernel(body, outs, *arrays):
+    return pl.pallas_call(
+        body,
+        out_shape=outs,
+        in_specs=[VMEM_SPEC] * len(arrays),
+        out_specs=[VMEM_SPEC] * len(outs),
+        compiler_params=params(),
+        cost_estimate=NO_COST,
+    )(*arrays)
+
+
+def residual(near, moved, tok, r_mix, gain):
+    rows, width = tok.shape
+
+    def body(near_ref, moved_ref, tok_ref, r_ref, gain_ref, resid_ref, out_ref):
+        branch = near_ref[...].astype(F32) + moved_ref[...].astype(F32)
+        resid = tok_ref[...].astype(F32) + r_ref[...] * branch
+        resid_ref[...] = resid
+        r = lax.rsqrt(jnp.sum(resid * resid, axis=-1, keepdims=True) / width + EPS)
+        out_ref[...] = (resid * r * gain_ref[...]).astype(BF16)
+
+    outs = [shape_of(rows, width), shape_of(rows, width, dtype=BF16)]
+    return whole_kernel(body, outs, near, moved, tok, r_mix, gain)
+
+
+def back_residual(near, moved, resid, cot, gain):
+    rows, width = resid.shape
+
+    def body(near_ref, first_ref, second_ref, resid_ref, cot_ref, gain_ref, grad_ref, out_ref, sum_ref):
+        g = near_ref[...].astype(F32) + joined((first_ref, second_ref))
+        resid = resid_ref[...]
+        r = lax.rsqrt(jnp.sum(resid * resid, axis=-1, keepdims=True) / width + EPS)
+        scaled = resid * r
+        sum_ref[...] = jnp.sum(g * scaled, axis=0, keepdims=True)
+        g = g * gain_ref[...]
+        inner = jnp.sum(resid * g, axis=-1, keepdims=True)
+        grad = cot_ref[...].astype(F32) + r * g - resid * (r * r * r * inner / width)
+        grad_ref[...] = grad
+        out_ref[...] = grad.astype(BF16)
+
+    outs = [shape_of(rows, width), shape_of(rows, width, dtype=BF16), shape_of(1, width)]
+    return whole_kernel(body, outs, near, *moved, resid, cot, gain)
+
+
+def block_output(near, moved, resid, live, count):
+    rows, width = resid.shape
+    cols = width // count
+
+    def body(near_ref, moved_ref, resid_ref, live_ref, out_ref):
+        for k in range(count):
+            at = slice(k * cols, (k + 1) * cols)
+            ffn = near_ref[:, at].astype(F32) + moved_ref[:, at].astype(F32)
+            out_ref[k] = (live_ref[...] * (resid_ref[:, at] + ffn)).astype(BF16)
+
+    return whole_kernel(body, [shape_of(count, rows, cols, dtype=BF16)], near, moved, resid, live)[0]
+
+
+def back_tokens(near, moved, tok, grad_resid, in_gain, mlp_sum, chan_rows):
+    rows, width = tok.shape
+    count, _, cols = chan_rows.shape
+
+    def body(near_ref, first_ref, second_ref, tok_ref, grad_ref, gain_ref, mlp_ref, chan_ref, out_ref):
+        g = near_ref[...].astype(F32) + joined((first_ref, second_ref))
+        x = tok_ref[...].astype(F32)
+        r = lax.rsqrt(jnp.sum(x * x, axis=-1, keepdims=True) / width + EPS)
+        in_sum = jnp.sum(g * x * r, axis=0, keepdims=True)
+        g = g * gain_ref[...]
+        inner = jnp.sum(x * g, axis=-1, keepdims=True)
+        grad = (grad_ref[...] + r * g - x * (r * r * r * inner / width)).astype(BF16)
+        place = lax.broadcasted_iota(jnp.int32, (16, cols), 0)
+        for k in range(count):
+            at = slice(k * cols, (k + 1) * cols)
+            out_ref[k, :rows, :] = grad[:, at]
+            extra = jnp.zeros((16, cols), F32)
+            for i, total in enumerate((in_sum[:, at], mlp_ref[:, at])):
+                high = total.astype(BF16).astype(F32)
+                extra = jnp.where(place == i, high, jnp.where(place == 2 + i, total - high, extra))
+            extra = jnp.where(place == 4, chan_ref[k], extra)
+            out_ref[k, rows:, :] = extra.astype(BF16)
+
+    outs = [shape_of(count, rows + 16, cols, dtype=BF16)]
+    return whole_kernel(body, outs, near, *moved, tok, grad_resid, in_gain, mlp_sum, chan_rows)[0]
 
 
 def order_rows(blocks, place):
@@ -748,6 +866,7 @@
         in_specs=[SMEM_SPEC] + [pl.BlockSpec((q, tile), lambda i: (0, i))] * count,
         out_specs=pl.BlockSpec((count * q, tile), lambda i: (0, i)),
         compiler_params=params(),
+        cost_estimate=NO_COST,
     )(place, *blocks)
 
 
@@ -770,6 +889,7 @@
         out_specs=pl.BlockSpec((tile, count * q), lambda i: (i, 0)),
         scratch_shapes=[pltpu.VMEM((count, q, tile), F32)],
         compiler_params=params(),
+        cost_estimate=NO_COST,
     )(place, *blocks)
 
 
@@ -826,9 +946,6 @@
     def in_place(x):
         return x.reshape(n_tp, slots, pos_n, cols).transpose(1, 0, 2, 3).reshape(tokens.shape)
 
-    def total(terms):
-        return sum(p.astype(F32) for p in terms)
-
     where = s * group + t * pos_n + jnp.arange(pos_n, dtype=jnp.int32)
     live = (where[None, :] < lengths[:, None]).astype(F32).reshape(rows, 1)
 
@@ -859,9 +976,11 @@
     w3, wo = Weights(), Weights()
     w3.add(mix_ring, [(i * dq, i * chan) for i in range(3)], dq, True)
     wo.add(mix_ring, [(3 * dq, 0)], dq, True)
-    gate_w = jnp.concatenate([quarter_t(w_gate, fq), quarter_t(w_up, fq)], 0)
-    gate_ring = RingGather(net, after(gate_w, *mix_ring.came))
+    gate_ring = RingGather(net, after(quarter_t(w_gate, fq), *mix_ring.came))
+    up_ring = RingGather(net, after(quarter_t(w_up, fq), *mix_ring.came))
     gate_ring.launch(gate_ring.sends())
+    up_ring.launch(up_ring.sends())
+    half = n_seq // 2
 
     pre, normed_all, decay, end = mixer_in(order, normed, w3, bound, slots, pos_n)
 
@@ -881,64 +1000,56 @@
             whole = tuple(jnp.where(upper, a, b) for a, b in zip(ahead, behind))
         return before, whole
 
-    (decay, end), gate_ring.came = hold((decay, end), gate_ring.came)
+    (decay, end), gate_ring.came, up_ring.came = hold((decay, end), gate_ring.came, up_ring.came)
     head = scan_heads(place, *spread((decay, end), False), False)
-    head, sends, cot_sent = hold(head, gate_ring.sends(), by_owner(cotangent))
+    head, sends, up_sends = hold(head, gate_ring.sends(), up_ring.sends())
     gate_ring.launch(sends)
-    cot_blocks = to_owner(cot_sent)
-    (state, mix, squares), parts = mixer_out(order, pre, bound, gain, head, wo, pos_n)
-    parts, sum_all = hold(parts, jnp.sum(squares, -1).reshape(n_seq, rows))
-    sum_all = net.total_near(sum_all)
-    near, sum_all = hold(net.quad_near(parts), sum_all)
-    branch, sum_all = net.quad_far(near), net.total_far(sum_all)
-    branch, sum_all, gate_ring.came = hold(branch, sum_all, gate_ring.came)
-    gate_ring.launch(gate_ring.sends())
+    some, far = mixer_out(order, pre, bound, gain, head, wo, pos_n, half, half)
+    head_near, some = hold(head, some)
+    (state, mix, squares), parts = mixer_out(order, pre, bound, gain, head_near, wo, pos_n, 0, half, some, False)
+    near_far = net.quad_far_part(far)
+    near_far, parts, squares, gate_ring.came = hold(near_far, parts, squares, gate_ring.came)
+    moved_far = net.swap(near_far, net.bits[-1])
+    up_ring.launch(up_sends)
+    sum_all = net.total_far(net.total_near(jnp.sum(squares, -1).reshape(n_seq, rows)))
+    near_own = net.quad_far_part(parts)
+    near_own, up_ring.came, sends = hold(near_own, up_ring.came, gate_ring.sends())
+    gate_ring.launch(sends)
+    near_own, moved_far, sum_all, gate_ring.came, sends = hold(
+        near_own, moved_far, sum_all, gate_ring.came, up_ring.sends()
+    )
+    up_ring.launch(sends)
     r_mix = lax.rsqrt(sum_all / width + EPS).reshape(n_seq * rows, 1)
-    branch = total(branch)
-    resid = tok.astype(F32) + r_mix[:rows] * branch
-    r_mlp = lax.rsqrt(jnp.mean(resid * resid, axis=-1, keepdims=True) + EPS)
-    scaled = resid * r_mlp
-    mlp_own = (scaled * mlp_full).astype(BF16)
+    resid, mlp_own = residual(near_own, moved_far, tok, r_mix[:rows], mlp_full)
     mlp_in = net.gather_first(mlp_own)
-    cot = mask_rows(after(cot_blocks, mlp_own), live)
-    half = n_seq // 2
-    mlp_in, gate_ring.came, cot = hold(mlp_in, gate_ring.came, cot)
-    gate_ring.launch(gate_ring.sends())
+    up_ring.came, mlp_own, sends = hold(up_ring.came, mlp_own, gate_ring.sends())
+    gate_ring.launch(sends)
+    up_ring.launch(up_ring.sends())
     gate_ring.finish()
-    mlp_in = net.gather_rest(mlp_in)
-    grad_out = net.gather_first(cot)
+    up_ring.finish()
+    mlp_in = net.gather_rest(mlp_in, half)
     wgu = Weights()
     wgu.add(gate_ring, [(0, 0)], fq, False)
-    wgu.add(gate_ring, [(fq, 0)], fq, False)
+    wgu.add(up_ring, [(0, 0)], fq, False)
     down_w = lax.dynamic_slice_in_dim(w_down, s * fq, fq, 0)
-    mlp_in, down_w, _ = hold(mlp_in, down_w, gate_ring.came)
+    near_in, down_w, cot_sent, _ = hold(mlp_in[:half], down_w, by_owner(cotangent), (gate_ring.came, up_ring.came))
 
     down_ring = RingGather(net, down_w)
     down_ring.launch(down_ring.sends())
-    some = feed_forward(order, mlp_in[:half], wgu, 0, n_seq)
-    some, down_ring.came, far_in = hold(some, down_ring.came, mlp_in[half:])
+    cot_blocks = to_owner(cot_sent)
+    some = feed_forward(order, near_in, wgu, 0, n_seq)
+    some, far_first, down_ring.came = hold(some, mlp_in[half], down_ring.came)
     down_ring.launch(down_ring.sends())
-    hidden, slope_up, act, mlp_all = feed_forward(order, far_in, wgu, half, n_seq, some)
-    hidden, down_ring.came, grad_out = hold(hidden, down_ring.came, grad_out)
+    mlp_in = net.gather_rest(mlp_in[:half] + [far_first] + mlp_in[half + 1 :])
+    hidden, slope_up, act, mlp_all = feed_forward(order, mlp_in[half:], wgu, half, n_seq, some, False)
+    hidden, down_ring.came, cot_blocks = hold(hidden, down_ring.came, cot_blocks)
     down_ring.launch(down_ring.sends())
-    grad_out = net.gather_rest(grad_out)
-    grad_out, hidden, sends = hold(grad_out, hidden, down_ring.sends())
-    down_ring.launch(sends)
+    cot = mask_rows(cot_blocks, live)
+    grad_out = net.gather_first(cot)
+    grad_out, down_ring.came = hold(grad_out, down_ring.came)
+    down_ring.launch(down_ring.sends())
     down_ring.finish()
-    grad_all = jnp.concatenate(grad_out, 0)
-
-    def ring_sum(wholes, canonical, *others):
-        def chunk(d):
-            out = []
-            for w in wholes:
-                q = w.shape[0] // n_tp
-                if canonical:
-                    out.append(lax.dynamic_slice_in_dim(w, net.behind[d] * q, q, 0))
-                else:
-                    out.append(w[d * q : (d + 1) * q])
-            return jnp.concatenate(out, 0) if len(out) > 1 else out[0]
-
-        return RingScatter(net, chunk)
+    grad_all = jnp.concatenate(net.gather_rest(grad_out), 0)
 
     def to_output(blocks, turned):
         q = blocks[0].shape[0]
@@ -951,7 +1062,7 @@
         return out.T if turned else out
 
     dw_down = dot_tn(hidden, grad_all).astype(BF16)
-    down_sum = ring_sum([dw_down], False)
+    down_sum = RingScatter(net, [dw_down], False)
     wd = Weights()
     wd.add(down_ring, [(0, 0)], fq, False)
     sends, grad_all, _ = hold(down_sum.sends(), grad_all, down_ring.came)
@@ -960,135 +1071,135 @@
     grad_gate, down_sum.came = hold(grad_gate, down_sum.came)
     sends, grad_gate = hold(down_sum.sends(), grad_gate)
     down_sum.launch(sends)
-    dw_gate = dot_tn(grad_gate, mlp_all).astype(BF16)
-    dw_gate, down_sum.came = hold(dw_gate, down_sum.came)
-    sends, grad_up = hold(down_sum.sends(), grad_up)
+    far = back_pair(order, grad_gate, grad_up, wgu, rows, half, half)
+    far, down_sum.came = hold(far, down_sum.came)
+    sent, sends, grad_gate = hold(net.halved(net.quad_far_part(far)), down_sum.sends(), grad_gate)
+    moved = [net.swap(x, net.bits[-1]) for x in sent]
     down_sum.launch(sends)
-    dw_up = dot_tn(grad_up, mlp_all).astype(BF16)
-    dw_up, down_sum.came = hold(dw_up, down_sum.came)
+    parts = back_pair(order, grad_gate, grad_up, wgu, rows, 0, half)
+    parts, moved[0], down_sum.came = hold(parts, moved[0], down_sum.came)
     sends, grad_gate = hold(down_sum.sends(), grad_gate)
     down_sum.launch(sends)
-    far = back_pair(order, grad_gate, grad_up, wgu, rows, half, half)
-    far, down_sum.came = hold(far, down_sum.came)
-    near_far = net.quad_far_part(far)
+    near_own = net.quad_far_part(parts)
+    dw_gate = dot_tn(grad_gate, mlp_all).astype(BF16)
+    dw_gate, moved[1], near_own, down_sum.came = hold(dw_gate, moved[1], near_own, down_sum.came)
+    grad_resid, branch_own, mlp_sum = back_residual(near_own, moved, resid, cot, mlp_full)
+    gate_sum = RingScatter(net, [dw_gate], False)
+    branch_own, sends, sent, hidden = hold(branch_own, gate_sum.sends(), net.halved(branch_own), hidden)
+    grad_branch = [[x] for x in net.gather_near(branch_own)]
+    moved = [net.swap(x, net.bits[-1]) for x in sent]
+    gate_sum.launch(sends)
+    ffn_parts = down_parts(order, hidden, wd, rows)
+    ffn_parts, moved[0], grad_branch, gate_sum.came = hold(ffn_parts, moved[0], grad_branch, gate_sum.came)
+    grad_branch_a = net.gather_near(moved[0])
     down_own = down_sum.result()
-    gu_sum = ring_sum([dw_gate, dw_up], False)
-    near_far, down_own, grad_gate, sends = hold(near_far, down_own, grad_gate, gu_sum.sends())
-    gu_sum.launch(sends)
-    moved_far = net.swap(near_far, net.bits[-1])
-    parts = back_pair(order, grad_gate, grad_up, wgu, rows, 0, half)
-    parts, gu_sum.came = hold(parts, gu_sum.came)
-    near_own = net.quad_far_part(parts)
-    sends, near_own, hidden = hold(gu_sum.sends(), near_own, hidden)
-    gu_sum.launch(sends)
-    ffn_parts = down_parts(order, hidden, wd, rows)
-    moved_far, near_own, ffn_parts = hold(moved_far, near_own, ffn_parts)
-    grad_mlp_in = total([near_own, moved_far])
-
-    grad_mlp_gain = jnp.sum(grad_mlp_in * scaled, axis=0)
-    grad_scaled = grad_mlp_in * mlp_full
-    inner = jnp.sum(resid * grad_scaled, axis=-1, keepdims=True)
-    grad_resid = cot.astype(F32) + r_mlp * grad_scaled - resid * r_mlp**3 * inner / width
-    branch_own = grad_resid.astype(BF16)
-    grad_branch = net.gather_first(branch_own)
-    branch_own, gu_sum.came = hold(branch_own, gu_sum.came)
-    sends = hold(gu_sum.sends())[0]
-    gu_sum.launch(sends)
-    down_blocks = net.gather_first(after(down_own, *sends))
-
-    grad_branch, gu_sum.came, down_blocks = hold(grad_branch, gu_sum.came, down_blocks)
-    grad_branch, down_blocks = net.gather_rest(grad_branch), net.gather_rest(down_blocks)
-    sends, grad_branch = hold(gu_sum.sends(), grad_branch)
-    gu_sum.launch(sends)
+    sends, grad_up = hold(gate_sum.sends(), grad_up)
+    gate_sum.launch(sends)
+    ffn_near = net.quad_near(ffn_parts)
+    dw_up = dot_tn(grad_up, mlp_all).astype(BF16)
+    dw_up, moved[1], gate_sum.came, ffn_near = hold(dw_up, moved[1], gate_sum.came, ffn_near)
+    grad_branch = grad_branch + [list(x) for x in zip(grad_branch_a, net.gather_near(moved[1]))]
+    up_sum = RingScatter(net, [dw_up], False)
+
+    sends, up_sends, grad_branch, down_own = hold(gate_sum.sends(), up_sum.sends(), grad_branch, down_own)
+    gate_sum.launch(sends)
+    up_sum.launch(up_sends)
+    down_blocks = net.gather_first(down_own)
     g_norm, grad_og, mixed_out, branch_all, inner_lanes, gain_sums = back_mixer(
-        order, grad_branch, wo, pre, state, mix, r_mix, gain
+        order, grad_branch, rows, wo, pre, state, mix, r_mix, gain
     )
+    inner_lanes, gate_sum.came, up_sum.came, down_blocks = hold(
+        inner_lanes, gate_sum.came, up_sum.came, down_blocks
+    )
+    sends, up_sends, inner_lanes = hold(gate_sum.sends(), up_sum.sends(), inner_lanes)
+    gate_sum.launch(sends)
+    up_sum.launch(up_sends)
     inner = net.total_far(net.total_near(jnp.sum(inner_lanes, -1).reshape(n_seq, rows))).reshape(-1, 1)
-    ffn = net.quad_far(net.quad_near([after(p, inner) for p in ffn_parts]))
+    ffn = net.quad_far([after(p, inner) for p in ffn_near])
     coef = r_mix**3 * inner / width
     back_end = back_ends(pre, bound, g_norm, state, r_mix, coef, slots, pos_n)
     dw_out = dot_tn(after(mixed_out, back_end), branch_all).astype(BF16)
     dw_og = dot_tn(after(grad_og, dw_out), normed_all).astype(BF16)
-    back_end, gu_sum.came, dw_og = hold(back_end, gu_sum.came, dw_og)
+    back_end, gate_sum.came, up_sum.came, dw_og = hold(back_end, gate_sum.came, up_sum.came, dw_og)
     tail = scan_heads(place, *spread((decay, back_end), True), True)
-    gu_own = gu_sum.result()
-    mixed = (live * (resid + total(ffn))).astype(BF16)
-    mixed_sent = mixed.reshape(rows, n_tp, cols).transpose(1, 0, 2)
-    first_sum = ring_sum([dw_out, dw_og], True)
-    tail, gu_own, mixed_sent, sends = hold(tail, gu_own, mixed_sent, first_sum.sends())
+    gate_own = gate_sum.result()
+    tail, up_sends, gate_own = hold(tail, up_sum.sends(), gate_own)
+    up_sum.launch(up_sends)
+
+    def back(start, tail, long):
+        return back_states(
+            order, pre, bound, g_norm, state, grad_og, r_mix, coef, head, tail, w3, pos_n, start, half, long
+        )
+
+    (far_in, far_fg, far_low), far = back(half, tail, True)
+    far, far_in, up_sum.came, ffn = hold(far, far_in, up_sum.came, ffn)
+    first_sum = RingScatter(net, [dw_out, dw_og], True)
+    mixed_sent = block_output(*ffn, resid, live, n_tp)
+    sent, tail, up_sends, sends, mixed_sent = hold(
+        net.halved(net.quad_far_part(far)), tail, up_sum.sends(), first_sum.sends(), mixed_sent
+    )
+    moved = [net.swap(x, net.bits[-1]) for x in sent]
+    up_sum.launch(up_sends)
     first_sum.launch(sends)
     mixed_got = to_owner(mixed_sent)
-
-    def back(start, tail):
-        return back_states(
-            order, pre, bound, g_norm, state, grad_og, r_mix, coef, head, tail, w3, pos_n, start, half
-        )
-
-    (far_in, far_fg, far_low), far = back(half, tail)
-    far, far_in, first_sum.came = hold(far, far_in, first_sum.came)
-    near_far = net.quad_far_part(far)
-    near_far, sends, tail = hold(near_far, first_sum.sends(), tail)
-    moved_far = net.swap(near_far, net.bits[-1])
-    first_sum.launch(sends)
-    (grad_in, grad_fg, low_sums), parts = back(0, tail)
-    near_own = net.quad_far_part(parts)
+    (grad_in, grad_fg, low_sums), parts = back(0, tail, True)
+    parts, moved[0], first_sum.came, up_sum.came = hold(parts, moved[0], first_sum.came, up_sum.came)
+    up_own = up_sum.result()
     low_sums = low_sums + far_low
     grad_in, grad_fg = (jnp.concatenate([a, b], 0) for a, b in ((grad_in, far_in), (grad_fg, far_fg)))
-    near_own, first_sum.came, grad_in = hold(near_own, first_sum.came, grad_in)
-    sends, grad_in = hold(first_sum.sends(), grad_in)
+    sends, up_own, grad_in = hold(first_sum.sends(), up_own, grad_in)
     first_sum.launch(sends)
+    near_own = net.quad_far_part(parts)
     dw_in = dot_tn(grad_in, normed_all).astype(BF16)
     dw_fg = dot_tn(after(grad_fg, dw_in), normed_all).astype(BF16)
-    last_sum = ring_sum([dw_in, dw_fg], True)
-    dw_fg, first_sum.came, last_sends, moved_far = hold(dw_fg, first_sum.came, last_sum.sends(), moved_far)
+    last_sum = RingScatter(net, [dw_in, dw_fg], True)
+    last_sends, near_own, first_sum.came = hold(last_sum.sends(), near_own, first_sum.came)
+    last_sum.launch(last_sends)
     first_sum.launch(first_sum.sends())
+    near_own, moved = hold(near_own, moved)
+    sums = jnp.stack([jnp.sum(low_sums, axis=(0, 1)), jnp.sum(gain_sums, axis=(0, 1))], 0).reshape(2, n_tp, dq)
+    high = hold(sums.astype(BF16))[0].astype(F32)
+    chan_rows = jnp.concatenate([high, sums - high], 0).transpose(1, 0, 2).reshape(n_tp, 1, 4 * dq)
+    chan_rows = jnp.pad(chan_rows, ((0, 0), (0, 0), (0, cols - 4 * dq)))
+    sent = back_tokens(near_own, moved, tok, grad_resid, in_gain.reshape(1, width), mlp_sum, chan_rows)
+
+    sent, up_own, last_sum.came, first_sum.came = hold(sent, up_own, last_sum.came, first_sum.came)
+    got = to_owner(sent)
+    up_blocks, gate_blocks = net.gather_first(up_own), net.gather_first(after(gate_own, up_own))
+    down_blocks = net.gather_rest([after(down_blocks[0], up_own)] + down_blocks[1:])
+    grad_w_down = to_output(down_blocks, False)
+    sends, last_sends = hold(first_sum.sends(), last_sum.sends())
     last_sum.launch(last_sends)
-    moved = [near_own, moved_far]
-    gu_blocks = net.gather_first(after(gu_own, moved_far))
-    grad_w_down = to_output(down_blocks, False)
-
-    grad_normed = total(moved)
-    x = tok.astype(F32)
-    r_in = lax.rsqrt(jnp.mean(x * x, axis=-1, keepdims=True) + EPS)
-    grad_in_gain = jnp.sum(grad_normed * x * r_in, axis=0)
-    scaled_g = grad_normed * in_gain
-    inner = jnp.sum(x * scaled_g, axis=-1, keepdims=True)
-    grad_tok = grad_resid + r_in * scaled_g - x * r_in**3 * inner / width
-
-    gains = jnp.stack([grad_in_gain, grad_mlp_gain], 0)
-    high = hold(gains.astype(BF16))[0]
-    low = (gains - high.astype(F32)).astype(BF16)
-    extra = jnp.concatenate([high, low, jnp.zeros((12, width), BF16)], 0)
-    sent = jnp.concatenate([grad_tok.astype(BF16), extra], 0).reshape(-1, n_tp, cols).transpose(1, 0, 2)
-    sent, first_sum.came, last_sum.came = hold(sent, first_sum.came, last_sum.came)
-    got = to_owner(sent)
+    first_sum.launch(sends)
+    last_sum.came, first_sum.came, grad_w_down = hold(last_sum.came, first_sum.came, grad_w_down)
+    last_sum.launch(hold(last_sum.sends())[0])
     first_own = first_sum.result()
-    last_own = last_sum.result()
-    first_blocks = net.gather_rest(net.gather_first(first_own))
-    gu_blocks = net.gather_rest(gu_blocks)
-    last_blocks = net.gather_rest(net.gather_first(last_own))
-    grad_w_gate = to_output([b[:fq] for b in gu_blocks], False).T
-    grad_w_up = to_output([b[fq:] for b in gu_blocks], False).T
+    first_blocks = net.gather_first(first_own)
+    grad_w_up = to_output(net.gather_rest(up_blocks), False)
+    grad_w_gate = to_output(net.gather_rest(gate_blocks), False)
+    last_sum.came, grad_w_up, grad_w_gate, got, mixed_got = hold(
+        last_sum.came, grad_w_up, grad_w_gate, got, mixed_got
+    )
+    last_sum.launch(hold(last_sum.sends())[0])
+    grad_w_gate, grad_w_up = grad_w_gate.T, grad_w_up.T
+    first_blocks = net.gather_rest(first_blocks)
     grad_w_out = to_output([b[:dq] for b in first_blocks], False)
     grad_w_og = to_output([b[dq:] for b in first_blocks], True)
+    last_sum.came, grad_w_out, grad_w_og = hold(last_sum.came, grad_w_out, grad_w_og)
+    last_own = last_sum.result()
+    last_blocks = net.gather_rest(net.gather_first(last_own))
     grad_w_in = to_output([b[:dq] for b in last_blocks], True)
     grad_w_fg = to_output([b[dq:] for b in last_blocks], True)
-    mine = jnp.sum(got[:, rows : rows + 4].astype(F32), 0)
-    mine = mine[:2] + mine[2:]
-    sums = jnp.stack([jnp.sum(low_sums, axis=(0, 1)), jnp.sum(gain_sums, axis=(0, 1))], 0).reshape(2, n_tp, dq)
-    for bit in reversed(net.tp_bits):
-        sums = sums.reshape(2, 2, bit, dq)
-        upper = jnp.bitwise_and(t, bit) != 0
-        keep = jnp.where(upper, sums[:, 1], sums[:, 0])
-        send = jnp.where(upper, sums[:, 0], sums[:, 1])
-        sums = keep + net.cross(send, bit)
-    chans = sums.reshape(1, 2, dq)
+    mixed = in_place(mixed_got)
+    sums = jnp.sum(got[:, rows : rows + 5].astype(F32), 0)
+    ends = jnp.concatenate([sums[:2] + sums[2:4], sums[4:5]], 0).reshape(1, 3, cols)
     for bit in net.bits:
-        chans = jnp.concatenate([chans, net.swap(chans, bit)], 0)
-        mine = mine + net.swap(mine, bit)
-    chans = chans[lax.bitwise_xor(s, jnp.arange(n_seq, dtype=jnp.int32))]
+        ends = jnp.concatenate([ends, net.swap(ends, bit)], 0)
+    mine = jnp.sum(ends[:, :2], 0)
+    chans = ends[lax.bitwise_xor(s, jnp.arange(n_seq, dtype=jnp.int32)), 2, : 4 * dq].reshape(n_seq, 2, 2, dq)
+    chans = chans[:, 0] + chans[:, 1]
     return (
-        in_place(mixed_got),
+        mixed,
         in_place(got[:, :rows]).astype(F32),
         mine[0],
         grad_w_in,

time: 1020 us -> 957 us (0.938)
  waiting for transfers between devices: 395 us -> 290 us
  Pallas kernels: 252 us -> 283 us
  starting transfers between devices: 130 us -> 152 us
    ppermute x44 -> x49, waiting for transfers between devices: 142 us -> 48.2 us  [swap(): return lax.ppermute(x, 'seq', [(i, i ^ bit) for i in range(self.seq)])]
    pallas_call x0 -> x4, Pallas kernels: none -> 25.2 us  [whole_kernel(): pl.pallas_call(body, out_shape=outs, in_specs=[VMEM_SPEC] * len(arrays),...]
    ppermute x56 -> x72, starting transfers between devices: 75.9 us -> 99.1 us  [shift(): lax.ppermute(x, 'tp', [(self.cycle[i], self.cycle[(i + k) % n]) for i in...]
    ppermute x56 -> x72, waiting for transfers between devices: 185 us -> 202 us  [shift(): lax.ppermute(x, 'tp', [(self.cycle[i], self.cycle[(i + k) % n]) for i in...]
    all_to_all x4, waiting for transfers between devices: 43.2 us -> 28 us  [to_owner(): return lax.all_to_all(x, 'tp', 0, 0, tiled=True)]
    ppermute x9 -> x6, waiting for transfers between devices: 25.4 us -> 11.2 us  [cross(): return lax.ppermute(x, 'tp', [(i, i ^ bit) for i in range(self.tp)])]
    unnamed x230 -> x214, local copies, waits for them, and re-layouts: 27.8 us -> 21.6 us
    pallas_call x11 -> x12, Pallas kernels: 198 us -> 203 us  [step_kernel(): pl.pallas_call(kernel, grid=(count,), out_shape=[shape for shape, _ in ou...]
  transfers between devices with their start and end apart: 113 -> 131, of which waited for: 46 -> 52; matrix products, arithmetic and copies ran while one was open for 19% -> 18% of each run, Pallas kernels for 21% -> 25%
where the time goes in v3:
time: 957 us; the launch traced here: 944 us
  waiting for transfers between devices  290 us (30%)
  Pallas kernels  283 us (30%)
  starting transfers between devices  152 us (16%)
  other arithmetic  78.7 us (8%)
  local copies, waits for them, and re-layouts  76.4 us (8%)
  matrix products  56.3 us (6%)
    pallas_call x12, Pallas kernels, step_kernel(): pl.pallas_call(kernel, grid=(count,), out_shape=[shape for shape, _ in ou...  203 us
    ppermute x72, waiting for transfers between devices, shift(): lax.ppermute(x, 'tp', [(self.cycle[i], self.cycle[(i + k) % n]) for i in...  202 us
    ppermute x72, starting transfers between devices, shift(): lax.ppermute(x, 'tp', [(self.cycle[i], self.cycle[(i + k) % n]) for i in...  99.1 us
    dot_general x7, matrix products, dot_tn(): lax.dot_general(a, b, (((0,), (0,)), ((), ())), preferred_element_type=F32)  56.3 us
    ppermute x49, waiting for transfers between devices, swap(): return lax.ppermute(x, 'seq', [(i, i ^ bit) for i in range(self.seq)])  48.2 us
    convert_element_type x26, other arithmetic, make(): made.append(whole.astype(BF16))  47.9 us
    all_to_all x4, waiting for transfers between devices, to_owner(): return lax.all_to_all(x, 'tp', 0, 0, tiled=True)  28 us
    pallas_call x4, Pallas kernels, whole_kernel(): pl.pallas_call(body, out_shape=outs, in_specs=[VMEM_SPEC] * len(arrays),...  25.2 us
  transfers between devices with their start and end apart: 131, of which 52 were waited for; matrix products, arithmetic and copies ran while one was open for 18% of the time, Pallas kernels for 25%

profile of v3, /device:TPU:0, one launch (start us, length us, event | category | flops | bytes accessed | tf_op | source)
XLA Modules:
  0.0 944.4 jit_solution(4498160799054918581)
XLA Ops:
  25.2 28.0 %all-to-all-done.in_ref = bf16[8,400,256]{2,1,0:T(8,128)(2,1)} async-done(((bf16[8,400,256]{2,1,0:T(8,128)(2,1)}), bf16[8,400,256]{2,1,0:T(8,128)(2,1)}, u32[]{:S(2)}, u32[]{:S(2)}) %all-to-all-start) | async-done | bytes 1638432 | tf_op jit(solution)/shard_map/all_to_all | solution.py:944
  60.7 20.3 %collective-permute-done.refs_5_.refs_1_.refs_7_ = bf16[256,2048]{1,0:T(8,128)(2,1)S(1)} collective-permute-done((bf16[256,2048]{1,0:T(8,128)(2,1)S(1)}, bf16[256,2048]{1,0:T(8,128)(2,1)S(1)}, u32[]{:S(2)}, u32[]{:S(2)}) %collective-permute-start) | collective-permute-done | bytes 1048608 | tf_op jit(solution)/shard_map/ppermute | solution.py:70
  83.8 20.7 %collective-permute-done.1.refs_6_.refs_2_.refs_8_ = bf16[256,2048]{1,0:T(8,128)(2,1)} collective-permute-done((bf16[256,2048]{1,0:T(8,128)(2,1)S(1)}, bf16[256,2048]{1,0:T(8,128)(2,1)}, u32[]{:S(2)}, u32[]{:S(2)}) %collective-permute-start.1) | collective-permute-done | bytes 1048608 | tf_op jit(solution)/shard_map/ppermute | solution.py:70
  111.5 15.6 %collective-permute-done.2.refs_7_.refs_3_.refs_9_ = bf16[256,2048]{1,0:T(8,128)(2,1)} collective-permute-done((bf16[256,2048]{1,0:T(8,128)(2,1)}, bf16[256,2048]{1,0:T(8,128)(2,1)}, u32[]{:S(2)}, u32[]{:S(2)}) %collective-permute-start.2) | collective-permute-done | bytes 1048608 | tf_op jit(solution)/shard_map/ppermute | solution.py:70
  149.1 24.2 %shard_map.247 = (f32[1536,1536]{1,0:T(8,128)}, bf16[1536,2048]{1,0:T(8,128)(2,1)}, f32[4,3,512]{2,1,0:T(4,128)}, f32[4,3,512]{2,1,0:T(4,128)}) custom-call(s32[8]{0:T(128)} %get-tuple-element.676.order_ref, bf16[384,2048]{1,0:T(8,128)(2,1)} %get-tuple-element.287.refs_0_, bf16[384,2048]{1,0:T(8,128)(2,1)} %collective-permute-done.8.refs_1_, ...), custom_call_target="tpu_custom_call" | custom-call | flops 999999995904 | bytes 1000000000 | tf_op jit(solution)/shard_map/pallas_call | solution.py:424
  195.5 11.5 %shard_map.249 = (f32[1536,512]{1,0:T(8,128)}, bf16[1536,512]{1,0:T(8,128)(2,1)}, f32[1536,128]{1,0:T(8,128)}, bf16[384,2048]{1,0:T(8,128)(2,1)}, bf16[384,2048]{1,0:T(8,128)(2,1)}) custom-call(s32[8]{0:T(128)} %get-tuple-element.676.order_ref, bf16[256,2048]{1,0:T(8,128)(2,1)} %pad_maximum_fusion.3.refs_4_.refs_0_.refs_6_, bf16[256,2048]{1,0:T(8,128)(2,1)} %copy-done.21, ...), custom_call_target="tpu_custom_call" | custom-call | flops 999999995904 | bytes 1000000000 | tf_op jit(solution)/shard_map/pallas_call | solution.py:424
  209.2 11.6 %shard_map.250 = (f32[1536,512]{1,0:T(8,128)}, bf16[1536,512]{1,0:T(8,128)(2,1)}, f32[1536,128]{1,0:T(8,128)}, bf16[384,2048]{1,0:T(8,128)(2,1)}, bf16[384,2048]{1,0:T(8,128)(2,1)}) custom-call(s32[8]{0:T(128)} %get-tuple-element.676.order_ref, ...), custom_call_target="tpu_custom_call", output_to_operand_aliasing={{0}: (14, {}), {1}: (15, {}), {2}: (16, {})} | custom-call | flops 1 | bytes 1 | tf_op jit(solution)/shard_map/pallas_call | solution.py:424
  236.5 11.0 %collective-permute-done.22.refs_13_.refs_11_ = bf16[176,2048]{1,0:T(8,128)(2,1)} collective-permute-done((bf16[176,2048]{1,0:T(8,128)(2,1)}, bf16[176,2048]{1,0:T(8,128)(2,1)}, u32[]{:S(2)}, u32[]{:S(2)}) %collective-permute-start.22) | collective-permute-done | bytes 720928 | tf_op jit(solution)/shard_map/ppermute | solution.py:70
  253.2 14.3 %collective-permute-done.26 = f32[4,384]{1,0:T(4,128)S(1)} collective-permute-done((f32[4,384]{1,0:T(4,128)S(1)}, f32[4,384]{1,0:T(4,128)S(1)}, u32[]{:S(2)}, u32[]{:S(2)}) %collective-permute-start.26) | collective-permute-done | bytes 6176 | tf_op jit(solution)/shard_map/ppermute | solution.py:76
  278.7 14.7 %collective-permute-done.30.refs_14_.refs_12_ = bf16[176,2048]{1,0:T(8,128)(2,1)S(1)} collective-permute-done((bf16[176,2048]{1,0:T(8,128)(2,1)}, bf16[176,2048]{1,0:T(8,128)(2,1)S(1)}, u32[]{:S(2)}, u32[]{:S(2)}) %collective-permute-start.30) | collective-permute-done | bytes 720928 | tf_op jit(solution)/shard_map/ppermute | solution.py:70
  322.0 19.1 %shard_map.252 = (bf16[1536,1408]{1,0:T(8,128)(2,1)}, bf16[1536,1408]{1,0:T(8,128)(2,1)}, bf16[1536,1408]{1,0:T(8,128)(2,1)}, bf16[1536,2048]{1,0:T(8,128)(2,1)}) custom-call(s32[8]{0:T(128)} %get-tuple-element.676.order_ref, bf16[384,2048]{1,0:T(8,128)(2,1)} %get-tuple-element.341.refs_0_, bf16[384,2048]{1,0:T(8,128)(2,1)} %copy-done.83, ...), custom_call_target="tpu_custom_call" | custom-call | flops 999999995904 | bytes 1000000000 | tf_op jit(solution)/shard_map/pallas_call | solution.py:424
  346.0 19.1 %shard_map.253 = (bf16[1536,1408]{1,0:T(8,128)(2,1)}, bf16[1536,1408]{1,0:T(8,128)(2,1)}, bf16[1536,1408]{1,0:T(8,128)(2,1)}, bf16[1536,2048]{1,0:T(8,128)(2,1)}) custom-call(s32[8]{0:T(128)} %get-tuple-element.676.order_ref, ...), custom_call_target="tpu_custom_call", output_to_operand_aliasing={{0}: (21, {}), {1}: (22, {}), {2}: (23, {}), {3}: (24, {})} | custom-call | flops 1 | bytes 1 | tf_op jit(solution)/shard_map/pallas_call | solution.py:424
  388.7 15.8 %collective-permute-done.44.refs_3_ = bf16[176,2048]{1,0:T(8,128)(2,1)S(1)} collective-permute-done((bf16[176,2048]{1,0:T(8,128)(2,1)S(1)}, bf16[176,2048]{1,0:T(8,128)(2,1)S(1)}, u32[]{:S(2)}, u32[]{:S(2)}) %collective-permute-start.44) | collective-permute-done | bytes 720928 | tf_op jit(solution)/shard_map/ppermute | solution.py:70
  442.2 17.5 %shard_map.255 = (bf16[1536,1408]{1,0:T(8,128)(2,1)}, bf16[1536,1408]{1,0:T(8,128)(2,1)}) custom-call(s32[8]{0:T(128)} %get-tuple-element.676.order_ref, bf16[176,2048]{1,0:T(8,128)(2,1)} %constant_dynamic-slice_fusion.32.refs_0_, bf16[176,2048]{1,0:T(8,128)(2,1)} %collective-permute-done.37.refs_1_, bf16[176,2048]{1,0:T(8,128)(2,1)} %copy-done.86, ...), custom_call_target="tpu_custom_call" | custom-call | flops 999999995904 | bytes 1000000000 | tf_op jit(solution)/shard_map/pallas_call | solution.py:424
  464.7 17.7 %shard_map.256 = (bf16[384,2048]{1,0:T(8,128)(2,1)}, bf16[384,2048]{1,0:T(8,128)(2,1)}) custom-call(s32[8]{0:T(128)} %get-tuple-element.676.order_ref, bf16[176,2048]{1,0:T(8,128)(2,1)} %get-tuple-element.292.refs_2_.refs_0_, bf16[176,2048]{1,0:T(8,128)(2,1)} %collective-permute-done.11.refs_3_.refs_1_, ...), custom_call_target="tpu_custom_call" | custom-call | flops 999999995904 | bytes 1000000000 | tf_op jit(solution)/shard_map/pallas_call | solution.py:424
  492.1 17.7 %shard_map.257 = (bf16[384,2048]{1,0:T(8,128)(2,1)}, bf16[384,2048]{1,0:T(8,128)(2,1)}) custom-call(s32[8]{0:T(128)} %get-tuple-element.676.order_ref, bf16[176,2048]{1,0:T(8,128)(2,1)} %get-tuple-element.292.refs_2_.refs_0_, bf16[176,2048]{1,0:T(8,128)(2,1)} %collective-permute-done.11.refs_3_.refs_1_, ...), custom_call_target="tpu_custom_call" | custom-call | flops 999999995904 | bytes 1000000000 | tf_op jit(solution)/shard_map/pallas_call | solution.py:424
  514.7 11.6 %convolution_convert_fusion.1 = bf16[1408,2048]{1,0:T(8,128)(2,1)S(1)} fusion(bf16[1536,1408]{1,0:T(8,128)(2,1)S(1)} %copy-done.91, bf16[1536,2048]{1,0:T(8,128)(2,1)} %get-tuple-element.394), kind=kOutput, calls=%fused_computation.2 | convolution fusion | flops 8861253632 | bytes 16384000 | tf_op jit(solution)/shard_map/dot_general | solution.py:905
  548.8 16.3 %shard_map.259 = (bf16[384,2048]{1,0:T(8,128)(2,1)}, bf16[384,2048]{1,0:T(8,128)(2,1)}, bf16[384,2048]{1,0:T(8,128)(2,1)}, bf16[384,2048]{1,0:T(8,128)(2,1)}) custom-call(s32[8]{0:T(128)} %get-tuple-element.676.order_ref, bf16[176,2048]{1,0:T(8,128)(2,1)} %constant_dynamic-slice_fusion.32.refs_0_, bf16[176,2048]{1,0:T(8,128)(2,1)} %collective-permute-done.37.refs_1_, ...), custom_call_target="tpu_custom_call" | custom-call | flops 999999995904 | bytes 1000000000 | tf_op jit(solution)/shard_map/pallas_call | solution.py:424
  570.2 12.6 %convolution_convert_fusion = bf16[1408,2048]{1,0:T(8,128)(2,1)S(1)} fusion(bf16[1536,1408]{1,0:T(8,128)(2,1)} %get-tuple-element.417.refs_19_, bf16[1536,2048]{1,0:T(8,128)(2,1)} %get-tuple-element.394), kind=kOutput, calls=%fused_computation.1 | convolution fusion | flops 8861253632 | bytes 16384000 | tf_op jit(solution)/shard_map/dot_general | solution.py:905
  604.7 13.8 %shard_map.260 = (f32[1536,512]{1,0:T(8,128)}, bf16[1536,512]{1,0:T(8,128)(2,1)}, bf16[1536,512]{1,0:T(8,128)(2,1)}, bf16[1536,2048]{1,0:T(8,128)(2,1)}, f32[1536,128]{1,0:T(8,128)}, /*index=5*/f32[4,8,512]{2,1,0:T(8,128)}) custom-call(s32[8]{0:T(128)} %get-tuple-element.676.order_ref, bf16[384,2048]{1,0:T(8,128)(2,1)} %get-tuple-element.434.refs_0_, ...), custom_call_target="tpu_custom_call" | custom-call | flops 999999995904 | bytes 1000000000 | tf_op jit(solution)/shard_map/pallas_call | solution.py:424
  686.1 17.6 %shard_map.263 = (bf16[768,512]{1,0:T(8,128)(2,1)}, bf16[768,512]{1,0:T(8,128)(2,1)}, f32[2,8,512]{2,1,0:T(8,128)}, bf16[384,2048]{1,0:T(8,128)(2,1)}, bf16[384,2048]{1,0:T(8,128)(2,1)}) custom-call(s32[8]{0:T(128)} %get-tuple-element.676.order_ref, bf16[256,2048]{1,0:T(8,128)(2,1)} %pad_maximum_fusion.3.refs_4_.refs_0_.refs_6_, ...), custom_call_target="tpu_custom_call" | custom-call | flops 999999995904 | bytes 1000000000 | tf_op jit(solution)/shard_map/pallas_call | solution.py:424
  736.9 17.4 %shard_map.265 = (bf16[768,512]{1,0:T(8,128)(2,1)}, bf16[768,512]{1,0:T(8,128)(2,1)}, f32[2,8,512]{2,1,0:T(8,128)}, bf16[384,2048]{1,0:T(8,128)(2,1)}, bf16[384,2048]{1,0:T(8,128)(2,1)}) custom-call(s32[8]{0:T(128)} %get-tuple-element.676.order_ref, bf16[256,2048]{1,0:T(8,128)(2,1)} %pad_maximum_fusion.3.refs_4_.refs_0_.refs_6_, ...), custom_call_target="tpu_custom_call" | custom-call | flops 999999995904 | bytes 1000000000 | tf_op jit(solution)/shard_map/pallas_call | solution.py:424
  858.4 9.8 %collective-permute-done.122 = bf16[128,2048]{1,0:T(8,128)(2,1)S(1)} collective-permute-done((bf16[128,2048]{1,0:T(8,128)(2,1)S(1)}, bf16[128,2048]{1,0:T(8,128)(2,1)S(1)}, u32[]{:S(2)}, u32[]{:S(2)}) %collective-permute-start.122) | collective-permute-done | bytes 524320 | tf_op jit(solution)/shard_map/ppermute | solution.py:76
  919.5 10.5 %collective-permute-done.125 = bf16[128,2048]{1,0:T(8,128)(2,1)S(1)} collective-permute-done((bf16[128,2048]{1,0:T(8,128)(2,1)S(1)}, bf16[128,2048]{1,0:T(8,128)(2,1)S(1)}, u32[]{:S(2)}, u32[]{:S(2)}) %collective-permute-start.125) | collective-permute-done | bytes 524320 | tf_op jit(solution)/shard_map/ppermute | solution.py:76
  (640 shorter events, 547.7 us)
Async XLA Ops:
  7.4 45.8 %all-to-all-start = ((bf16[8,400,256]{2,1,0:T(8,128)(2,1)}), bf16[8,400,256]{2,1,0:T(8,128)(2,1)}, u32[]{:S(2)}, u32[]{:S(2)}) async-start(bf16[8,400,256]{2,1,0:T(8,128)(2,1)} %pad_maximum_fusion), calls=%async_computation | async-start | bytes 3276800 | tf_op jit(solution)/shard_map/all_to_all | solution.py:944
  59.2 48.0 %collective-permute-start.9 = (bf16[384,2048]{1,0:T(8,128)(2,1)}, bf16[384,2048]{1,0:T(8,128)(2,1)}, u32[]{:S(2)}, u32[]{:S(2)}) collective-permute-start(bf16[384,2048]{1,0:T(8,128)(2,1)} %get-tuple-element.287.refs_0_), channel_id=1, source_target_pairs={{0,16},{8,24},{16,0},{24,8},{1,17},{9,25},{17,1},{25,9},{2,18},{10... | collective-permute-start | bytes 4718600 | tf_op jit(solution)/shard_map/ppermute | solution.py:76
  107.2 41.9 %collective-permute-start.8 = (bf16[384,2048]{1,0:T(8,128)(2,1)}, bf16[384,2048]{1,0:T(8,128)(2,1)}, u32[]{:S(2)}, u32[]{:S(2)}) collective-permute-start(bf16[384,2048]{1,0:T(8,128)(2,1)} %get-tuple-element.287.refs_0_), channel_id=1, source_target_pairs={{0,8},{8,0},{16,24},{24,16},{1,9},{9,1},{17,25},{25,17},{2,10},{10... | collective-permute-start | bytes 4718600 | tf_op jit(solution)/shard_map/ppermute | solution.py:76
  107.2 41.9 %collective-permute-start.10 = (bf16[384,2048]{1,0:T(8,128)(2,1)}, bf16[384,2048]{1,0:T(8,128)(2,1)}, u32[]{:S(2)}, u32[]{:S(2)}) collective-permute-start(bf16[384,2048]{1,0:T(8,128)(2,1)} %collective-permute-done.9.refs_2_), channel_id=1, source_target_pairs={{0,8},{8,0},{16,24},{24,16},{1,9},{9,1},{17,25},{25,17},{2,10},{10... | collective-permute-start | bytes 4718600 | tf_op jit(solution)/shard_map/ppermute | solution.py:76
  144.5 28.7 %collective-permute-start.11 = (bf16[176,2048]{1,0:T(8,128)(2,1)}, bf16[176,2048]{1,0:T(8,128)(2,1)}, u32[]{:S(2)}, u32[]{:S(2)}) collective-permute-start(bf16[176,2048]{1,0:T(8,128)(2,1)} %get-tuple-element.292.refs_2_.refs_0_), channel_id=1, source_target_pairs={{0,2},{2,4},{4,6},{6,7},{7,5},{5,3},{3,1},{1,0},{8,10},{10,12},{12... | collective-permute-start | bytes 2162696 | tf_op jit(solution)/shard_map/ppermute | solution.py:70
  231.3 36.2 %collective-permute-start.24 = (bf16[384,2048]{1,0:T(8,128)(2,1)}, bf16[384,2048]{1,0:T(8,128)(2,1)}, u32[]{:S(2)}, u32[]{:S(2)}) collective-permute-start(bf16[384,2048]{1,0:T(8,128)(2,1)} %add_convert_fusion.7), channel_id=1, source_target_pairs={{0,16},{8,24},{16,0},{24,8},{1,17},{9,25},{17,1},{25,9},{2,18},{10... | collective-permute-start | bytes 4718600 | tf_op jit(solution)/shard_map/ppermute | solution.py:76
  274.6 39.9 %collective-permute-start.29 = (bf16[384,2048]{1,0:T(8,128)(2,1)}, bf16[384,2048]{1,0:T(8,128)(2,1)S(1)}, u32[]{:S(2)}, u32[]{:S(2)}) collective-permute-start(bf16[384,2048]{1,0:T(8,128)(2,1)} %get-tuple-element.341.refs_0_), channel_id=1, source_target_pairs={{0,8},{8,0},{16,24},{24,16},{1,9},{9,1},{17,25},{25,17},{2,10},{10... | collective-permute-start | bytes 4718600 | tf_op jit(solution)/shard_map/ppermute | solution.py:76
  307.6 33.6 %collective-permute-start.36 = (bf16[384,2048]{1,0:T(8,128)(2,1)}, bf16[384,2048]{1,0:T(8,128)(2,1)}, u32[]{:S(2)}, u32[]{:S(2)}) collective-permute-start(bf16[384,2048]{1,0:T(8,128)(2,1)} %get-tuple-element.341.refs_0_), channel_id=1, source_target_pairs={{0,16},{8,24},{16,0},{24,8},{1,17},{9,25},{17,1},{25,9},{2,18},{10... | collective-permute-start | bytes 4718600 | tf_op jit(solution)/shard_map/ppermute | solution.py:76
  317.6 56.9 %all-to-all-start.1 = ((bf16[8,384,256]{2,1,0:T(8,128)(2,1)}), bf16[8,384,256]{2,1,0:T(8,128)(2,1)}, u32[]{:S(2)}, u32[]{:S(2)}) async-start(bf16[8,384,256]{2,1,0:T(8,128)(2,1)} %bitcast.235), calls=%async_computation.1 | async-start | bytes 3145728 | tf_op jit(solution)/shard_map/all_to_all | solution.py:944
  341.2 31.1 %collective-permute-start.40 = (bf16[176,2048]{1,0:T(8,128)(2,1)}, bf16[176,2048]{1,0:T(8,128)(2,1)S(1)}, u32[]{:S(2)}, u32[]{:S(2)}) collective-permute-start(bf16[176,2048]{1,0:T(8,128)(2,1)} %collective-permute-done.37.refs_1_), channel_id=1, source_target_pairs={{0,2},{2,4},{4,6},{6,7},{7,5},{5,3},{3,1},{1,0},{8,10},{10,12},{12... | collective-permute-start | bytes 2162696 | tf_op jit(solution)/shard_map/ppermute | solution.py:70
  343.1 31.4 %collective-permute-start.41 = (bf16[176,2048]{1,0:T(8,128)(2,1)}, bf16[176,2048]{1,0:T(8,128)(2,1)}, u32[]{:S(2)}, u32[]{:S(2)}) collective-permute-start(bf16[176,2048]{1,0:T(8,128)(2,1)} %collective-permute-done.38.refs_8_), channel_id=1, source_target_pairs={{0,1},{2,0},{4,2},{6,4},{7,6},{5,7},{3,5},{1,3},{8,9},{10,8},{12,1... | collective-permute-start | bytes 2162696 | tf_op jit(solution)/shard_map/ppermute | solution.py:70
  377.7 29.1 %collective-permute-start.42 = (bf16[384,2048]{1,0:T(8,128)(2,1)}, bf16[384,2048]{1,0:T(8,128)(2,1)S(1)}, u32[]{:S(2)}, u32[]{:S(2)}) collective-permute-start(bf16[384,2048]{1,0:T(8,128)(2,1)} %shard_map.254.cot_ref), channel_id=1, source_target_pairs={{0,8},{8,0},{16,24},{24,16},{1,9},{9,1},{17,25},{25,17},{2,10},{10... | collective-permute-start | bytes 4718600 | tf_op jit(solution)/shard_map/ppermute | solution.py:76
  377.7 37.0 %collective-permute-start.43 = (bf16[384,2048]{1,0:T(8,128)(2,1)}, bf16[384,2048]{1,0:T(8,128)(2,1)S(1)}, u32[]{:S(2)}, u32[]{:S(2)}) collective-permute-start(bf16[384,2048]{1,0:T(8,128)(2,1)} %shard_map.254.cot_ref), channel_id=1, source_target_pairs={{0,16},{8,24},{16,0},{24,8},{1,17},{9,25},{17,1},{25,9},{2,18},{10... | collective-permute-start | bytes 4718600 | tf_op jit(solution)/shard_map/ppermute | solution.py:76
  491.6 36.9 %collective-permute-start.57 = (bf16[192,2048]{1,0:T(8,128)(2,1)}, bf16[192,2048]{1,0:T(8,128)(2,1)}, u32[]{:S(2)}, u32[]{:S(2)}) collective-permute-start(bf16[192,2048]{1,0:T(8,128)(2,1)} %get-tuple-element.395), channel_id=1, source_target_pairs={{0,16},{8,24},{16,0},{24,8},{1,17},{9,25},{17,1},{25,9},{2,18},{10... | collective-permute-start | bytes 2359304 | tf_op jit(solution)/shard_map/ppermute | solution.py:76
  548.3 38.8 %collective-permute-start.65 = (bf16[192,2048]{1,0:T(8,128)(2,1)}, bf16[192,2048]{1,0:T(8,128)(2,1)}, u32[]{:S(2)}, u32[]{:S(2)}) collective-permute-start(bf16[192,2048]{1,0:T(8,128)(2,1)} %get-tuple-element.418), channel_id=1, source_target_pairs={{0,16},{8,24},{16,0},{24,8},{1,17},{9,25},{17,1},{25,9},{2,18},{10... | collective-permute-start | bytes 2359304 | tf_op jit(solution)/shard_map/ppermute | solution.py:76
  595.4 29.0 %collective-permute-start.76 = (bf16[176,2048]{1,0:T(8,128)(2,1)}, bf16[176,2048]{1,0:T(8,128)(2,1)}, u32[]{:S(2)}, u32[]{:S(2)}) collective-permute-start(bf16[176,2048]{1,0:T(8,128)(2,1)} %add_convert_fusion.18.refs_0_), channel_id=1, source_target_pairs={{0,8},{8,0},{16,24},{24,16},{1,9},{9,1},{17,25},{25,17},{2,10},{10... | collective-permute-start | bytes 2162696 | tf_op jit(solution)/shard_map/ppermute | solution.py:76
  635.1 31.7 %collective-permute-start.82 = (bf16[176,2048]{1,0:T(8,128)(2,1)}, bf16[176,2048]{1,0:T(8,128)(2,1)}, u32[]{:S(2)}, u32[]{:S(2)}) collective-permute-start(bf16[176,2048]{1,0:T(8,128)(2,1)} %get-tuple-element.460), channel_id=1, source_target_pairs={{0,2},{2,4},{4,6},{6,7},{7,5},{5,3},{3,1},{1,0},{8,10},{10,12},{12... | collective-permute-start | bytes 2162696 | tf_op jit(solution)/shard_map/ppermute | solution.py:70
  635.5 31.4 %collective-permute-start.83 = (bf16[176,2048]{1,0:T(8,128)(2,1)}, bf16[176,2048]{1,0:T(8,128)(2,1)}, u32[]{:S(2)}, u32[]{:S(2)}) collective-permute-start(bf16[176,2048]{1,0:T(8,128)(2,1)} %get-tuple-element.461), channel_id=1, source_target_pairs={{0,1},{2,0},{4,2},{6,4},{7,6},{5,7},{3,5},{1,3},{8,9},{10,8},{12,1... | collective-permute-start | bytes 2162696 | tf_op jit(solution)/shard_map/ppermute | solution.py:70
  668.6 35.1 %collective-permute-start.89 = (bf16[384,2048]{1,0:T(8,128)(2,1)}, bf16[384,2048]{1,0:T(8,128)(2,1)}, u32[]{:S(2)}, u32[]{:S(2)}) collective-permute-start(bf16[384,2048]{1,0:T(8,128)(2,1)} %add_convert_fusion.2), channel_id=1, source_target_pairs={{0,16},{8,24},{16,0},{24,8},{1,17},{9,25},{17,1},{25,9},{2,18},{10... | collective-permute-start | bytes 4718600 | tf_op jit(solution)/shard_map/ppermute | solution.py:76
  726.5 30.2 %collective-permute-start.91 = (bf16[192,2048]{1,0:T(8,128)(2,1)}, bf16[192,2048]{1,0:T(8,128)(2,1)}, u32[]{:S(2)}, u32[]{:S(2)}) collective-permute-start(bf16[192,2048]{1,0:T(8,128)(2,1)} %get-tuple-element.490), channel_id=1, source_target_pairs={{0,16},{8,24},{16,0},{24,8},{1,17},{9,25},{17,1},{25,9},{2,18},{10... | collective-permute-start | bytes 2359304 | tf_op jit(solution)/shard_map/ppermute | solution.py:76
  728.0 28.7 %collective-permute-start.94 = (bf16[176,2048]{1,0:T(8,128)(2,1)}, bf16[176,2048]{1,0:T(8,128)(2,1)}, u32[]{:S(2)}, u32[]{:S(2)}) collective-permute-start(bf16[176,2048]{1,0:T(8,128)(2,1)} %get-tuple-element.493), channel_id=1, source_target_pairs={{0,2},{2,4},{4,6},{6,7},{7,5},{5,3},{3,1},{1,0},{8,10},{10,12},{12... | collective-permute-start | bytes 2162696 | tf_op jit(solution)/shard_map/ppermute | solution.py:70
  732.0 114.9 %all-to-all-start.3 = ((bf16[8,384,256]{2,1,0:T(8,128)(2,1)}), bf16[8,384,256]{2,1,0:T(8,128)(2,1)}, u32[]{:S(2)}, u32[]{:S(2)}) async-start(bf16[8,384,256]{2,1,0:T(8,128)(2,1)} %shard_map.264), calls=%async_computation.3 | async-start | bytes 3145728 | tf_op jit(solution)/shard_map/all_to_all | solution.py:944
  756.1 47.9 %collective-permute-start.99 = (bf16[192,2048]{1,0:T(8,128)(2,1)}, bf16[192,2048]{1,0:T(8,128)(2,1)}, u32[]{:S(2)}, u32[]{:S(2)}) collective-permute-start(bf16[192,2048]{1,0:T(8,128)(2,1)} %get-tuple-element.511), channel_id=1, source_target_pairs={{0,16},{8,24},{16,0},{24,8},{1,17},{9,25},{17,1},{25,9},{2,18},{10... | collective-permute-start | bytes 2359304 | tf_op jit(solution)/shard_map/ppermute | solution.py:76
  846.9 46.7 %all-to-all-start.2 = ((bf16[8,400,256]{2,1,0:T(8,128)(2,1)}), bf16[8,400,256]{2,1,0:T(8,128)(2,1)S(1)}, u32[]{:S(2)}, u32[]{:S(2)}) async-start(bf16[8,400,256]{2,1,0:T(8,128)(2,1)} %shard_map.266), calls=%async_computation.2 | async-start | bytes 3276800 | tf_op jit(solution)/shard_map/all_to_all | solution.py:944
  (205 other events, 2955.0 us)

commit v4 on v3

--- a/solution.py
+++ b/solution.py
@@ -389,10 +389,22 @@
 
         @pl.when(j == 0)
         def _():
-            for load in loads + x_loads:
+            first = [x for x, (at, _, _, _) in zip(x_loads, pieces) if at == 0]
+            for load in first + loads + x_loads[len(first) :]:
                 load.start()
-            for load in loads:
-                load.wait()
+
+        left = list(zip(weights.takes, loads))
+
+        def ready(which):
+            now = [x for x in left if x[0][3] == which]
+            for x in now:
+                left.remove(x)
+            if now:
+
+                @pl.when(j == 0)
+                def _():
+                    for _, load in now:
+                        load.wait()
 
         for k in range(n_x):
 
@@ -401,7 +413,9 @@
                 x_loads[k].wait()
 
         x = xs[j] if n_x else None
-        part = body(x, held, in_refs, out_refs)
+        part = body(x, held, in_refs, out_refs, ready)
+        for which in range(n_held):
+            ready(which)
         stores = [pltpu.make_async_copy(kept.at[k % 2], part_refs[k], part_sems.at[k]) for k in range(n_part)]
         for k in range(n_part):
 
@@ -458,10 +472,11 @@
 def mixer_in(order, blocks, weights, bound, slots, pos_n):
     count, (rows, depth), wide = len(blocks), blocks[0].shape, bound.shape[1]
 
-    def body(x, held, ins, outs):
+    def body(x, held, ins, outs, ready):
         pre_ref, all_ref, decay_ref, end_ref = outs
         low = ins[0][...]
         all_ref[...] = x
+        ready(0)
         pre_ref[...] = dot_nt(x, held[0][...])
 
         def one(i, carry):
@@ -517,7 +532,7 @@
     rows = slots * pos_n
     depth = weights.shapes[0][1]
 
-    def body(x, held, ins, outs):
+    def body(x, held, ins, outs, ready):
         pre_ref, bound_ref, gain_ref, head_ref = ins
         state_ref, mix_ref, sum_ref = outs
         low = bound_ref[...]
@@ -539,6 +554,7 @@
         og = pre_ref[:, 2 * wide :]
         mix = (state_ref[...] * gain_ref[...] * (og * fast_sigmoid(og))).astype(BF16)
         mix_ref[...] = mix
+        ready(0)
         return dot_nn(mix, held[0][...]).astype(BF16)
 
     ins = [
@@ -558,9 +574,11 @@
 def feed_forward(order, blocks, weights, first, count, onto=(), long=True):
     (rows, depth), wide = blocks[0].shape, weights.shapes[0][0]
 
-    def body(x, held, ins, outs):
+    def body(x, held, ins, outs, ready):
         hid_ref, slope_ref, act_ref, all_ref = outs
         all_ref[...] = x
+        ready(0)
+        ready(1)
         for at in columns(wide):
             gate = dot_nt(x, held[0][at, :])
             up = dot_nt(x, held[1][at, :])
@@ -579,7 +597,8 @@
     wide, depth = weights.shapes[0]
     count = hidden.shape[0] // rows
 
-    def body(x, held, ins, outs):
+    def body(x, held, ins, outs, ready):
+        ready(0)
         return dot_nn(ins[0][...], held[0][...]).astype(BF16)
 
     return step_kernel(
@@ -591,8 +610,9 @@
     wide, depth = weights.shapes[0]
     count = g.shape[0] // rows
 
-    def body(x, held, ins, outs):
+    def body(x, held, ins, outs, ready):
         g_ref, slope_ref, act_ref = ins
+        ready(0)
         for at in columns(wide):
             hid = dot_nt(g_ref[...], held[0][at, :])
             outs[0][:, at] = (hid * slope_ref[:, at].astype(F32)).astype(BF16)
@@ -607,7 +627,9 @@
 def back_pair(order, a, b, weights, rows, first, count):
     wide, depth = weights.shapes[0]
 
-    def body(x, held, ins, outs):
+    def body(x, held, ins, outs, ready):
+        ready(0)
+        ready(1)
         return (dot_nn(ins[0][...], held[0][...]) + dot_nn(ins[1][...], held[1][...])).astype(BF16)
 
     block = by_block(rows, wide, first)
@@ -619,10 +641,11 @@
 def back_mixer(order, blocks, rows, weights, pre, state, mix, r_mix, gain):
     count, depth, wide = len(blocks), blocks[0][0].shape[1], gain.shape[1]
 
-    def body(x, held, ins, outs):
+    def body(x, held, ins, outs, ready):
         og_ref, state_ref, mix_ref, r_ref, gain_ref = ins
         norm_ref, og_out, mix_out, all_ref, inner_ref, sum_ref = outs
         all_ref[...] = x
+        ready(0)
         mix_out[...] = (mix_ref[...].astype(F32) * r_ref[...]).astype(BF16)
         g = dot_nt(x, held[0][...])
         og, state = og_ref[...], state_ref[...]
@@ -703,7 +726,7 @@
     pairs = pos_n // 16
     depth = weights.shapes[0][1]
 
-    def body(x, held, ins, outs):
+    def body(x, held, ins, outs, ready):
         in_ref, fg_ref, bound_ref, norm_ref, state_ref, og_ref, r_ref, coef_ref, head_ref, tail_ref = ins
         gin_ref, gfg_ref, low_ref = outs
         low = bound_ref[...]
@@ -739,6 +762,7 @@
             return tuple(out)
 
         lax.fori_loop(0, pairs, one, tuple(tail_ref[0, k : k + 1] for k in range(slots)))
+        ready(0)
         part = dot_nn(gin_ref[...], held[0][:wide]) + dot_nn(gfg_ref[...], held[0][wide : 2 * wide])
         return (part + dot_nn(og_ref[...], held[0][2 * wide :])).astype(BF16)
 
@@ -760,19 +784,43 @@
     return step_kernel(body, order, count, rows, [], weights, ins, outs, depth, (), long)
 
 
-def joined(refs):
-    return jnp.concatenate([r[...].astype(F32) for r in refs], 0)
-
-
-def whole_kernel(body, outs, *arrays):
+STEPS = 4
+
+
+def row_kernel(body, outs, ins, scratch=()):
+    def spec(a, kind):
+        if kind == "whole":
+            return pl.BlockSpec(a.shape, lambda i: (0,) * len(a.shape))
+        if kind == "rows":
+            return pl.BlockSpec((a.shape[0] // STEPS,) + a.shape[1:], lambda i: (i, 0))
+        size = a.shape[0] // (STEPS // 2)
+        if kind == "first":
+            return pl.BlockSpec((size,) + a.shape[1:], lambda i: (jnp.minimum(i, STEPS // 2 - 1), 0))
+        return pl.BlockSpec((size,) + a.shape[1:], lambda i: (jnp.maximum(i - STEPS // 2, 0), 0))
+
     return pl.pallas_call(
         body,
-        out_shape=outs,
-        in_specs=[VMEM_SPEC] * len(arrays),
-        out_specs=[VMEM_SPEC] * len(outs),
+        grid=(STEPS,),
+        out_shape=[a for a, _ in outs],
+        in_specs=[spec(*x) for x in ins],
+        out_specs=[spec(*x) for x in outs],
+        scratch_shapes=scratch,
         compiler_params=params(),
         cost_estimate=NO_COST,
-    )(*arrays)
+    )(*[a for a, _ in ins])
+
+
+def half_rows(first_ref, second_ref):
+    early = pl.program_id(0) < STEPS // 2
+    return jnp.where(early, first_ref[...].astype(F32), second_ref[...].astype(F32))
+
+
+def add_to(ref, value):
+    @pl.when(pl.program_id(0) == 0)
+    def _():
+        ref[...] = jnp.zeros_like(ref)
+
+    ref[...] += value
 
 
 def residual(near, moved, tok, r_mix, gain):
@@ -785,67 +833,84 @@
         r = lax.rsqrt(jnp.sum(resid * resid, axis=-1, keepdims=True) / width + EPS)
         out_ref[...] = (resid * r * gain_ref[...]).astype(BF16)
 
-    outs = [shape_of(rows, width), shape_of(rows, width, dtype=BF16)]
-    return whole_kernel(body, outs, near, moved, tok, r_mix, gain)
+    outs = [(shape_of(rows, width), "rows"), (shape_of(rows, width, dtype=BF16), "rows")]
+    ins = [(near, "rows"), (moved, "rows"), (tok, "rows"), (r_mix, "rows"), (gain, "whole")]
+    return row_kernel(body, outs, ins)
 
 
 def back_residual(near, moved, resid, cot, gain):
     rows, width = resid.shape
 
     def body(near_ref, first_ref, second_ref, resid_ref, cot_ref, gain_ref, grad_ref, out_ref, sum_ref):
-        g = near_ref[...].astype(F32) + joined((first_ref, second_ref))
+        g = near_ref[...].astype(F32) + half_rows(first_ref, second_ref)
         resid = resid_ref[...]
         r = lax.rsqrt(jnp.sum(resid * resid, axis=-1, keepdims=True) / width + EPS)
         scaled = resid * r
-        sum_ref[...] = jnp.sum(g * scaled, axis=0, keepdims=True)
+        add_to(sum_ref, jnp.sum(g * scaled, axis=0, keepdims=True))
         g = g * gain_ref[...]
         inner = jnp.sum(resid * g, axis=-1, keepdims=True)
         grad = cot_ref[...].astype(F32) + r * g - resid * (r * r * r * inner / width)
         grad_ref[...] = grad
         out_ref[...] = grad.astype(BF16)
 
-    outs = [shape_of(rows, width), shape_of(rows, width, dtype=BF16), shape_of(1, width)]
-    return whole_kernel(body, outs, near, *moved, resid, cot, gain)
+    outs = [
+        (shape_of(rows, width), "rows"),
+        (shape_of(rows, width, dtype=BF16), "rows"),
+        (shape_of(1, width), "whole"),
+    ]
+    ins = [(near, "rows"), (moved[0], "first"), (moved[1], "second"), (resid, "rows"), (cot, "rows"), (gain, "whole")]
+    return row_kernel(body, outs, ins)
 
 
 def block_output(near, moved, resid, live, count):
     rows, width = resid.shape
-    cols = width // count
+    cols, size = width // count, rows // STEPS
 
     def body(near_ref, moved_ref, resid_ref, live_ref, out_ref):
+        at_rows = pl.ds(pl.multiple_of(pl.program_id(0) * size, size), size)
         for k in range(count):
             at = slice(k * cols, (k + 1) * cols)
             ffn = near_ref[:, at].astype(F32) + moved_ref[:, at].astype(F32)
-            out_ref[k] = (live_ref[...] * (resid_ref[:, at] + ffn)).astype(BF16)
-
-    return whole_kernel(body, [shape_of(count, rows, cols, dtype=BF16)], near, moved, resid, live)[0]
+            out_ref[k, at_rows, :] = (live_ref[...] * (resid_ref[:, at] + ffn)).astype(BF16)
+
+    outs = [(shape_of(count, rows, cols, dtype=BF16), "whole")]
+    ins = [(near, "rows"), (moved, "rows"), (resid, "rows"), (live, "rows")]
+    return row_kernel(body, outs, ins)[0]
 
 
 def back_tokens(near, moved, tok, grad_resid, in_gain, mlp_sum, chan_rows):
     rows, width = tok.shape
     count, _, cols = chan_rows.shape
-
-    def body(near_ref, first_ref, second_ref, tok_ref, grad_ref, gain_ref, mlp_ref, chan_ref, out_ref):
-        g = near_ref[...].astype(F32) + joined((first_ref, second_ref))
+    size = rows // STEPS
+
+    def body(near_ref, first_ref, second_ref, tok_ref, grad_ref, gain_ref, mlp_ref, chan_ref, out_ref, sum_ref):
+        g = near_ref[...].astype(F32) + half_rows(first_ref, second_ref)
         x = tok_ref[...].astype(F32)
         r = lax.rsqrt(jnp.sum(x * x, axis=-1, keepdims=True) / width + EPS)
-        in_sum = jnp.sum(g * x * r, axis=0, keepdims=True)
+        add_to(sum_ref, jnp.sum(g * x * r, axis=0, keepdims=True))
         g = g * gain_ref[...]
         inner = jnp.sum(x * g, axis=-1, keepdims=True)
         grad = (grad_ref[...] + r * g - x * (r * r * r * inner / width)).astype(BF16)
-        place = lax.broadcasted_iota(jnp.int32, (16, cols), 0)
+        at_rows = pl.ds(pl.multiple_of(pl.program_id(0) * size, size), size)
         for k in range(count):
-            at = slice(k * cols, (k + 1) * cols)
-            out_ref[k, :rows, :] = grad[:, at]
-            extra = jnp.zeros((16, cols), F32)
-            for i, total in enumerate((in_sum[:, at], mlp_ref[:, at])):
-                high = total.astype(BF16).astype(F32)
-                extra = jnp.where(place == i, high, jnp.where(place == 2 + i, total - high, extra))
-            extra = jnp.where(place == 4, chan_ref[k], extra)
-            out_ref[k, rows:, :] = extra.astype(BF16)
-
-    outs = [shape_of(count, rows + 16, cols, dtype=BF16)]
-    return whole_kernel(body, outs, near, *moved, tok, grad_resid, in_gain, mlp_sum, chan_rows)[0]
+            out_ref[k, at_rows, :] = grad[:, k * cols : (k + 1) * cols]
+
+        @pl.when(pl.program_id(0) == STEPS - 1)
+        def _():
+            place = lax.broadcasted_iota(jnp.int32, (16, cols), 0)
+            for k in range(count):
+                at = slice(k * cols, (k + 1) * cols)
+                extra = jnp.zeros((16, cols), F32)
+                for i, total in enumerate((sum_ref[:, at], mlp_ref[:, at])):
+                    high = total.astype(BF16).astype(F32)
+                    extra = jnp.where(place == i, high, jnp.where(place == 2 + i, total - high, extra))
+                extra = jnp.where(place == 4, chan_ref[k], extra)
+                out_ref[k, rows:, :] = extra.astype(BF16)
+
+    outs = [(shape_of(count, rows + 16, cols, dtype=BF16), "whole")]
+    ins = [(near, "rows"), (moved[0], "first"), (moved[1], "second"), (tok, "rows"), (grad_resid, "rows")]
+    ins += [(in_gain, "whole"), (mlp_sum, "whole"), (chan_rows, "whole")]
+    return row_kernel(body, outs, ins, [pltpu.VMEM((1, width), F32)])[0]
 
 
 def order_rows(blocks, place):
@@ -1042,10 +1107,11 @@
     down_ring.launch(down_ring.sends())
     mlp_in = net.gather_rest(mlp_in[:half] + [far_first] + mlp_in[half + 1 :])
     hidden, slope_up, act, mlp_all = feed_forward(order, mlp_in[half:], wgu, half, n_seq, some, False)
-    hidden, down_ring.came, cot_blocks = hold(hidden, down_ring.came, cot_blocks)
-    down_ring.launch(down_ring.sends())
+    hidden, cot_blocks = hold(hidden, cot_blocks)
     cot = mask_rows(cot_blocks, live)
     grad_out = net.gather_first(cot)
+    cot, down_ring.came = hold(cot, down_ring.came)
+    down_ring.launch(down_ring.sends())
     grad_out, down_ring.came = hold(grad_out, down_ring.came)
     down_ring.launch(down_ring.sends())
     down_ring.finish()

time: 957 us -> 940 us (0.982)
    ppermute x72, starting transfers between devices: 99.1 us -> 88.6 us  [shift(): lax.ppermute(x, 'tp', [(self.cycle[i], self.cycle[(i + k) % n]) for i in...]
    unnamed x214 -> x216, local copies, waits for them, and re-layouts: 21.6 us -> 21 us
  transfers between devices with their start and end apart: 131 -> 131, of which waited for: 52 -> 53; matrix products, arithmetic and copies ran while one was open for 18% -> 18% of each run, Pallas kernels for 25% -> 25%
where the time goes in v4:
time: 940 us; the launch traced here: 929 us
  waiting for transfers between devices  290 us (31%)
  Pallas kernels  277 us (29%)
  starting transfers between devices  143 us (15%)
  other arithmetic  78.7 us (8%)
  local copies, waits for them, and re-layouts  75.9 us (8%)
  matrix products  56.3 us (6%)
    ppermute x72, waiting for transfers between devices, shift(): lax.ppermute(x, 'tp', [(self.cycle[i], self.cycle[(i + k) % n]) for i in...  203 us
    pallas_call x12, Pallas kernels, step_kernel(): pl.pallas_call(kernel, grid=(count,), out_shape=[shape for shape, _ in ou...  198 us
    ppermute x72, starting transfers between devices, shift(): lax.ppermute(x, 'tp', [(self.cycle[i], self.cycle[(i + k) % n]) for i in...  88.6 us
    dot_general x7, matrix products, dot_tn(): lax.dot_general(a, b, (((0,), (0,)), ((), ())), preferred_element_type=F32)  56.3 us
    convert_element_type x26, other arithmetic, make(): made.append(whole.astype(BF16))  47.9 us
    ppermute x49, waiting for transfers between devices, swap(): return lax.ppermute(x, 'seq', [(i, i ^ bit) for i in range(self.seq)])  43.5 us
    all_to_all x4, waiting for transfers between devices, to_owner(): return lax.all_to_all(x, 'tp', 0, 0, tiled=True)  30.1 us
    ppermute x49, starting transfers between devices, swap(): return lax.ppermute(x, 'seq', [(i, i ^ bit) for i in range(self.seq)])  27.2 us
  transfers between devices with their start and end apart: 131, of which 53 were waited for; matrix products, arithmetic and copies ran while one was open for 18% of the time, Pallas kernels for 25%

profile of v4, /device:TPU:0, one launch (start us, length us, event | category | flops | bytes accessed | tf_op | source)
XLA Modules:
  0.0 929.2 jit_solution(13313546942505931660)
XLA Ops:
  25.2 28.0 %all-to-all-done.in_ref = bf16[8,400,256]{2,1,0:T(8,128)(2,1)} async-done(((bf16[8,400,256]{2,1,0:T(8,128)(2,1)}), bf16[8,400,256]{2,1,0:T(8,128)(2,1)}, u32[]{:S(2)}, u32[]{:S(2)}) %all-to-all-start) | async-done | bytes 1638432 | tf_op jit(solution)/shard_map/all_to_all | solution.py:1009
  60.7 20.3 %collective-permute-done.refs_5_.refs_1_.refs_7_ = bf16[256,2048]{1,0:T(8,128)(2,1)S(1)} collective-permute-done((bf16[256,2048]{1,0:T(8,128)(2,1)S(1)}, bf16[256,2048]{1,0:T(8,128)(2,1)S(1)}, u32[]{:S(2)}, u32[]{:S(2)}) %collective-permute-start) | collective-permute-done | bytes 1048608 | tf_op jit(solution)/shard_map/ppermute | solution.py:70
  83.8 20.7 %collective-permute-done.1.refs_6_.refs_2_.refs_8_ = bf16[256,2048]{1,0:T(8,128)(2,1)} collective-permute-done((bf16[256,2048]{1,0:T(8,128)(2,1)S(1)}, bf16[256,2048]{1,0:T(8,128)(2,1)}, u32[]{:S(2)}, u32[]{:S(2)}) %collective-permute-start.1) | collective-permute-done | bytes 1048608 | tf_op jit(solution)/shard_map/ppermute | solution.py:70
  111.5 15.6 %collective-permute-done.2.refs_7_.refs_3_.refs_9_ = bf16[256,2048]{1,0:T(8,128)(2,1)} collective-permute-done((bf16[256,2048]{1,0:T(8,128)(2,1)}, bf16[256,2048]{1,0:T(8,128)(2,1)}, u32[]{:S(2)}, u32[]{:S(2)}) %collective-permute-start.2) | collective-permute-done | bytes 1048608 | tf_op jit(solution)/shard_map/ppermute | solution.py:70
  149.1 24.6 %shard_map.247 = (f32[1536,1536]{1,0:T(8,128)}, bf16[1536,2048]{1,0:T(8,128)(2,1)}, f32[4,3,512]{2,1,0:T(4,128)}, f32[4,3,512]{2,1,0:T(4,128)}) custom-call(s32[8]{0:T(128)} %get-tuple-element.678.order_ref, bf16[384,2048]{1,0:T(8,128)(2,1)} %get-tuple-element.288.refs_0_, bf16[384,2048]{1,0:T(8,128)(2,1)} %collective-permute-done.8.refs_1_, ...), custom_call_target="tpu_custom_call" | custom-call | flops 999999995904 | bytes 1000000000 | tf_op jit(solution)/shard_map/pallas_call | solution.py:438
  195.5 10.2 %shard_map.249 = (f32[1536,512]{1,0:T(8,128)}, bf16[1536,512]{1,0:T(8,128)(2,1)}, f32[1536,128]{1,0:T(8,128)}, bf16[384,2048]{1,0:T(8,128)(2,1)}, bf16[384,2048]{1,0:T(8,128)(2,1)}) custom-call(s32[8]{0:T(128)} %get-tuple-element.678.order_ref, bf16[256,2048]{1,0:T(8,128)(2,1)} %pad_maximum_fusion.3.refs_4_.refs_0_.refs_6_, bf16[256,2048]{1,0:T(8,128)(2,1)} %copy-done.21, ...), custom_call_target="tpu_custom_call" | custom-call | flops 999999995904 | bytes 1000000000 | tf_op jit(solution)/shard_map/pallas_call | solution.py:438
  208.4 10.3 %shard_map.250 = (f32[1536,512]{1,0:T(8,128)}, bf16[1536,512]{1,0:T(8,128)(2,1)}, f32[1536,128]{1,0:T(8,128)}, bf16[384,2048]{1,0:T(8,128)(2,1)}, bf16[384,2048]{1,0:T(8,128)(2,1)}) custom-call(s32[8]{0:T(128)} %get-tuple-element.678.order_ref, ...), custom_call_target="tpu_custom_call", output_to_operand_aliasing={{0}: (14, {}), {1}: (15, {}), {2}: (16, {})} | custom-call | flops 1 | bytes 1 | tf_op jit(solution)/shard_map/pallas_call | solution.py:438
  235.6 11.2 %collective-permute-done.22.refs_13_.refs_11_ = bf16[176,2048]{1,0:T(8,128)(2,1)} collective-permute-done((bf16[176,2048]{1,0:T(8,128)(2,1)}, bf16[176,2048]{1,0:T(8,128)(2,1)}, u32[]{:S(2)}, u32[]{:S(2)}) %collective-permute-start.22) | collective-permute-done | bytes 720928 | tf_op jit(solution)/shard_map/ppermute | solution.py:70
  252.2 14.3 %collective-permute-done.26 = f32[4,384]{1,0:T(4,128)S(1)} collective-permute-done((f32[4,384]{1,0:T(4,128)S(1)}, f32[4,384]{1,0:T(4,128)S(1)}, u32[]{:S(2)}, u32[]{:S(2)}) %collective-permute-start.26) | collective-permute-done | bytes 6176 | tf_op jit(solution)/shard_map/ppermute | solution.py:76
  277.6 14.6 %collective-permute-done.30.refs_14_.refs_12_ = bf16[176,2048]{1,0:T(8,128)(2,1)S(1)} collective-permute-done((bf16[176,2048]{1,0:T(8,128)(2,1)}, bf16[176,2048]{1,0:T(8,128)(2,1)S(1)}, u32[]{:S(2)}, u32[]{:S(2)}) %collective-permute-start.30) | collective-permute-done | bytes 720928 | tf_op jit(solution)/shard_map/ppermute | solution.py:70
  320.9 19.5 %shard_map.252 = (bf16[1536,1408]{1,0:T(8,128)(2,1)}, bf16[1536,1408]{1,0:T(8,128)(2,1)}, bf16[1536,1408]{1,0:T(8,128)(2,1)}, bf16[1536,2048]{1,0:T(8,128)(2,1)}) custom-call(s32[8]{0:T(128)} %get-tuple-element.678.order_ref, bf16[384,2048]{1,0:T(8,128)(2,1)} %get-tuple-element.342.refs_0_, bf16[384,2048]{1,0:T(8,128)(2,1)} %copy-done.83, ...), custom_call_target="tpu_custom_call" | custom-call | flops 999999995904 | bytes 1000000000 | tf_op jit(solution)/shard_map/pallas_call | solution.py:438
  345.3 19.4 %shard_map.253 = (bf16[1536,1408]{1,0:T(8,128)(2,1)}, bf16[1536,1408]{1,0:T(8,128)(2,1)}, bf16[1536,1408]{1,0:T(8,128)(2,1)}, bf16[1536,2048]{1,0:T(8,128)(2,1)}) custom-call(s32[8]{0:T(128)} %get-tuple-element.678.order_ref, ...), custom_call_target="tpu_custom_call", output_to_operand_aliasing={{0}: (21, {}), {1}: (22, {}), {2}: (23, {}), {3}: (24, {})} | custom-call | flops 1 | bytes 1 | tf_op jit(solution)/shard_map/pallas_call | solution.py:438
  373.4 16.5 %collective-permute-done.42.refs_2_ = bf16[176,2048]{1,0:T(8,128)(2,1)S(1)} collective-permute-done((bf16[176,2048]{1,0:T(8,128)(2,1)}, bf16[176,2048]{1,0:T(8,128)(2,1)S(1)}, u32[]{:S(2)}, u32[]{:S(2)}) %collective-permute-start.42) | collective-permute-done | bytes 720928 | tf_op jit(solution)/shard_map/ppermute | solution.py:70
  391.9 15.4 %collective-permute-done.44.refs_3_ = bf16[176,2048]{1,0:T(8,128)(2,1)S(1)} collective-permute-done((bf16[176,2048]{1,0:T(8,128)(2,1)S(1)}, bf16[176,2048]{1,0:T(8,128)(2,1)S(1)}, u32[]{:S(2)}, u32[]{:S(2)}) %collective-permute-start.44) | collective-permute-done | bytes 720928 | tf_op jit(solution)/shard_map/ppermute | solution.py:70
  428.2 17.5 %shard_map.255 = (bf16[1536,1408]{1,0:T(8,128)(2,1)}, bf16[1536,1408]{1,0:T(8,128)(2,1)}) custom-call(s32[8]{0:T(128)} %get-tuple-element.678.order_ref, bf16[176,2048]{1,0:T(8,128)(2,1)} %constant_dynamic-slice_fusion.32.refs_0_, bf16[176,2048]{1,0:T(8,128)(2,1)} %collective-permute-done.37.refs_1_, bf16[176,2048]{1,0:T(8,128)(2,1)} %copy-done.86, ...), custom_call_target="tpu_custom_call" | custom-call | flops 999999995904 | bytes 1000000000 | tf_op jit(solution)/shard_map/pallas_call | solution.py:438
  451.1 17.7 %shard_map.256 = (bf16[384,2048]{1,0:T(8,128)(2,1)}, bf16[384,2048]{1,0:T(8,128)(2,1)}) custom-call(s32[8]{0:T(128)} %get-tuple-element.678.order_ref, bf16[176,2048]{1,0:T(8,128)(2,1)} %get-tuple-element.293.refs_2_.refs_0_, bf16[176,2048]{1,0:T(8,128)(2,1)} %collective-permute-done.11.refs_3_.refs_1_, ...), custom_call_target="tpu_custom_call" | custom-call | flops 999999995904 | bytes 1000000000 | tf_op jit(solution)/shard_map/pallas_call | solution.py:438
  478.5 17.7 %shard_map.257 = (bf16[384,2048]{1,0:T(8,128)(2,1)}, bf16[384,2048]{1,0:T(8,128)(2,1)}) custom-call(s32[8]{0:T(128)} %get-tuple-element.678.order_ref, bf16[176,2048]{1,0:T(8,128)(2,1)} %get-tuple-element.293.refs_2_.refs_0_, bf16[176,2048]{1,0:T(8,128)(2,1)} %collective-permute-done.11.refs_3_.refs_1_, ...), custom_call_target="tpu_custom_call" | custom-call | flops 999999995904 | bytes 1000000000 | tf_op jit(solution)/shard_map/pallas_call | solution.py:438
  501.0 11.6 %convolution_convert_fusion.1 = bf16[1408,2048]{1,0:T(8,128)(2,1)S(1)} fusion(bf16[1536,1408]{1,0:T(8,128)(2,1)S(1)} %copy-done.92, bf16[1536,2048]{1,0:T(8,128)(2,1)} %get-tuple-element.395), kind=kOutput, calls=%fused_computation.2 | convolution fusion | flops 8861253632 | bytes 16384000 | tf_op jit(solution)/shard_map/dot_general | solution.py:970
  534.4 16.3 %shard_map.259 = (bf16[384,2048]{1,0:T(8,128)(2,1)}, bf16[384,2048]{1,0:T(8,128)(2,1)}, bf16[384,2048]{1,0:T(8,128)(2,1)}, bf16[384,2048]{1,0:T(8,128)(2,1)}) custom-call(s32[8]{0:T(128)} %get-tuple-element.678.order_ref, bf16[176,2048]{1,0:T(8,128)(2,1)} %constant_dynamic-slice_fusion.32.refs_0_, bf16[176,2048]{1,0:T(8,128)(2,1)} %collective-permute-done.37.refs_1_, ...), custom_call_target="tpu_custom_call" | custom-call | flops 999999995904 | bytes 1000000000 | tf_op jit(solution)/shard_map/pallas_call | solution.py:438
  555.6 12.6 %convolution_convert_fusion = bf16[1408,2048]{1,0:T(8,128)(2,1)S(1)} fusion(bf16[1536,1408]{1,0:T(8,128)(2,1)} %get-tuple-element.419.refs_19_, bf16[1536,2048]{1,0:T(8,128)(2,1)} %get-tuple-element.395), kind=kOutput, calls=%fused_computation.1 | convolution fusion | flops 8861253632 | bytes 16384000 | tf_op jit(solution)/shard_map/dot_general | solution.py:970
  590.0 13.8 %shard_map.260 = (f32[1536,512]{1,0:T(8,128)}, bf16[1536,512]{1,0:T(8,128)(2,1)}, bf16[1536,512]{1,0:T(8,128)(2,1)}, bf16[1536,2048]{1,0:T(8,128)(2,1)}, f32[1536,128]{1,0:T(8,128)}, /*index=5*/f32[4,8,512]{2,1,0:T(8,128)}) custom-call(s32[8]{0:T(128)} %get-tuple-element.678.order_ref, bf16[384,2048]{1,0:T(8,128)(2,1)} %get-tuple-element.436.refs_0_, ...), custom_call_target="tpu_custom_call" | custom-call | flops 999999995904 | bytes 1000000000 | tf_op jit(solution)/shard_map/pallas_call | solution.py:438
  672.6 15.7 %shard_map.263 = (bf16[768,512]{1,0:T(8,128)(2,1)}, bf16[768,512]{1,0:T(8,128)(2,1)}, f32[2,8,512]{2,1,0:T(8,128)}, bf16[384,2048]{1,0:T(8,128)(2,1)}, bf16[384,2048]{1,0:T(8,128)(2,1)}) custom-call(s32[8]{0:T(128)} %get-tuple-element.678.order_ref, bf16[256,2048]{1,0:T(8,128)(2,1)} %pad_maximum_fusion.3.refs_4_.refs_0_.refs_6_, ...), custom_call_target="tpu_custom_call" | custom-call | flops 999999995904 | bytes 1000000000 | tf_op jit(solution)/shard_map/pallas_call | solution.py:438
  722.4 15.4 %shard_map.265 = (bf16[768,512]{1,0:T(8,128)(2,1)}, bf16[768,512]{1,0:T(8,128)(2,1)}, f32[2,8,512]{2,1,0:T(8,128)}, bf16[384,2048]{1,0:T(8,128)(2,1)}, bf16[384,2048]{1,0:T(8,128)(2,1)}) custom-call(s32[8]{0:T(128)} %get-tuple-element.678.order_ref, bf16[256,2048]{1,0:T(8,128)(2,1)} %pad_maximum_fusion.3.refs_4_.refs_0_.refs_6_, ...), custom_call_target="tpu_custom_call" | custom-call | flops 999999995904 | bytes 1000000000 | tf_op jit(solution)/shard_map/pallas_call | solution.py:438
  843.9 9.8 %collective-permute-done.122 = bf16[128,2048]{1,0:T(8,128)(2,1)S(1)} collective-permute-done((bf16[128,2048]{1,0:T(8,128)(2,1)S(1)}, bf16[128,2048]{1,0:T(8,128)(2,1)S(1)}, u32[]{:S(2)}, u32[]{:S(2)}) %collective-permute-start.122) | collective-permute-done | bytes 524320 | tf_op jit(solution)/shard_map/ppermute | solution.py:76
  (642 shorter events, 532.7 us)
Async XLA Ops:
  7.4 45.8 %all-to-all-start = ((bf16[8,400,256]{2,1,0:T(8,128)(2,1)}), bf16[8,400,256]{2,1,0:T(8,128)(2,1)}, u32[]{:S(2)}, u32[]{:S(2)}) async-start(bf16[8,400,256]{2,1,0:T(8,128)(2,1)} %pad_maximum_fusion), calls=%async_computation | async-start | bytes 3276800 | tf_op jit(solution)/shard_map/all_to_all | solution.py:1009
  59.2 48.0 %collective-permute-start.9 = (bf16[384,2048]{1,0:T(8,128)(2,1)}, bf16[384,2048]{1,0:T(8,128)(2,1)}, u32[]{:S(2)}, u32[]{:S(2)}) collective-permute-start(bf16[384,2048]{1,0:T(8,128)(2,1)} %get-tuple-element.288.refs_0_), channel_id=1, source_target_pairs={{0,16},{8,24},{16,0},{24,8},{1,17},{9,25},{17,1},{25,9},{2,18},{10... | collective-permute-start | bytes 4718600 | tf_op jit(solution)/shard_map/ppermute | solution.py:76
  107.2 41.9 %collective-permute-start.8 = (bf16[384,2048]{1,0:T(8,128)(2,1)}, bf16[384,2048]{1,0:T(8,128)(2,1)}, u32[]{:S(2)}, u32[]{:S(2)}) collective-permute-start(bf16[384,2048]{1,0:T(8,128)(2,1)} %get-tuple-element.288.refs_0_), channel_id=1, source_target_pairs={{0,8},{8,0},{16,24},{24,16},{1,9},{9,1},{17,25},{25,17},{2,10},{10... | collective-permute-start | bytes 4718600 | tf_op jit(solution)/shard_map/ppermute | solution.py:76
  107.2 41.9 %collective-permute-start.10 = (bf16[384,2048]{1,0:T(8,128)(2,1)}, bf16[384,2048]{1,0:T(8,128)(2,1)}, u32[]{:S(2)}, u32[]{:S(2)}) collective-permute-start(bf16[384,2048]{1,0:T(8,128)(2,1)} %collective-permute-done.9.refs_2_), channel_id=1, source_target_pairs={{0,8},{8,0},{16,24},{24,16},{1,9},{9,1},{17,25},{25,17},{2,10},{10... | collective-permute-start | bytes 4718600 | tf_op jit(solution)/shard_map/ppermute | solution.py:76
  144.5 29.1 %collective-permute-start.11 = (bf16[176,2048]{1,0:T(8,128)(2,1)}, bf16[176,2048]{1,0:T(8,128)(2,1)}, u32[]{:S(2)}, u32[]{:S(2)}) collective-permute-start(bf16[176,2048]{1,0:T(8,128)(2,1)} %get-tuple-element.293.refs_2_.refs_0_), channel_id=1, source_target_pairs={{0,2},{2,4},{4,6},{6,7},{7,5},{5,3},{3,1},{1,0},{8,10},{10,12},{12... | collective-permute-start | bytes 2162696 | tf_op jit(solution)/shard_map/ppermute | solution.py:70
  230.3 36.2 %collective-permute-start.24 = (bf16[384,2048]{1,0:T(8,128)(2,1)}, bf16[384,2048]{1,0:T(8,128)(2,1)}, u32[]{:S(2)}, u32[]{:S(2)}) collective-permute-start(bf16[384,2048]{1,0:T(8,128)(2,1)} %add_convert_fusion.7), channel_id=1, source_target_pairs={{0,16},{8,24},{16,0},{24,8},{1,17},{9,25},{17,1},{25,9},{2,18},{10... | collective-permute-start | bytes 4718600 | tf_op jit(solution)/shard_map/ppermute | solution.py:76
  273.5 39.8 %collective-permute-start.29 = (bf16[384,2048]{1,0:T(8,128)(2,1)}, bf16[384,2048]{1,0:T(8,128)(2,1)S(1)}, u32[]{:S(2)}, u32[]{:S(2)}) collective-permute-start(bf16[384,2048]{1,0:T(8,128)(2,1)} %get-tuple-element.342.refs_0_), channel_id=1, source_target_pairs={{0,8},{8,0},{16,24},{24,16},{1,9},{9,1},{17,25},{25,17},{2,10},{10... | collective-permute-start | bytes 4718600 | tf_op jit(solution)/shard_map/ppermute | solution.py:76
  306.5 33.9 %collective-permute-start.36 = (bf16[384,2048]{1,0:T(8,128)(2,1)}, bf16[384,2048]{1,0:T(8,128)(2,1)}, u32[]{:S(2)}, u32[]{:S(2)}) collective-permute-start(bf16[384,2048]{1,0:T(8,128)(2,1)} %get-tuple-element.342.refs_0_), channel_id=1, source_target_pairs={{0,16},{8,24},{16,0},{24,8},{1,17},{9,25},{17,1},{25,9},{2,18},{10... | collective-permute-start | bytes 4718600 | tf_op jit(solution)/shard_map/ppermute | solution.py:76
  316.4 50.3 %all-to-all-start.1 = ((bf16[8,384,256]{2,1,0:T(8,128)(2,1)}), bf16[8,384,256]{2,1,0:T(8,128)(2,1)}, u32[]{:S(2)}, u32[]{:S(2)}) async-start(bf16[8,384,256]{2,1,0:T(8,128)(2,1)} %bitcast.235), calls=%async_computation.1 | async-start | bytes 3145728 | tf_op jit(solution)/shard_map/all_to_all | solution.py:1009
  369.9 37.8 %collective-permute-start.40 = (bf16[384,2048]{1,0:T(8,128)(2,1)}, bf16[384,2048]{1,0:T(8,128)(2,1)S(1)}, u32[]{:S(2)}, u32[]{:S(2)}) collective-permute-start(bf16[384,2048]{1,0:T(8,128)(2,1)} %shard_map.254.cot_ref), channel_id=1, source_target_pairs={{0,8},{8,0},{16,24},{24,16},{1,9},{9,1},{17,25},{25,17},{2,10},{10... | collective-permute-start | bytes 4718600 | tf_op jit(solution)/shard_map/ppermute | solution.py:76
  369.9 37.8 %collective-permute-start.41 = (bf16[384,2048]{1,0:T(8,128)(2,1)}, bf16[384,2048]{1,0:T(8,128)(2,1)S(1)}, u32[]{:S(2)}, u32[]{:S(2)}) collective-permute-start(bf16[384,2048]{1,0:T(8,128)(2,1)} %shard_map.254.cot_ref), channel_id=1, source_target_pairs={{0,16},{8,24},{16,0},{24,8},{1,17},{9,25},{17,1},{25,9},{2,18},{10... | collective-permute-start | bytes 4718600 | tf_op jit(solution)/shard_map/ppermute | solution.py:76
  477.0 37.9 %collective-permute-start.57 = (bf16[192,2048]{1,0:T(8,128)(2,1)}, bf16[192,2048]{1,0:T(8,128)(2,1)}, u32[]{:S(2)}, u32[]{:S(2)}) collective-permute-start(bf16[192,2048]{1,0:T(8,128)(2,1)} %get-tuple-element.396), channel_id=1, source_target_pairs={{0,16},{8,24},{16,0},{24,8},{1,17},{9,25},{17,1},{25,9},{2,18},{10... | collective-permute-start | bytes 2359304 | tf_op jit(solution)/shard_map/ppermute | solution.py:76
  532.9 39.7 %collective-permute-start.65 = (bf16[192,2048]{1,0:T(8,128)(2,1)}, bf16[192,2048]{1,0:T(8,128)(2,1)}, u32[]{:S(2)}, u32[]{:S(2)}) collective-permute-start(bf16[192,2048]{1,0:T(8,128)(2,1)} %get-tuple-element.420), channel_id=1, source_target_pairs={{0,16},{8,24},{16,0},{24,8},{1,17},{9,25},{17,1},{25,9},{2,18},{10... | collective-permute-start | bytes 2359304 | tf_op jit(solution)/shard_map/ppermute | solution.py:76
  581.9 28.5 %collective-permute-start.76 = (bf16[176,2048]{1,0:T(8,128)(2,1)}, bf16[176,2048]{1,0:T(8,128)(2,1)}, u32[]{:S(2)}, u32[]{:S(2)}) collective-permute-start(bf16[176,2048]{1,0:T(8,128)(2,1)} %add_convert_fusion.18.refs_0_), channel_id=1, source_target_pairs={{0,8},{8,0},{16,24},{24,16},{1,9},{9,1},{17,25},{25,17},{2,10},{10... | collective-permute-start | bytes 2162696 | tf_op jit(solution)/shard_map/ppermute | solution.py:76
  582.1 28.3 %collective-permute-start.77 = (bf16[176,2048]{1,0:T(8,128)(2,1)}, bf16[176,2048]{1,0:T(8,128)(2,1)}, u32[]{:S(2)}, u32[]{:S(2)}) collective-permute-start(bf16[176,2048]{1,0:T(8,128)(2,1)} %add_convert_fusion.18.refs_0_), channel_id=1, source_target_pairs={{0,16},{8,24},{16,0},{24,8},{1,17},{9,25},{17,1},{25,9},{2,18},{10... | collective-permute-start | bytes 2162696 | tf_op jit(solution)/shard_map/ppermute | solution.py:76
  622.1 31.7 %collective-permute-start.82 = (bf16[176,2048]{1,0:T(8,128)(2,1)}, bf16[176,2048]{1,0:T(8,128)(2,1)}, u32[]{:S(2)}, u32[]{:S(2)}) collective-permute-start(bf16[176,2048]{1,0:T(8,128)(2,1)} %get-tuple-element.462), channel_id=1, source_target_pairs={{0,2},{2,4},{4,6},{6,7},{7,5},{5,3},{3,1},{1,0},{8,10},{10,12},{12... | collective-permute-start | bytes 2162696 | tf_op jit(solution)/shard_map/ppermute | solution.py:70
  623.1 31.4 %collective-permute-start.83 = (bf16[176,2048]{1,0:T(8,128)(2,1)}, bf16[176,2048]{1,0:T(8,128)(2,1)}, u32[]{:S(2)}, u32[]{:S(2)}) collective-permute-start(bf16[176,2048]{1,0:T(8,128)(2,1)} %get-tuple-element.463), channel_id=1, source_target_pairs={{0,1},{2,0},{4,2},{6,4},{7,6},{5,7},{3,5},{1,3},{8,9},{10,8},{12,1... | collective-permute-start | bytes 2162696 | tf_op jit(solution)/shard_map/ppermute | solution.py:70
  655.6 35.0 %collective-permute-start.89 = (bf16[384,2048]{1,0:T(8,128)(2,1)}, bf16[384,2048]{1,0:T(8,128)(2,1)}, u32[]{:S(2)}, u32[]{:S(2)}) collective-permute-start(bf16[384,2048]{1,0:T(8,128)(2,1)} %add_convert_fusion.2), channel_id=1, source_target_pairs={{0,16},{8,24},{16,0},{24,8},{1,17},{9,25},{17,1},{25,9},{2,18},{10... | collective-permute-start | bytes 4718600 | tf_op jit(solution)/shard_map/ppermute | solution.py:76
  713.3 29.4 %collective-permute-start.91 = (bf16[192,2048]{1,0:T(8,128)(2,1)}, bf16[192,2048]{1,0:T(8,128)(2,1)}, u32[]{:S(2)}, u32[]{:S(2)}) collective-permute-start(bf16[192,2048]{1,0:T(8,128)(2,1)} %get-tuple-element.492), channel_id=1, source_target_pairs={{0,16},{8,24},{16,0},{24,8},{1,17},{9,25},{17,1},{25,9},{2,18},{10... | collective-permute-start | bytes 2359304 | tf_op jit(solution)/shard_map/ppermute | solution.py:76
  713.8 28.9 %collective-permute-start.94 = (bf16[176,2048]{1,0:T(8,128)(2,1)}, bf16[176,2048]{1,0:T(8,128)(2,1)}, u32[]{:S(2)}, u32[]{:S(2)}) collective-permute-start(bf16[176,2048]{1,0:T(8,128)(2,1)} %get-tuple-element.495), channel_id=1, source_target_pairs={{0,2},{2,4},{4,6},{6,7},{7,5},{5,3},{3,1},{1,0},{8,10},{10,12},{12... | collective-permute-start | bytes 2162696 | tf_op jit(solution)/shard_map/ppermute | solution.py:70
  714.6 28.2 %collective-permute-start.95 = (bf16[176,2048]{1,0:T(8,128)(2,1)}, bf16[176,2048]{1,0:T(8,128)(2,1)}, u32[]{:S(2)}, u32[]{:S(2)}) collective-permute-start(bf16[176,2048]{1,0:T(8,128)(2,1)} %get-tuple-element.496), channel_id=1, source_target_pairs={{0,1},{2,0},{4,2},{6,4},{7,6},{5,7},{3,5},{1,3},{8,9},{10,8},{12,1... | collective-permute-start | bytes 2162696 | tf_op jit(solution)/shard_map/ppermute | solution.py:70
  717.9 113.9 %all-to-all-start.3 = ((bf16[8,384,256]{2,1,0:T(8,128)(2,1)}), bf16[8,384,256]{2,1,0:T(8,128)(2,1)}, u32[]{:S(2)}, u32[]{:S(2)}) async-start(bf16[8,384,256]{2,1,0:T(8,128)(2,1)} %shard_map.264), calls=%async_computation.3 | async-start | bytes 3145728 | tf_op jit(solution)/shard_map/all_to_all | solution.py:1009
  739.5 49.3 %collective-permute-start.99 = (bf16[192,2048]{1,0:T(8,128)(2,1)}, bf16[192,2048]{1,0:T(8,128)(2,1)}, u32[]{:S(2)}, u32[]{:S(2)}) collective-permute-start(bf16[192,2048]{1,0:T(8,128)(2,1)} %get-tuple-element.513), channel_id=1, source_target_pairs={{0,16},{8,24},{16,0},{24,8},{1,17},{9,25},{17,1},{25,9},{2,18},{10... | collective-permute-start | bytes 2359304 | tf_op jit(solution)/shard_map/ppermute | solution.py:76
  831.8 47.4 %all-to-all-start.2 = ((bf16[8,400,256]{2,1,0:T(8,128)(2,1)}), bf16[8,400,256]{2,1,0:T(8,128)(2,1)S(1)}, u32[]{:S(2)}, u32[]{:S(2)}) async-start(bf16[8,400,256]{2,1,0:T(8,128)(2,1)} %shard_map.266), calls=%async_computation.2 | async-start | bytes 3276800 | tf_op jit(solution)/shard_map/all_to_all | solution.py:1009
  (206 other events, 2915.8 us)

commit v5 on v4

--- a/solution.py
+++ b/solution.py
@@ -1189,8 +1189,10 @@
     back_end, gate_sum.came, up_sum.came, dw_og = hold(back_end, gate_sum.came, up_sum.came, dw_og)
     tail = scan_heads(place, *spread((decay, back_end), True), True)
     gate_own = gate_sum.result()
-    tail, up_sends, gate_own = hold(tail, up_sum.sends(), gate_own)
+    first_sum = RingScatter(net, [dw_out, dw_og], True)
+    tail, up_sends, sends, gate_own = hold(tail, up_sum.sends(), first_sum.sends(), gate_own)
     up_sum.launch(up_sends)
+    first_sum.launch(sends)
 
     def back(start, tail, long):
         return back_states(
@@ -1198,8 +1200,7 @@
         )
 
     (far_in, far_fg, far_low), far = back(half, tail, True)
-    far, far_in, up_sum.came, ffn = hold(far, far_in, up_sum.came, ffn)
-    first_sum = RingScatter(net, [dw_out, dw_og], True)
+    far, far_in, up_sum.came, first_sum.came, ffn = hold(far, far_in, up_sum.came, first_sum.came, ffn)
     mixed_sent = block_output(*ffn, resid, live, n_tp)
     sent, tail, up_sends, sends, mixed_sent = hold(
         net.halved(net.quad_far_part(far)), tail, up_sum.sends(), first_sum.sends(), mixed_sent

time: 940 us -> 939 us (level)
    unnamed x216 -> x214, local copies, waits for them, and re-layouts: 21 us -> 22 us
  transfers between devices with their start and end apart: 131 -> 131, of which waited for: 53 -> 55; matrix products, arithmetic and copies ran while one was open for 18% -> 18% of each run, Pallas kernels for 25% -> 25%
where the time goes in v5:
time: 939 us; the launch traced here: 928 us
  waiting for transfers between devices  295 us (31%)
  Pallas kernels  277 us (29%)
  starting transfers between devices  139 us (15%)
  other arithmetic  79.2 us (8%)
  local copies, waits for them, and re-layouts  75.3 us (8%)
  matrix products  54.3 us (6%)
    ppermute x72, waiting for transfers between devices, shift(): lax.ppermute(x, 'tp', [(self.cycle[i], self.cycle[(i + k) % n]) for i in...  202 us
    pallas_call x12, Pallas kernels, step_kernel(): pl.pallas_call(kernel, grid=(count,), out_shape=[shape for shape, _ in ou...  198 us
    ppermute x72, starting transfers between devices, shift(): lax.ppermute(x, 'tp', [(self.cycle[i], self.cycle[(i + k) % n]) for i in...  84.6 us
    dot_general x7, matrix products, dot_tn(): lax.dot_general(a, b, (((0,), (0,)), ((), ())), preferred_element_type=F32)  54.3 us
    ppermute x49, waiting for transfers between devices, swap(): return lax.ppermute(x, 'seq', [(i, i ^ bit) for i in range(self.seq)])  50.4 us
    convert_element_type x26, other arithmetic, make(): made.append(whole.astype(BF16))  48.4 us
    all_to_all x4, waiting for transfers between devices, to_owner(): return lax.all_to_all(x, 'tp', 0, 0, tiled=True)  30.1 us
    ppermute x49, starting transfers between devices, swap(): return lax.ppermute(x, 'seq', [(i, i ^ bit) for i in range(self.seq)])  26.1 us
  transfers between devices with their start and end apart: 131, of which 55 were waited for; matrix products, arithmetic and copies ran while one was open for 18% of the time, Pallas kernels for 25%

profile of v5, /device:TPU:0, one launch (start us, length us, event | category | flops | bytes accessed | tf_op | source)
XLA Modules:
  0.0 927.6 jit_solution(7988810329909712220)
XLA Ops:
  25.2 28.0 %all-to-all-done.in_ref = bf16[8,400,256]{2,1,0:T(8,128)(2,1)} async-done(((bf16[8,400,256]{2,1,0:T(8,128)(2,1)}), bf16[8,400,256]{2,1,0:T(8,128)(2,1)}, u32[]{:S(2)}, u32[]{:S(2)}) %all-to-all-start) | async-done | bytes 1638432 | tf_op jit(solution)/shard_map/all_to_all | solution.py:1009
  60.7 20.3 %collective-permute-done.refs_5_.refs_1_.refs_7_ = bf16[256,2048]{1,0:T(8,128)(2,1)S(1)} collective-permute-done((bf16[256,2048]{1,0:T(8,128)(2,1)S(1)}, bf16[256,2048]{1,0:T(8,128)(2,1)S(1)}, u32[]{:S(2)}, u32[]{:S(2)}) %collective-permute-start) | collective-permute-done | bytes 1048608 | tf_op jit(solution)/shard_map/ppermute | solution.py:70
  83.8 20.7 %collective-permute-done.1.refs_6_.refs_2_.refs_8_ = bf16[256,2048]{1,0:T(8,128)(2,1)} collective-permute-done((bf16[256,2048]{1,0:T(8,128)(2,1)S(1)}, bf16[256,2048]{1,0:T(8,128)(2,1)}, u32[]{:S(2)}, u32[]{:S(2)}) %collective-permute-start.1) | collective-permute-done | bytes 1048608 | tf_op jit(solution)/shard_map/ppermute | solution.py:70
  111.5 15.6 %collective-permute-done.2.refs_7_.refs_3_.refs_9_ = bf16[256,2048]{1,0:T(8,128)(2,1)} collective-permute-done((bf16[256,2048]{1,0:T(8,128)(2,1)}, bf16[256,2048]{1,0:T(8,128)(2,1)}, u32[]{:S(2)}, u32[]{:S(2)}) %collective-permute-start.2) | collective-permute-done | bytes 1048608 | tf_op jit(solution)/shard_map/ppermute | solution.py:70
  149.1 24.6 %shard_map.247 = (f32[1536,1536]{1,0:T(8,128)}, bf16[1536,2048]{1,0:T(8,128)(2,1)}, f32[4,3,512]{2,1,0:T(4,128)}, f32[4,3,512]{2,1,0:T(4,128)}) custom-call(s32[8]{0:T(128)} %get-tuple-element.682.order_ref, bf16[384,2048]{1,0:T(8,128)(2,1)} %get-tuple-element.290.refs_0_, bf16[384,2048]{1,0:T(8,128)(2,1)} %collective-permute-done.8.refs_1_, ...), custom_call_target="tpu_custom_call" | custom-call | flops 999999995904 | bytes 1000000000 | tf_op jit(solution)/shard_map/pallas_call | solution.py:438
  195.5 10.2 %shard_map.249 = (f32[1536,512]{1,0:T(8,128)}, bf16[1536,512]{1,0:T(8,128)(2,1)}, f32[1536,128]{1,0:T(8,128)}, bf16[384,2048]{1,0:T(8,128)(2,1)}, bf16[384,2048]{1,0:T(8,128)(2,1)}) custom-call(s32[8]{0:T(128)} %get-tuple-element.682.order_ref, bf16[256,2048]{1,0:T(8,128)(2,1)} %pad_maximum_fusion.3.refs_4_.refs_0_.refs_6_, bf16[256,2048]{1,0:T(8,128)(2,1)} %copy-done.20, ...), custom_call_target="tpu_custom_call" | custom-call | flops 999999995904 | bytes 1000000000 | tf_op jit(solution)/shard_map/pallas_call | solution.py:438
  208.4 10.3 %shard_map.250 = (f32[1536,512]{1,0:T(8,128)}, bf16[1536,512]{1,0:T(8,128)(2,1)}, f32[1536,128]{1,0:T(8,128)}, bf16[384,2048]{1,0:T(8,128)(2,1)}, bf16[384,2048]{1,0:T(8,128)(2,1)}) custom-call(s32[8]{0:T(128)} %get-tuple-element.682.order_ref, ...), custom_call_target="tpu_custom_call", output_to_operand_aliasing={{0}: (14, {}), {1}: (15, {}), {2}: (16, {})} | custom-call | flops 1 | bytes 1 | tf_op jit(solution)/shard_map/pallas_call | solution.py:438
  235.6 11.2 %collective-permute-done.22.refs_13_.refs_11_ = bf16[176,2048]{1,0:T(8,128)(2,1)} collective-permute-done((bf16[176,2048]{1,0:T(8,128)(2,1)}, bf16[176,2048]{1,0:T(8,128)(2,1)}, u32[]{:S(2)}, u32[]{:S(2)}) %collective-permute-start.22) | collective-permute-done | bytes 720928 | tf_op jit(solution)/shard_map/ppermute | solution.py:70
  252.3 14.3 %collective-permute-done.26 = f32[4,384]{1,0:T(4,128)S(1)} collective-permute-done((f32[4,384]{1,0:T(4,128)S(1)}, f32[4,384]{1,0:T(4,128)S(1)}, u32[]{:S(2)}, u32[]{:S(2)}) %collective-permute-start.26) | collective-permute-done | bytes 6176 | tf_op jit(solution)/shard_map/ppermute | solution.py:76
  277.7 14.6 %collective-permute-done.30.refs_14_.refs_12_ = bf16[176,2048]{1,0:T(8,128)(2,1)S(1)} collective-permute-done((bf16[176,2048]{1,0:T(8,128)(2,1)}, bf16[176,2048]{1,0:T(8,128)(2,1)S(1)}, u32[]{:S(2)}, u32[]{:S(2)}) %collective-permute-start.30) | collective-permute-done | bytes 720928 | tf_op jit(solution)/shard_map/ppermute | solution.py:70
  321.0 19.5 %shard_map.252 = (bf16[1536,1408]{1,0:T(8,128)(2,1)}, bf16[1536,1408]{1,0:T(8,128)(2,1)}, bf16[1536,1408]{1,0:T(8,128)(2,1)}, bf16[1536,2048]{1,0:T(8,128)(2,1)}) custom-call(s32[8]{0:T(128)} %get-tuple-element.682.order_ref, bf16[384,2048]{1,0:T(8,128)(2,1)} %get-tuple-element.344.refs_0_, bf16[384,2048]{1,0:T(8,128)(2,1)} %copy-done.82, ...), custom_call_target="tpu_custom_call" | custom-call | flops 999999995904 | bytes 1000000000 | tf_op jit(solution)/shard_map/pallas_call | solution.py:438
  345.3 19.4 %shard_map.253 = (bf16[1536,1408]{1,0:T(8,128)(2,1)}, bf16[1536,1408]{1,0:T(8,128)(2,1)}, bf16[1536,1408]{1,0:T(8,128)(2,1)}, bf16[1536,2048]{1,0:T(8,128)(2,1)}) custom-call(s32[8]{0:T(128)} %get-tuple-element.682.order_ref, ...), custom_call_target="tpu_custom_call", output_to_operand_aliasing={{0}: (21, {}), {1}: (22, {}), {2}: (23, {}), {3}: (24, {})} | custom-call | flops 1 | bytes 1 | tf_op jit(solution)/shard_map/pallas_call | solution.py:438
  373.4 16.5 %collective-permute-done.42.refs_2_ = bf16[176,2048]{1,0:T(8,128)(2,1)S(1)} collective-permute-done((bf16[176,2048]{1,0:T(8,128)(2,1)}, bf16[176,2048]{1,0:T(8,128)(2,1)S(1)}, u32[]{:S(2)}, u32[]{:S(2)}) %collective-permute-start.42) | collective-permute-done | bytes 720928 | tf_op jit(solution)/shard_map/ppermute | solution.py:70
  392.0 15.4 %collective-permute-done.44.refs_3_ = bf16[176,2048]{1,0:T(8,128)(2,1)S(1)} collective-permute-done((bf16[176,2048]{1,0:T(8,128)(2,1)S(1)}, bf16[176,2048]{1,0:T(8,128)(2,1)S(1)}, u32[]{:S(2)}, u32[]{:S(2)}) %collective-permute-start.44) | collective-permute-done | bytes 720928 | tf_op jit(solution)/shard_map/ppermute | solution.py:70
  428.2 17.5 %shard_map.255 = (bf16[1536,1408]{1,0:T(8,128)(2,1)}, bf16[1536,1408]{1,0:T(8,128)(2,1)}) custom-call(s32[8]{0:T(128)} %get-tuple-element.682.order_ref, bf16[176,2048]{1,0:T(8,128)(2,1)} %constant_dynamic-slice_fusion.32.refs_0_, bf16[176,2048]{1,0:T(8,128)(2,1)} %collective-permute-done.37.refs_1_, bf16[176,2048]{1,0:T(8,128)(2,1)} %copy-done.85, ...), custom_call_target="tpu_custom_call" | custom-call | flops 999999995904 | bytes 1000000000 | tf_op jit(solution)/shard_map/pallas_call | solution.py:438
  451.1 17.7 %shard_map.256 = (bf16[384,2048]{1,0:T(8,128)(2,1)}, bf16[384,2048]{1,0:T(8,128)(2,1)}) custom-call(s32[8]{0:T(128)} %get-tuple-element.682.order_ref, bf16[176,2048]{1,0:T(8,128)(2,1)} %get-tuple-element.295.refs_2_.refs_0_, bf16[176,2048]{1,0:T(8,128)(2,1)} %collective-permute-done.11.refs_3_.refs_1_, ...), custom_call_target="tpu_custom_call" | custom-call | flops 999999995904 | bytes 1000000000 | tf_op jit(solution)/shard_map/pallas_call | solution.py:438
  478.5 17.7 %shard_map.257 = (bf16[384,2048]{1,0:T(8,128)(2,1)}, bf16[384,2048]{1,0:T(8,128)(2,1)}) custom-call(s32[8]{0:T(128)} %get-tuple-element.682.order_ref, bf16[176,2048]{1,0:T(8,128)(2,1)} %get-tuple-element.295.refs_2_.refs_0_, bf16[176,2048]{1,0:T(8,128)(2,1)} %collective-permute-done.11.refs_3_.refs_1_, ...), custom_call_target="tpu_custom_call" | custom-call | flops 999999995904 | bytes 1000000000 | tf_op jit(solution)/shard_map/pallas_call | solution.py:438
  501.0 11.6 %convolution_convert_fusion.1 = bf16[1408,2048]{1,0:T(8,128)(2,1)S(1)} fusion(bf16[1536,1408]{1,0:T(8,128)(2,1)S(1)} %copy-done.91, bf16[1536,2048]{1,0:T(8,128)(2,1)} %get-tuple-element.397), kind=kOutput, calls=%fused_computation.2 | convolution fusion | flops 8861253632 | bytes 16384000 | tf_op jit(solution)/shard_map/dot_general | solution.py:970
  534.3 16.4 %shard_map.259 = (bf16[384,2048]{1,0:T(8,128)(2,1)}, bf16[384,2048]{1,0:T(8,128)(2,1)}, bf16[384,2048]{1,0:T(8,128)(2,1)}, bf16[384,2048]{1,0:T(8,128)(2,1)}) custom-call(s32[8]{0:T(128)} %get-tuple-element.682.order_ref, bf16[176,2048]{1,0:T(8,128)(2,1)} %constant_dynamic-slice_fusion.32.refs_0_, bf16[176,2048]{1,0:T(8,128)(2,1)} %collective-permute-done.37.refs_1_, ...), custom_call_target="tpu_custom_call" | custom-call | flops 999999995904 | bytes 1000000000 | tf_op jit(solution)/shard_map/pallas_call | solution.py:438
  555.5 12.6 %convolution_convert_fusion = bf16[1408,2048]{1,0:T(8,128)(2,1)S(1)} fusion(bf16[1536,1408]{1,0:T(8,128)(2,1)} %get-tuple-element.421.refs_19_, bf16[1536,2048]{1,0:T(8,128)(2,1)} %get-tuple-element.397), kind=kOutput, calls=%fused_computation.1 | convolution fusion | flops 8861253632 | bytes 16384000 | tf_op jit(solution)/shard_map/dot_general | solution.py:970
  589.9 13.8 %shard_map.260 = (f32[1536,512]{1,0:T(8,128)}, bf16[1536,512]{1,0:T(8,128)(2,1)}, bf16[1536,512]{1,0:T(8,128)(2,1)}, bf16[1536,2048]{1,0:T(8,128)(2,1)}, f32[1536,128]{1,0:T(8,128)}, /*index=5*/f32[4,8,512]{2,1,0:T(8,128)}) custom-call(s32[8]{0:T(128)} %get-tuple-element.682.order_ref, bf16[384,2048]{1,0:T(8,128)(2,1)} %get-tuple-element.438.refs_0_, ...), custom_call_target="tpu_custom_call" | custom-call | flops 999999995904 | bytes 1000000000 | tf_op jit(solution)/shard_map/pallas_call | solution.py:438
  681.4 15.7 %shard_map.263 = (bf16[768,512]{1,0:T(8,128)(2,1)}, bf16[768,512]{1,0:T(8,128)(2,1)}, f32[2,8,512]{2,1,0:T(8,128)}, bf16[384,2048]{1,0:T(8,128)(2,1)}, bf16[384,2048]{1,0:T(8,128)(2,1)}) custom-call(s32[8]{0:T(128)} %get-tuple-element.682.order_ref, bf16[256,2048]{1,0:T(8,128)(2,1)} %pad_maximum_fusion.3.refs_4_.refs_0_.refs_6_, ...), custom_call_target="tpu_custom_call" | custom-call | flops 999999995904 | bytes 1000000000 | tf_op jit(solution)/shard_map/pallas_call | solution.py:438
  723.4 15.4 %shard_map.265 = (bf16[768,512]{1,0:T(8,128)(2,1)}, bf16[768,512]{1,0:T(8,128)(2,1)}, f32[2,8,512]{2,1,0:T(8,128)}, bf16[384,2048]{1,0:T(8,128)(2,1)}, bf16[384,2048]{1,0:T(8,128)(2,1)}) custom-call(s32[8]{0:T(128)} %get-tuple-element.682.order_ref, bf16[256,2048]{1,0:T(8,128)(2,1)} %pad_maximum_fusion.3.refs_4_.refs_0_.refs_6_, ...), custom_call_target="tpu_custom_call" | custom-call | flops 999999995904 | bytes 1000000000 | tf_op jit(solution)/shard_map/pallas_call | solution.py:438
  834.2 14.1 %collective-permute-done.112.refs_2_ = bf16[176,2048]{1,0:T(8,128)(2,1)} collective-permute-done((bf16[176,2048]{1,0:T(8,128)(2,1)}, bf16[176,2048]{1,0:T(8,128)(2,1)}, u32[]{:S(2)}, u32[]{:S(2)}) %collective-permute-start.112) | collective-permute-done | bytes 720928 | tf_op jit(solution)/shard_map/ppermute | solution.py:76
  (640 shorter events, 526.9 us)
Async XLA Ops:
  7.4 45.8 %all-to-all-start = ((bf16[8,400,256]{2,1,0:T(8,128)(2,1)}), bf16[8,400,256]{2,1,0:T(8,128)(2,1)}, u32[]{:S(2)}, u32[]{:S(2)}) async-start(bf16[8,400,256]{2,1,0:T(8,128)(2,1)} %pad_maximum_fusion), calls=%async_computation | async-start | bytes 3276800 | tf_op jit(solution)/shard_map/all_to_all | solution.py:1009
  59.2 48.0 %collective-permute-start.9 = (bf16[384,2048]{1,0:T(8,128)(2,1)}, bf16[384,2048]{1,0:T(8,128)(2,1)}, u32[]{:S(2)}, u32[]{:S(2)}) collective-permute-start(bf16[384,2048]{1,0:T(8,128)(2,1)} %get-tuple-element.290.refs_0_), channel_id=1, source_target_pairs={{0,16},{8,24},{16,0},{24,8},{1,17},{9,25},{17,1},{25,9},{2,18},{10... | collective-permute-start | bytes 4718600 | tf_op jit(solution)/shard_map/ppermute | solution.py:76
  107.2 41.9 %collective-permute-start.8 = (bf16[384,2048]{1,0:T(8,128)(2,1)}, bf16[384,2048]{1,0:T(8,128)(2,1)}, u32[]{:S(2)}, u32[]{:S(2)}) collective-permute-start(bf16[384,2048]{1,0:T(8,128)(2,1)} %get-tuple-element.290.refs_0_), channel_id=1, source_target_pairs={{0,8},{8,0},{16,24},{24,16},{1,9},{9,1},{17,25},{25,17},{2,10},{10... | collective-permute-start | bytes 4718600 | tf_op jit(solution)/shard_map/ppermute | solution.py:76
  107.2 41.9 %collective-permute-start.10 = (bf16[384,2048]{1,0:T(8,128)(2,1)}, bf16[384,2048]{1,0:T(8,128)(2,1)}, u32[]{:S(2)}, u32[]{:S(2)}) collective-permute-start(bf16[384,2048]{1,0:T(8,128)(2,1)} %collective-permute-done.9.refs_2_), channel_id=1, source_target_pairs={{0,8},{8,0},{16,24},{24,16},{1,9},{9,1},{17,25},{25,17},{2,10},{10... | collective-permute-start | bytes 4718600 | tf_op jit(solution)/shard_map/ppermute | solution.py:76
  230.4 36.2 %collective-permute-start.24 = (bf16[384,2048]{1,0:T(8,128)(2,1)}, bf16[384,2048]{1,0:T(8,128)(2,1)}, u32[]{:S(2)}, u32[]{:S(2)}) collective-permute-start(bf16[384,2048]{1,0:T(8,128)(2,1)} %add_convert_fusion.7), channel_id=1, source_target_pairs={{0,16},{8,24},{16,0},{24,8},{1,17},{9,25},{17,1},{25,9},{2,18},{10... | collective-permute-start | bytes 4718600 | tf_op jit(solution)/shard_map/ppermute | solution.py:76
  273.5 39.8 %collective-permute-start.29 = (bf16[384,2048]{1,0:T(8,128)(2,1)}, bf16[384,2048]{1,0:T(8,128)(2,1)S(1)}, u32[]{:S(2)}, u32[]{:S(2)}) collective-permute-start(bf16[384,2048]{1,0:T(8,128)(2,1)} %get-tuple-element.344.refs_0_), channel_id=1, source_target_pairs={{0,8},{8,0},{16,24},{24,16},{1,9},{9,1},{17,25},{25,17},{2,10},{10... | collective-permute-start | bytes 4718600 | tf_op jit(solution)/shard_map/ppermute | solution.py:76
  306.5 33.9 %collective-permute-start.36 = (bf16[384,2048]{1,0:T(8,128)(2,1)}, bf16[384,2048]{1,0:T(8,128)(2,1)}, u32[]{:S(2)}, u32[]{:S(2)}) collective-permute-start(bf16[384,2048]{1,0:T(8,128)(2,1)} %get-tuple-element.344.refs_0_), channel_id=1, source_target_pairs={{0,16},{8,24},{16,0},{24,8},{1,17},{9,25},{17,1},{25,9},{2,18},{10... | collective-permute-start | bytes 4718600 | tf_op jit(solution)/shard_map/ppermute | solution.py:76
  316.5 50.3 %all-to-all-start.1 = ((bf16[8,384,256]{2,1,0:T(8,128)(2,1)}), bf16[8,384,256]{2,1,0:T(8,128)(2,1)}, u32[]{:S(2)}, u32[]{:S(2)}) async-start(bf16[8,384,256]{2,1,0:T(8,128)(2,1)} %bitcast.235), calls=%async_computation.1 | async-start | bytes 3145728 | tf_op jit(solution)/shard_map/all_to_all | solution.py:1009
  369.9 37.8 %collective-permute-start.40 = (bf16[384,2048]{1,0:T(8,128)(2,1)}, bf16[384,2048]{1,0:T(8,128)(2,1)S(1)}, u32[]{:S(2)}, u32[]{:S(2)}) collective-permute-start(bf16[384,2048]{1,0:T(8,128)(2,1)} %shard_map.254.cot_ref), channel_id=1, source_target_pairs={{0,8},{8,0},{16,24},{24,16},{1,9},{9,1},{17,25},{25,17},{2,10},{10... | collective-permute-start | bytes 4718600 | tf_op jit(solution)/shard_map/ppermute | solution.py:76
  369.9 37.8 %collective-permute-start.41 = (bf16[384,2048]{1,0:T(8,128)(2,1)}, bf16[384,2048]{1,0:T(8,128)(2,1)S(1)}, u32[]{:S(2)}, u32[]{:S(2)}) collective-permute-start(bf16[384,2048]{1,0:T(8,128)(2,1)} %shard_map.254.cot_ref), channel_id=1, source_target_pairs={{0,16},{8,24},{16,0},{24,8},{1,17},{9,25},{17,1},{25,9},{2,18},{10... | collective-permute-start | bytes 4718600 | tf_op jit(solution)/shard_map/ppermute | solution.py:76
  477.0 37.8 %collective-permute-start.57 = (bf16[192,2048]{1,0:T(8,128)(2,1)}, bf16[192,2048]{1,0:T(8,128)(2,1)}, u32[]{:S(2)}, u32[]{:S(2)}) collective-permute-start(bf16[192,2048]{1,0:T(8,128)(2,1)} %get-tuple-element.398), channel_id=1, source_target_pairs={{0,16},{8,24},{16,0},{24,8},{1,17},{9,25},{17,1},{25,9},{2,18},{10... | collective-permute-start | bytes 2359304 | tf_op jit(solution)/shard_map/ppermute | solution.py:76
  532.8 39.6 %collective-permute-start.65 = (bf16[192,2048]{1,0:T(8,128)(2,1)}, bf16[192,2048]{1,0:T(8,128)(2,1)}, u32[]{:S(2)}, u32[]{:S(2)}) collective-permute-start(bf16[192,2048]{1,0:T(8,128)(2,1)} %get-tuple-element.422), channel_id=1, source_target_pairs={{0,16},{8,24},{16,0},{24,8},{1,17},{9,25},{17,1},{25,9},{2,18},{10... | collective-permute-start | bytes 2359304 | tf_op jit(solution)/shard_map/ppermute | solution.py:76
  627.9 31.7 %collective-permute-start.82 = (bf16[176,2048]{1,0:T(8,128)(2,1)}, bf16[176,2048]{1,0:T(8,128)(2,1)}, u32[]{:S(2)}, u32[]{:S(2)}) collective-permute-start(bf16[176,2048]{1,0:T(8,128)(2,1)} %get-tuple-element.464), channel_id=1, source_target_pairs={{0,2},{2,4},{4,6},{6,7},{7,5},{5,3},{3,1},{1,0},{8,10},{10,12},{12... | collective-permute-start | bytes 2162696 | tf_op jit(solution)/shard_map/ppermute | solution.py:70
  628.9 31.4 %collective-permute-start.83 = (bf16[176,2048]{1,0:T(8,128)(2,1)}, bf16[176,2048]{1,0:T(8,128)(2,1)}, u32[]{:S(2)}, u32[]{:S(2)}) collective-permute-start(bf16[176,2048]{1,0:T(8,128)(2,1)} %get-tuple-element.465), channel_id=1, source_target_pairs={{0,1},{2,0},{4,2},{6,4},{7,6},{5,7},{3,5},{1,3},{8,9},{10,8},{12,1... | collective-permute-start | bytes 2162696 | tf_op jit(solution)/shard_map/ppermute | solution.py:70
  632.1 65.8 %collective-permute-start.91 = (bf16[384,2048]{1,0:T(8,128)(2,1)}, bf16[384,2048]{1,0:T(8,128)(2,1)}, u32[]{:S(2)}, u32[]{:S(2)}) collective-permute-start(bf16[384,2048]{1,0:T(8,128)(2,1)} %add_convert_fusion.2), channel_id=1, source_target_pairs={{0,16},{8,24},{16,0},{24,8},{1,17},{9,25},{17,1},{25,9},{2,18},{10... | collective-permute-start | bytes 4718600 | tf_op jit(solution)/shard_map/ppermute | solution.py:76
  714.4 34.8 %collective-permute-start.93 = (bf16[192,2048]{1,0:T(8,128)(2,1)}, bf16[192,2048]{1,0:T(8,128)(2,1)}, u32[]{:S(2)}, u32[]{:S(2)}) collective-permute-start(bf16[192,2048]{1,0:T(8,128)(2,1)} %get-tuple-element.498), channel_id=1, source_target_pairs={{0,16},{8,24},{16,0},{24,8},{1,17},{9,25},{17,1},{25,9},{2,18},{10... | collective-permute-start | bytes 2359304 | tf_op jit(solution)/shard_map/ppermute | solution.py:76
  714.9 34.2 %collective-permute-start.96 = (bf16[176,2048]{1,0:T(8,128)(2,1)}, bf16[176,2048]{1,0:T(8,128)(2,1)}, u32[]{:S(2)}, u32[]{:S(2)}) collective-permute-start(bf16[176,2048]{1,0:T(8,128)(2,1)} %get-tuple-element.501), channel_id=1, source_target_pairs={{0,2},{2,4},{4,6},{6,7},{7,5},{5,3},{3,1},{1,0},{8,10},{10,12},{12... | collective-permute-start | bytes 2162696 | tf_op jit(solution)/shard_map/ppermute | solution.py:70
  715.2 33.9 %collective-permute-start.97 = (bf16[176,2048]{1,0:T(8,128)(2,1)}, bf16[176,2048]{1,0:T(8,128)(2,1)}, u32[]{:S(2)}, u32[]{:S(2)}) collective-permute-start(bf16[176,2048]{1,0:T(8,128)(2,1)} %get-tuple-element.502), channel_id=1, source_target_pairs={{0,1},{2,0},{4,2},{6,4},{7,6},{5,7},{3,5},{1,3},{8,9},{10,8},{12,1... | collective-permute-start | bytes 2162696 | tf_op jit(solution)/shard_map/ppermute | solution.py:70
  717.3 31.9 %collective-permute-start.95 = (bf16[128,2048]{1,0:T(8,128)(2,1)}, bf16[128,2048]{1,0:T(8,128)(2,1)}, u32[]{:S(2)}, u32[]{:S(2)}) collective-permute-start(bf16[128,2048]{1,0:T(8,128)(2,1)} %add_convert_fusion.41), channel_id=1, source_target_pairs={{0,1},{2,0},{4,2},{6,4},{7,6},{5,7},{3,5},{1,3},{8,9},{10,8},{12,1... | collective-permute-start | bytes 1572872 | tf_op jit(solution)/shard_map/ppermute | solution.py:70
  719.0 105.2 %all-to-all-start.3 = ((bf16[8,384,256]{2,1,0:T(8,128)(2,1)}), bf16[8,384,256]{2,1,0:T(8,128)(2,1)}, u32[]{:S(2)}, u32[]{:S(2)}) async-start(bf16[8,384,256]{2,1,0:T(8,128)(2,1)} %shard_map.264), calls=%async_computation.3 | async-start | bytes 3145728 | tf_op jit(solution)/shard_map/all_to_all | solution.py:1009
  745.4 50.0 %collective-permute-start.101 = (bf16[192,2048]{1,0:T(8,128)(2,1)}, bf16[192,2048]{1,0:T(8,128)(2,1)}, u32[]{:S(2)}, u32[]{:S(2)}) collective-permute-start(bf16[192,2048]{1,0:T(8,128)(2,1)} %get-tuple-element.519), channel_id=1, source_target_pairs={{0,16},{8,24},{16,0},{24,8},{1,17},{9,25},{17,1},{25,9},{2,18},{10... | collective-permute-start | bytes 2359304 | tf_op jit(solution)/shard_map/ppermute | solution.py:76
  815.1 33.2 %collective-permute-start.112 = (bf16[176,2048]{1,0:T(8,128)(2,1)}, bf16[176,2048]{1,0:T(8,128)(2,1)}, u32[]{:S(2)}, u32[]{:S(2)}) collective-permute-start(bf16[176,2048]{1,0:T(8,128)(2,1)} %add_convert_fusion.8.refs_0_), channel_id=1, source_target_pairs={{0,16},{8,24},{16,0},{24,8},{1,17},{9,25},{17,1},{25,9},{2,18},{10... | collective-permute-start | bytes 2162696 | tf_op jit(solution)/shard_map/ppermute | solution.py:76
  824.9 56.9 %all-to-all-start.2 = ((bf16[8,400,256]{2,1,0:T(8,128)(2,1)}), bf16[8,400,256]{2,1,0:T(8,128)(2,1)S(1)}, u32[]{:S(2)}, u32[]{:S(2)}) async-start(bf16[8,400,256]{2,1,0:T(8,128)(2,1)} %shard_map.266), calls=%async_computation.2 | async-start | bytes 3276800 | tf_op jit(solution)/shard_map/all_to_all | solution.py:1009
  834.2 31.0 %collective-permute-start.111 = (bf16[176,2048]{1,0:T(8,128)(2,1)}, bf16[176,2048]{1,0:T(8,128)(2,1)S(1)}, u32[]{:S(2)}, u32[]{:S(2)}) collective-permute-start(bf16[176,2048]{1,0:T(8,128)(2,1)} %add_convert_fusion.8.refs_0_), channel_id=1, source_target_pairs={{0,8},{8,0},{16,24},{24,16},{1,9},{9,1},{17,25},{25,17},{2,10},{10... | collective-permute-start | bytes 2162696 | tf_op jit(solution)/shard_map/ppermute | solution.py:76
  (205 other events, 2893.8 us)

commit v6 on v5

--- a/solution.py
+++ b/solution.py
@@ -938,7 +938,7 @@
 def turn_rows(blocks, place):
     count = len(blocks)
     q, width = blocks[0].shape
-    tile = 256
+    tile = 512
 
     def body(place_ref, *refs):
         out_ref, held = refs[count], refs[count + 1]

time: 939 us -> 933 us (level)
  no operation moved by 1% of the time
where the time goes in v6:
time: 933 us; the launch traced here: 923 us
  waiting for transfers between devices  295 us (32%)
  Pallas kernels  273 us (29%)
  starting transfers between devices  139 us (15%)
  other arithmetic  79.2 us (8%)
  local copies, waits for them, and re-layouts  75.3 us (8%)
  matrix products  54.3 us (6%)
    ppermute x72, waiting for transfers between devices, shift(): lax.ppermute(x, 'tp', [(self.cycle[i], self.cycle[(i + k) % n]) for i in...  202 us
    pallas_call x12, Pallas kernels, step_kernel(): pl.pallas_call(kernel, grid=(count,), out_shape=[shape for shape, _ in ou...  198 us
    ppermute x72, starting transfers between devices, shift(): lax.ppermute(x, 'tp', [(self.cycle[i], self.cycle[(i + k) % n]) for i in...  84.6 us
    dot_general x7, matrix products, dot_tn(): lax.dot_general(a, b, (((0,), (0,)), ((), ())), preferred_element_type=F32)  54.3 us
    ppermute x49, waiting for transfers between devices, swap(): return lax.ppermute(x, 'seq', [(i, i ^ bit) for i in range(self.seq)])  50.4 us
    convert_element_type x26, other arithmetic, make(): made.append(whole.astype(BF16))  48.4 us
    all_to_all x4, waiting for transfers between devices, to_owner(): return lax.all_to_all(x, 'tp', 0, 0, tiled=True)  30.1 us
    ppermute x49, starting transfers between devices, swap(): return lax.ppermute(x, 'seq', [(i, i ^ bit) for i in range(self.seq)])  26.1 us
  transfers between devices with their start and end apart: 131, of which 55 were waited for; matrix products, arithmetic and copies ran while one was open for 18% of the time, Pallas kernels for 25%

profile of v6, /device:TPU:0, one launch (start us, length us, event | category | flops | bytes accessed | tf_op | source)
XLA Modules:
  0.0 923.0 jit_solution(2443998530948187530)
XLA Ops:
  25.2 28.0 %all-to-all-done.in_ref = bf16[8,400,256]{2,1,0:T(8,128)(2,1)} async-done(((bf16[8,400,256]{2,1,0:T(8,128)(2,1)}), bf16[8,400,256]{2,1,0:T(8,128)(2,1)}, u32[]{:S(2)}, u32[]{:S(2)}) %all-to-all-start) | async-done | bytes 1638432 | tf_op jit(solution)/shard_map/all_to_all | solution.py:1009
  60.7 20.3 %collective-permute-done.refs_5_.refs_1_.refs_7_ = bf16[256,2048]{1,0:T(8,128)(2,1)S(1)} collective-permute-done((bf16[256,2048]{1,0:T(8,128)(2,1)S(1)}, bf16[256,2048]{1,0:T(8,128)(2,1)S(1)}, u32[]{:S(2)}, u32[]{:S(2)}) %collective-permute-start) | collective-permute-done | bytes 1048608 | tf_op jit(solution)/shard_map/ppermute | solution.py:70
  83.8 20.7 %collective-permute-done.1.refs_6_.refs_2_.refs_8_ = bf16[256,2048]{1,0:T(8,128)(2,1)} collective-permute-done((bf16[256,2048]{1,0:T(8,128)(2,1)S(1)}, bf16[256,2048]{1,0:T(8,128)(2,1)}, u32[]{:S(2)}, u32[]{:S(2)}) %collective-permute-start.1) | collective-permute-done | bytes 1048608 | tf_op jit(solution)/shard_map/ppermute | solution.py:70
  111.5 15.6 %collective-permute-done.2.refs_7_.refs_3_.refs_9_ = bf16[256,2048]{1,0:T(8,128)(2,1)} collective-permute-done((bf16[256,2048]{1,0:T(8,128)(2,1)}, bf16[256,2048]{1,0:T(8,128)(2,1)}, u32[]{:S(2)}, u32[]{:S(2)}) %collective-permute-start.2) | collective-permute-done | bytes 1048608 | tf_op jit(solution)/shard_map/ppermute | solution.py:70
  149.1 24.6 %shard_map.247 = (f32[1536,1536]{1,0:T(8,128)}, bf16[1536,2048]{1,0:T(8,128)(2,1)}, f32[4,3,512]{2,1,0:T(4,128)}, f32[4,3,512]{2,1,0:T(4,128)}) custom-call(s32[8]{0:T(128)} %get-tuple-element.682.order_ref, bf16[384,2048]{1,0:T(8,128)(2,1)} %get-tuple-element.290.refs_0_, bf16[384,2048]{1,0:T(8,128)(2,1)} %collective-permute-done.8.refs_1_, ...), custom_call_target="tpu_custom_call" | custom-call | flops 999999995904 | bytes 1000000000 | tf_op jit(solution)/shard_map/pallas_call | solution.py:438
  195.5 10.2 %shard_map.249 = (f32[1536,512]{1,0:T(8,128)}, bf16[1536,512]{1,0:T(8,128)(2,1)}, f32[1536,128]{1,0:T(8,128)}, bf16[384,2048]{1,0:T(8,128)(2,1)}, bf16[384,2048]{1,0:T(8,128)(2,1)}) custom-call(s32[8]{0:T(128)} %get-tuple-element.682.order_ref, bf16[256,2048]{1,0:T(8,128)(2,1)} %pad_maximum_fusion.3.refs_4_.refs_0_.refs_6_, bf16[256,2048]{1,0:T(8,128)(2,1)} %copy-done.20, ...), custom_call_target="tpu_custom_call" | custom-call | flops 999999995904 | bytes 1000000000 | tf_op jit(solution)/shard_map/pallas_call | solution.py:438
  208.4 10.3 %shard_map.250 = (f32[1536,512]{1,0:T(8,128)}, bf16[1536,512]{1,0:T(8,128)(2,1)}, f32[1536,128]{1,0:T(8,128)}, bf16[384,2048]{1,0:T(8,128)(2,1)}, bf16[384,2048]{1,0:T(8,128)(2,1)}) custom-call(s32[8]{0:T(128)} %get-tuple-element.682.order_ref, ...), custom_call_target="tpu_custom_call", output_to_operand_aliasing={{0}: (14, {}), {1}: (15, {}), {2}: (16, {})} | custom-call | flops 1 | bytes 1 | tf_op jit(solution)/shard_map/pallas_call | solution.py:438
  235.6 11.2 %collective-permute-done.22.refs_13_.refs_11_ = bf16[176,2048]{1,0:T(8,128)(2,1)} collective-permute-done((bf16[176,2048]{1,0:T(8,128)(2,1)}, bf16[176,2048]{1,0:T(8,128)(2,1)}, u32[]{:S(2)}, u32[]{:S(2)}) %collective-permute-start.22) | collective-permute-done | bytes 720928 | tf_op jit(solution)/shard_map/ppermute | solution.py:70
  252.3 14.3 %collective-permute-done.26 = f32[4,384]{1,0:T(4,128)S(1)} collective-permute-done((f32[4,384]{1,0:T(4,128)S(1)}, f32[4,384]{1,0:T(4,128)S(1)}, u32[]{:S(2)}, u32[]{:S(2)}) %collective-permute-start.26) | collective-permute-done | bytes 6176 | tf_op jit(solution)/shard_map/ppermute | solution.py:76
  277.7 14.6 %collective-permute-done.30.refs_14_.refs_12_ = bf16[176,2048]{1,0:T(8,128)(2,1)S(1)} collective-permute-done((bf16[176,2048]{1,0:T(8,128)(2,1)}, bf16[176,2048]{1,0:T(8,128)(2,1)S(1)}, u32[]{:S(2)}, u32[]{:S(2)}) %collective-permute-start.30) | collective-permute-done | bytes 720928 | tf_op jit(solution)/shard_map/ppermute | solution.py:70
  321.0 19.5 %shard_map.252 = (bf16[1536,1408]{1,0:T(8,128)(2,1)}, bf16[1536,1408]{1,0:T(8,128)(2,1)}, bf16[1536,1408]{1,0:T(8,128)(2,1)}, bf16[1536,2048]{1,0:T(8,128)(2,1)}) custom-call(s32[8]{0:T(128)} %get-tuple-element.682.order_ref, bf16[384,2048]{1,0:T(8,128)(2,1)} %get-tuple-element.344.refs_0_, bf16[384,2048]{1,0:T(8,128)(2,1)} %copy-done.82, ...), custom_call_target="tpu_custom_call" | custom-call | flops 999999995904 | bytes 1000000000 | tf_op jit(solution)/shard_map/pallas_call | solution.py:438
  345.3 19.4 %shard_map.253 = (bf16[1536,1408]{1,0:T(8,128)(2,1)}, bf16[1536,1408]{1,0:T(8,128)(2,1)}, bf16[1536,1408]{1,0:T(8,128)(2,1)}, bf16[1536,2048]{1,0:T(8,128)(2,1)}) custom-call(s32[8]{0:T(128)} %get-tuple-element.682.order_ref, ...), custom_call_target="tpu_custom_call", output_to_operand_aliasing={{0}: (21, {}), {1}: (22, {}), {2}: (23, {}), {3}: (24, {})} | custom-call | flops 1 | bytes 1 | tf_op jit(solution)/shard_map/pallas_call | solution.py:438
  373.4 16.5 %collective-permute-done.42.refs_2_ = bf16[176,2048]{1,0:T(8,128)(2,1)S(1)} collective-permute-done((bf16[176,2048]{1,0:T(8,128)(2,1)}, bf16[176,2048]{1,0:T(8,128)(2,1)S(1)}, u32[]{:S(2)}, u32[]{:S(2)}) %collective-permute-start.42) | collective-permute-done | bytes 720928 | tf_op jit(solution)/shard_map/ppermute | solution.py:70
  392.0 15.4 %collective-permute-done.44.refs_3_ = bf16[176,2048]{1,0:T(8,128)(2,1)S(1)} collective-permute-done((bf16[176,2048]{1,0:T(8,128)(2,1)S(1)}, bf16[176,2048]{1,0:T(8,128)(2,1)S(1)}, u32[]{:S(2)}, u32[]{:S(2)}) %collective-permute-start.44) | collective-permute-done | bytes 720928 | tf_op jit(solution)/shard_map/ppermute | solution.py:70
  428.2 17.5 %shard_map.255 = (bf16[1536,1408]{1,0:T(8,128)(2,1)}, bf16[1536,1408]{1,0:T(8,128)(2,1)}) custom-call(s32[8]{0:T(128)} %get-tuple-element.682.order_ref, bf16[176,2048]{1,0:T(8,128)(2,1)} %constant_dynamic-slice_fusion.32.refs_0_, bf16[176,2048]{1,0:T(8,128)(2,1)} %collective-permute-done.37.refs_1_, bf16[176,2048]{1,0:T(8,128)(2,1)} %copy-done.85, ...), custom_call_target="tpu_custom_call" | custom-call | flops 999999995904 | bytes 1000000000 | tf_op jit(solution)/shard_map/pallas_call | solution.py:438
  451.1 17.7 %shard_map.256 = (bf16[384,2048]{1,0:T(8,128)(2,1)}, bf16[384,2048]{1,0:T(8,128)(2,1)}) custom-call(s32[8]{0:T(128)} %get-tuple-element.682.order_ref, bf16[176,2048]{1,0:T(8,128)(2,1)} %get-tuple-element.295.refs_2_.refs_0_, bf16[176,2048]{1,0:T(8,128)(2,1)} %collective-permute-done.11.refs_3_.refs_1_, ...), custom_call_target="tpu_custom_call" | custom-call | flops 999999995904 | bytes 1000000000 | tf_op jit(solution)/shard_map/pallas_call | solution.py:438
  478.5 17.7 %shard_map.257 = (bf16[384,2048]{1,0:T(8,128)(2,1)}, bf16[384,2048]{1,0:T(8,128)(2,1)}) custom-call(s32[8]{0:T(128)} %get-tuple-element.682.order_ref, bf16[176,2048]{1,0:T(8,128)(2,1)} %get-tuple-element.295.refs_2_.refs_0_, bf16[176,2048]{1,0:T(8,128)(2,1)} %collective-permute-done.11.refs_3_.refs_1_, ...), custom_call_target="tpu_custom_call" | custom-call | flops 999999995904 | bytes 1000000000 | tf_op jit(solution)/shard_map/pallas_call | solution.py:438
  501.0 11.6 %convolution_convert_fusion.1 = bf16[1408,2048]{1,0:T(8,128)(2,1)S(1)} fusion(bf16[1536,1408]{1,0:T(8,128)(2,1)S(1)} %copy-done.91, bf16[1536,2048]{1,0:T(8,128)(2,1)} %get-tuple-element.397), kind=kOutput, calls=%fused_computation.2 | convolution fusion | flops 8861253632 | bytes 16384000 | tf_op jit(solution)/shard_map/dot_general | solution.py:970
  534.3 16.4 %shard_map.259 = (bf16[384,2048]{1,0:T(8,128)(2,1)}, bf16[384,2048]{1,0:T(8,128)(2,1)}, bf16[384,2048]{1,0:T(8,128)(2,1)}, bf16[384,2048]{1,0:T(8,128)(2,1)}) custom-call(s32[8]{0:T(128)} %get-tuple-element.682.order_ref, bf16[176,2048]{1,0:T(8,128)(2,1)} %constant_dynamic-slice_fusion.32.refs_0_, bf16[176,2048]{1,0:T(8,128)(2,1)} %collective-permute-done.37.refs_1_, ...), custom_call_target="tpu_custom_call" | custom-call | flops 999999995904 | bytes 1000000000 | tf_op jit(solution)/shard_map/pallas_call | solution.py:438
  555.5 12.6 %convolution_convert_fusion = bf16[1408,2048]{1,0:T(8,128)(2,1)S(1)} fusion(bf16[1536,1408]{1,0:T(8,128)(2,1)} %get-tuple-element.421.refs_19_, bf16[1536,2048]{1,0:T(8,128)(2,1)} %get-tuple-element.397), kind=kOutput, calls=%fused_computation.1 | convolution fusion | flops 8861253632 | bytes 16384000 | tf_op jit(solution)/shard_map/dot_general | solution.py:970
  589.9 13.8 %shard_map.260 = (f32[1536,512]{1,0:T(8,128)}, bf16[1536,512]{1,0:T(8,128)(2,1)}, bf16[1536,512]{1,0:T(8,128)(2,1)}, bf16[1536,2048]{1,0:T(8,128)(2,1)}, f32[1536,128]{1,0:T(8,128)}, /*index=5*/f32[4,8,512]{2,1,0:T(8,128)}) custom-call(s32[8]{0:T(128)} %get-tuple-element.682.order_ref, bf16[384,2048]{1,0:T(8,128)(2,1)} %get-tuple-element.438.refs_0_, ...), custom_call_target="tpu_custom_call" | custom-call | flops 999999995904 | bytes 1000000000 | tf_op jit(solution)/shard_map/pallas_call | solution.py:438
  681.4 15.7 %shard_map.263 = (bf16[768,512]{1,0:T(8,128)(2,1)}, bf16[768,512]{1,0:T(8,128)(2,1)}, f32[2,8,512]{2,1,0:T(8,128)}, bf16[384,2048]{1,0:T(8,128)(2,1)}, bf16[384,2048]{1,0:T(8,128)(2,1)}) custom-call(s32[8]{0:T(128)} %get-tuple-element.682.order_ref, bf16[256,2048]{1,0:T(8,128)(2,1)} %pad_maximum_fusion.3.refs_4_.refs_0_.refs_6_, ...), custom_call_target="tpu_custom_call" | custom-call | flops 999999995904 | bytes 1000000000 | tf_op jit(solution)/shard_map/pallas_call | solution.py:438
  723.4 15.4 %shard_map.265 = (bf16[768,512]{1,0:T(8,128)(2,1)}, bf16[768,512]{1,0:T(8,128)(2,1)}, f32[2,8,512]{2,1,0:T(8,128)}, bf16[384,2048]{1,0:T(8,128)(2,1)}, bf16[384,2048]{1,0:T(8,128)(2,1)}) custom-call(s32[8]{0:T(128)} %get-tuple-element.682.order_ref, bf16[256,2048]{1,0:T(8,128)(2,1)} %pad_maximum_fusion.3.refs_4_.refs_0_.refs_6_, ...), custom_call_target="tpu_custom_call" | custom-call | flops 999999995904 | bytes 1000000000 | tf_op jit(solution)/shard_map/pallas_call | solution.py:438
  834.2 14.1 %collective-permute-done.112.refs_2_ = bf16[176,2048]{1,0:T(8,128)(2,1)} collective-permute-done((bf16[176,2048]{1,0:T(8,128)(2,1)}, bf16[176,2048]{1,0:T(8,128)(2,1)}, u32[]{:S(2)}, u32[]{:S(2)}) %collective-permute-start.112) | collective-permute-done | bytes 720928 | tf_op jit(solution)/shard_map/ppermute | solution.py:76
  (640 shorter events, 522.2 us)
Async XLA Ops:
  7.4 45.8 %all-to-all-start = ((bf16[8,400,256]{2,1,0:T(8,128)(2,1)}), bf16[8,400,256]{2,1,0:T(8,128)(2,1)}, u32[]{:S(2)}, u32[]{:S(2)}) async-start(bf16[8,400,256]{2,1,0:T(8,128)(2,1)} %pad_maximum_fusion), calls=%async_computation | async-start | bytes 3276800 | tf_op jit(solution)/shard_map/all_to_all | solution.py:1009
  59.2 48.0 %collective-permute-start.9 = (bf16[384,2048]{1,0:T(8,128)(2,1)}, bf16[384,2048]{1,0:T(8,128)(2,1)}, u32[]{:S(2)}, u32[]{:S(2)}) collective-permute-start(bf16[384,2048]{1,0:T(8,128)(2,1)} %get-tuple-element.290.refs_0_), channel_id=1, source_target_pairs={{0,16},{8,24},{16,0},{24,8},{1,17},{9,25},{17,1},{25,9},{2,18},{10... | collective-permute-start | bytes 4718600 | tf_op jit(solution)/shard_map/ppermute | solution.py:76
  107.2 41.9 %collective-permute-start.8 = (bf16[384,2048]{1,0:T(8,128)(2,1)}, bf16[384,2048]{1,0:T(8,128)(2,1)}, u32[]{:S(2)}, u32[]{:S(2)}) collective-permute-start(bf16[384,2048]{1,0:T(8,128)(2,1)} %get-tuple-element.290.refs_0_), channel_id=1, source_target_pairs={{0,8},{8,0},{16,24},{24,16},{1,9},{9,1},{17,25},{25,17},{2,10},{10... | collective-permute-start | bytes 4718600 | tf_op jit(solution)/shard_map/ppermute | solution.py:76
  107.2 41.9 %collective-permute-start.10 = (bf16[384,2048]{1,0:T(8,128)(2,1)}, bf16[384,2048]{1,0:T(8,128)(2,1)}, u32[]{:S(2)}, u32[]{:S(2)}) collective-permute-start(bf16[384,2048]{1,0:T(8,128)(2,1)} %collective-permute-done.9.refs_2_), channel_id=1, source_target_pairs={{0,8},{8,0},{16,24},{24,16},{1,9},{9,1},{17,25},{25,17},{2,10},{10... | collective-permute-start | bytes 4718600 | tf_op jit(solution)/shard_map/ppermute | solution.py:76
  230.4 36.2 %collective-permute-start.24 = (bf16[384,2048]{1,0:T(8,128)(2,1)}, bf16[384,2048]{1,0:T(8,128)(2,1)}, u32[]{:S(2)}, u32[]{:S(2)}) collective-permute-start(bf16[384,2048]{1,0:T(8,128)(2,1)} %add_convert_fusion.7), channel_id=1, source_target_pairs={{0,16},{8,24},{16,0},{24,8},{1,17},{9,25},{17,1},{25,9},{2,18},{10... | collective-permute-start | bytes 4718600 | tf_op jit(solution)/shard_map/ppermute | solution.py:76
  273.5 39.8 %collective-permute-start.29 = (bf16[384,2048]{1,0:T(8,128)(2,1)}, bf16[384,2048]{1,0:T(8,128)(2,1)S(1)}, u32[]{:S(2)}, u32[]{:S(2)}) collective-permute-start(bf16[384,2048]{1,0:T(8,128)(2,1)} %get-tuple-element.344.refs_0_), channel_id=1, source_target_pairs={{0,8},{8,0},{16,24},{24,16},{1,9},{9,1},{17,25},{25,17},{2,10},{10... | collective-permute-start | bytes 4718600 | tf_op jit(solution)/shard_map/ppermute | solution.py:76
  306.5 33.9 %collective-permute-start.36 = (bf16[384,2048]{1,0:T(8,128)(2,1)}, bf16[384,2048]{1,0:T(8,128)(2,1)}, u32[]{:S(2)}, u32[]{:S(2)}) collective-permute-start(bf16[384,2048]{1,0:T(8,128)(2,1)} %get-tuple-element.344.refs_0_), channel_id=1, source_target_pairs={{0,16},{8,24},{16,0},{24,8},{1,17},{9,25},{17,1},{25,9},{2,18},{10... | collective-permute-start | bytes 4718600 | tf_op jit(solution)/shard_map/ppermute | solution.py:76
  316.5 50.3 %all-to-all-start.1 = ((bf16[8,384,256]{2,1,0:T(8,128)(2,1)}), bf16[8,384,256]{2,1,0:T(8,128)(2,1)}, u32[]{:S(2)}, u32[]{:S(2)}) async-start(bf16[8,384,256]{2,1,0:T(8,128)(2,1)} %bitcast.235), calls=%async_computation.1 | async-start | bytes 3145728 | tf_op jit(solution)/shard_map/all_to_all | solution.py:1009
  369.9 37.8 %collective-permute-start.40 = (bf16[384,2048]{1,0:T(8,128)(2,1)}, bf16[384,2048]{1,0:T(8,128)(2,1)S(1)}, u32[]{:S(2)}, u32[]{:S(2)}) collective-permute-start(bf16[384,2048]{1,0:T(8,128)(2,1)} %shard_map.254.cot_ref), channel_id=1, source_target_pairs={{0,8},{8,0},{16,24},{24,16},{1,9},{9,1},{17,25},{25,17},{2,10},{10... | collective-permute-start | bytes 4718600 | tf_op jit(solution)/shard_map/ppermute | solution.py:76
  369.9 37.8 %collective-permute-start.41 = (bf16[384,2048]{1,0:T(8,128)(2,1)}, bf16[384,2048]{1,0:T(8,128)(2,1)S(1)}, u32[]{:S(2)}, u32[]{:S(2)}) collective-permute-start(bf16[384,2048]{1,0:T(8,128)(2,1)} %shard_map.254.cot_ref), channel_id=1, source_target_pairs={{0,16},{8,24},{16,0},{24,8},{1,17},{9,25},{17,1},{25,9},{2,18},{10... | collective-permute-start | bytes 4718600 | tf_op jit(solution)/shard_map/ppermute | solution.py:76
  477.0 37.8 %collective-permute-start.57 = (bf16[192,2048]{1,0:T(8,128)(2,1)}, bf16[192,2048]{1,0:T(8,128)(2,1)}, u32[]{:S(2)}, u32[]{:S(2)}) collective-permute-start(bf16[192,2048]{1,0:T(8,128)(2,1)} %get-tuple-element.398), channel_id=1, source_target_pairs={{0,16},{8,24},{16,0},{24,8},{1,17},{9,25},{17,1},{25,9},{2,18},{10... | collective-permute-start | bytes 2359304 | tf_op jit(solution)/shard_map/ppermute | solution.py:76
  532.8 39.6 %collective-permute-start.65 = (bf16[192,2048]{1,0:T(8,128)(2,1)}, bf16[192,2048]{1,0:T(8,128)(2,1)}, u32[]{:S(2)}, u32[]{:S(2)}) collective-permute-start(bf16[192,2048]{1,0:T(8,128)(2,1)} %get-tuple-element.422), channel_id=1, source_target_pairs={{0,16},{8,24},{16,0},{24,8},{1,17},{9,25},{17,1},{25,9},{2,18},{10... | collective-permute-start | bytes 2359304 | tf_op jit(solution)/shard_map/ppermute | solution.py:76
  627.9 31.7 %collective-permute-start.82 = (bf16[176,2048]{1,0:T(8,128)(2,1)}, bf16[176,2048]{1,0:T(8,128)(2,1)}, u32[]{:S(2)}, u32[]{:S(2)}) collective-permute-start(bf16[176,2048]{1,0:T(8,128)(2,1)} %get-tuple-element.464), channel_id=1, source_target_pairs={{0,2},{2,4},{4,6},{6,7},{7,5},{5,3},{3,1},{1,0},{8,10},{10,12},{12... | collective-permute-start | bytes 2162696 | tf_op jit(solution)/shard_map/ppermute | solution.py:70
  628.9 31.4 %collective-permute-start.83 = (bf16[176,2048]{1,0:T(8,128)(2,1)}, bf16[176,2048]{1,0:T(8,128)(2,1)}, u32[]{:S(2)}, u32[]{:S(2)}) collective-permute-start(bf16[176,2048]{1,0:T(8,128)(2,1)} %get-tuple-element.465), channel_id=1, source_target_pairs={{0,1},{2,0},{4,2},{6,4},{7,6},{5,7},{3,5},{1,3},{8,9},{10,8},{12,1... | collective-permute-start | bytes 2162696 | tf_op jit(solution)/shard_map/ppermute | solution.py:70
  632.1 65.8 %collective-permute-start.91 = (bf16[384,2048]{1,0:T(8,128)(2,1)}, bf16[384,2048]{1,0:T(8,128)(2,1)}, u32[]{:S(2)}, u32[]{:S(2)}) collective-permute-start(bf16[384,2048]{1,0:T(8,128)(2,1)} %add_convert_fusion.2), channel_id=1, source_target_pairs={{0,16},{8,24},{16,0},{24,8},{1,17},{9,25},{17,1},{25,9},{2,18},{10... | collective-permute-start | bytes 4718600 | tf_op jit(solution)/shard_map/ppermute | solution.py:76
  714.4 34.8 %collective-permute-start.93 = (bf16[192,2048]{1,0:T(8,128)(2,1)}, bf16[192,2048]{1,0:T(8,128)(2,1)}, u32[]{:S(2)}, u32[]{:S(2)}) collective-permute-start(bf16[192,2048]{1,0:T(8,128)(2,1)} %get-tuple-element.498), channel_id=1, source_target_pairs={{0,16},{8,24},{16,0},{24,8},{1,17},{9,25},{17,1},{25,9},{2,18},{10... | collective-permute-start | bytes 2359304 | tf_op jit(solution)/shard_map/ppermute | solution.py:76
  714.9 34.2 %collective-permute-start.96 = (bf16[176,2048]{1,0:T(8,128)(2,1)}, bf16[176,2048]{1,0:T(8,128)(2,1)}, u32[]{:S(2)}, u32[]{:S(2)}) collective-permute-start(bf16[176,2048]{1,0:T(8,128)(2,1)} %get-tuple-element.501), channel_id=1, source_target_pairs={{0,2},{2,4},{4,6},{6,7},{7,5},{5,3},{3,1},{1,0},{8,10},{10,12},{12... | collective-permute-start | bytes 2162696 | tf_op jit(solution)/shard_map/ppermute | solution.py:70
  715.2 33.9 %collective-permute-start.97 = (bf16[176,2048]{1,0:T(8,128)(2,1)}, bf16[176,2048]{1,0:T(8,128)(2,1)}, u32[]{:S(2)}, u32[]{:S(2)}) collective-permute-start(bf16[176,2048]{1,0:T(8,128)(2,1)} %get-tuple-element.502), channel_id=1, source_target_pairs={{0,1},{2,0},{4,2},{6,4},{7,6},{5,7},{3,5},{1,3},{8,9},{10,8},{12,1... | collective-permute-start | bytes 2162696 | tf_op jit(solution)/shard_map/ppermute | solution.py:70
  717.3 31.9 %collective-permute-start.95 = (bf16[128,2048]{1,0:T(8,128)(2,1)}, bf16[128,2048]{1,0:T(8,128)(2,1)}, u32[]{:S(2)}, u32[]{:S(2)}) collective-permute-start(bf16[128,2048]{1,0:T(8,128)(2,1)} %add_convert_fusion.41), channel_id=1, source_target_pairs={{0,1},{2,0},{4,2},{6,4},{7,6},{5,7},{3,5},{1,3},{8,9},{10,8},{12,1... | collective-permute-start | bytes 1572872 | tf_op jit(solution)/shard_map/ppermute | solution.py:70
  719.0 105.2 %all-to-all-start.3 = ((bf16[8,384,256]{2,1,0:T(8,128)(2,1)}), bf16[8,384,256]{2,1,0:T(8,128)(2,1)}, u32[]{:S(2)}, u32[]{:S(2)}) async-start(bf16[8,384,256]{2,1,0:T(8,128)(2,1)} %shard_map.264), calls=%async_computation.3 | async-start | bytes 3145728 | tf_op jit(solution)/shard_map/all_to_all | solution.py:1009
  745.4 50.0 %collective-permute-start.101 = (bf16[192,2048]{1,0:T(8,128)(2,1)}, bf16[192,2048]{1,0:T(8,128)(2,1)}, u32[]{:S(2)}, u32[]{:S(2)}) collective-permute-start(bf16[192,2048]{1,0:T(8,128)(2,1)} %get-tuple-element.519), channel_id=1, source_target_pairs={{0,16},{8,24},{16,0},{24,8},{1,17},{9,25},{17,1},{25,9},{2,18},{10... | collective-permute-start | bytes 2359304 | tf_op jit(solution)/shard_map/ppermute | solution.py:76
  815.1 33.2 %collective-permute-start.112 = (bf16[176,2048]{1,0:T(8,128)(2,1)}, bf16[176,2048]{1,0:T(8,128)(2,1)}, u32[]{:S(2)}, u32[]{:S(2)}) collective-permute-start(bf16[176,2048]{1,0:T(8,128)(2,1)} %add_convert_fusion.8.refs_0_), channel_id=1, source_target_pairs={{0,16},{8,24},{16,0},{24,8},{1,17},{9,25},{17,1},{25,9},{2,18},{10... | collective-permute-start | bytes 2162696 | tf_op jit(solution)/shard_map/ppermute | solution.py:76
  824.9 55.4 %all-to-all-start.2 = ((bf16[8,400,256]{2,1,0:T(8,128)(2,1)}), bf16[8,400,256]{2,1,0:T(8,128)(2,1)S(1)}, u32[]{:S(2)}, u32[]{:S(2)}) async-start(bf16[8,400,256]{2,1,0:T(8,128)(2,1)} %shard_map.266), calls=%async_computation.2 | async-start | bytes 3276800 | tf_op jit(solution)/shard_map/all_to_all | solution.py:1009
  834.2 31.0 %collective-permute-start.111 = (bf16[176,2048]{1,0:T(8,128)(2,1)}, bf16[176,2048]{1,0:T(8,128)(2,1)S(1)}, u32[]{:S(2)}, u32[]{:S(2)}) collective-permute-start(bf16[176,2048]{1,0:T(8,128)(2,1)} %add_convert_fusion.8.refs_0_), channel_id=1, source_target_pairs={{0,8},{8,0},{16,24},{24,16},{1,9},{9,1},{17,25},{25,17},{2,10},{10... | collective-permute-start | bytes 2162696 | tf_op jit(solution)/shard_map/ppermute | solution.py:76
  (205 other events, 2889.1 us)
